TPU v7x, 32 devices: a whole 2x2x4 slice. The times are simulated.
32 devices in a mesh: section: 2 (over core), seq: 4 (over y, x), dp: 4 (over z).
Axes of the slice: x: 2, y: 2, z: 4, core: 2. Of those that a mesh axis runs over, the one named last changes fastest.
Arguments:
- layer_in: bfloat16 [2, 4, 1024, 768], P(None, 'dp', 'seq'), may hold values from -6 to 6
- cotangent: bfloat16 [2, 4, 152, 768], P(None, 'dp', 'seq'), may hold values from -6 to 6
- masked_rows: int32 [2, 4, 152], P(None, 'dp', 'seq'), may hold values from 0 to 1023, as said below
- global_positions: int32 [2, 4, 64], P(None, 'dp'), may hold values from 0 to 1023, as said below
- local_weight: bfloat16 [2, 768, 2304], P('section'), may hold values from -0.3125 to 0.3125
- local_bias: bfloat16 [2, 2, 768], P('section'), may hold values from -3 to 3
- global_weight: bfloat16 [2, 768, 2304], P('section'), may hold values from -0.3125 to 0.3125
- global_bias: bfloat16 [2, 2, 768], P('section'), may hold values from -3 to 3
- out_weight: bfloat16 [2, 768, 768], P('section'), may hold values from -1.75 to 1.75
- out_bias: bfloat16 [2, 768], P('section'), may hold values from -2 to 2
- norm_gain: bfloat16 [2, 2, 768], P('section'), may hold values from 0.5 to 1.5
- norm_shift: bfloat16 [2, 2, 768], P('section'), may hold values from -2 to 2
- up_weight: bfloat16 [2, 768, 3072], P('section'), may hold values from -0.21875 to 0.21875
- up_bias: bfloat16 [2, 3072], P('section'), may hold values from -3 to 3
- down_weight: bfloat16 [2, 3072, 768], P('section'), may hold values from -0.109375 to 0.109375
- down_bias: bfloat16 [2, 768], P('section'), may hold values from -2 to 2
Outputs:
- layer_outputs: bfloat16 [2, 2, 4, 1024, 768], P('section', None, 'dp', 'seq')
- input_grads: bfloat16 [2, 2, 4, 1024, 768], P('section', None, 'dp', 'seq')
- grad_local_weight: float32 [2, 768, 2304], P('section', ('seq', 'dp'))
- grad_local_bias: float32 [2, 2, 768], P('section')
- grad_global_weight: float32 [2, 768, 2304], P('section', ('seq', 'dp'))
- grad_global_bias: float32 [2, 2, 768], P('section')
- grad_out_weight: float32 [2, 768, 768], P('section', ('seq', 'dp'))
- grad_out_bias: float32 [2, 768], P('section', ('seq', 'dp'))
- grad_norm_gain: float32 [2, 2, 768], P('section')
- grad_norm_shift: float32 [2, 2, 768], P('section')
- grad_up_weight: float32 [2, 768, 3072], P('section', ('seq', 'dp'))
- grad_up_bias: float32 [2, 3072], P('section', ('seq', 'dp'))
- grad_down_weight: float32 [2, 3072, 768], P('section', ('seq', 'dp'))
- grad_down_bias: float32 [2, 768], P('section', ('seq', 'dp'))
Inputs may be any that keep to these rules, and one draw needn't show every extreme that they name: `global_positions`: in each document the 64 positions increase, the first is 0, the last is 1023, and number k lies in [k * 16, (k + 1) * 16). `masked_rows`: in each document, block k of 38 entries holds distinct positions of [k * 256, (k + 1) * 256); positions 0 and 1023 are always masked.
All inputs are finite; a program needn't handle non-finite values.
Results may differ from a plain program's by a relative error of at most 0.035.
Values may be sent and summed in bfloat16 or wider, within the bound.
No kernel may reach another device: no remote copies, remote signals or barrier semaphores. Data moves between devices by JAX's collectives and lax.ppermute only.
A program may use at most 320 MiB of HBM per device.

v0:
```python
from functools import partial
from types import SimpleNamespace

import jax
import jax.numpy as jnp
import numpy as np
from jax import lax
from jax.experimental import pallas as pl
from jax.experimental.pallas import tpu as pltpu
from jax.sharding import PartitionSpec as P

HEAD = 64
HALF = 256

SECTION, SEQ, DP = "section", "seq", "dp"
BOTH = (SECTION, SEQ)


far_below = -1e30
norm_eps = 1e-05


def padded(block, sides, width):
    for axis, dim in sides:
        count = lax.axis_size(axis)
        forward = [(i, i + 1) for i in range(count - 1)]
        backward = [(target, source) for source, target in forward]
        low = lax.ppermute(
            lax.slice_in_dim(block, block.shape[dim] - width, None, axis=dim), axis, forward
        )
        high = lax.ppermute(lax.slice_in_dim(block, 0, width, axis=dim), axis, backward)
        block = jnp.concatenate([low, block, high], axis=dim)
    return block


def joined(value, axis, join):
    pieces = jax.tree.map(lambda part: lax.all_gather(part, axis), value)
    head = jax.tree.map(lambda part: part[0], pieces)
    tail = jax.tree.map(lambda part: part[1:], pieces)
    running, _ = lax.scan(lambda running, piece: (join(running, piece), None), head, tail)
    return running


def shifted(shard, axis, by):
    length = lax.axis_size(axis)
    pairs = [(i, i + by) for i in range(length) if 0 <= i + by < length]
    return lax.ppermute(shard, axis, pairs)


def band_mask(first_row, row_count, reach_rows, length, positions, dilated):
    rows_at = first_row + jnp.arange(row_count)
    cols_at = first_row - reach_rows + jnp.arange(row_count + 2 * reach_rows)
    offset = cols_at[None, :] - rows_at[:, None]
    inside = (jnp.abs(offset) <= reach_rows) & (cols_at >= 0)[None, :] & (cols_at < length)[None, :]
    plain_key = jnp.logical_not(jnp.any(cols_at[:, None] == positions[None, :], axis=1))
    usable = inside & plain_key[None, :]
    even_gap = offset % 2 == 0
    return usable[None, :, :] & (jnp.logical_not(dilated)[:, None, None] | even_gap[None, :, :])


def layer_norm(values, gain_row, shift_row):
    center = values - jnp.mean(values, axis=-1, keepdims=True)
    scaled = lax.rsqrt(jnp.mean(center * center, axis=-1, keepdims=True) + norm_eps)
    unit_rows = center * scaled
    return (unit_rows * gain_row + shift_row, unit_rows, scaled)


def norm_back(unit_rows, scaled, gain_row, upstream):
    d_unit = upstream * gain_row
    inward = scaled * (
        d_unit
        - jnp.mean(d_unit, axis=-1, keepdims=True)
        - unit_rows * jnp.mean(d_unit * unit_rows, axis=-1, keepdims=True)
    )
    return (inward, jnp.sum(upstream * unit_rows, axis=0), jnp.sum(upstream, axis=0))


def join_stats(first_pair, second_pair):
    top_value = jnp.maximum(first_pair[0], second_pair[0])
    merged = first_pair[1] * jnp.exp(first_pair[0] - top_value) + second_pair[1] * jnp.exp(
        second_pair[0] - top_value
    )
    return (top_value, merged)


def forward_layer(source, positions, weights, first_row, length, dilated, active):
    local_w, local_b, glob_w, glob_b, out_w, out_b, gains, shifts, up_w, up_b, down_w, down_b = (
        weights
    )
    row_count = source.shape[0]
    model_width = source.shape[1]
    ff_width = up_w.shape[1]
    head_count = dilated.shape[0]
    head_size = model_width // head_count
    glob_count = positions.shape[0]
    score_scale = head_size ** (-0.5)
    owner_hit = (first_row + jnp.arange(row_count))[:, None] == positions[None, :]
    owner_low = owner_hit.astype(jnp.bfloat16)
    owner_full = owner_hit.astype(jnp.float32)
    is_global = jnp.any(owner_hit, axis=1)
    picked = jnp.einsum("cg,cd->gd", owner_low, source, preferred_element_type=jnp.float32)
    global_rows = lax.psum(picked.astype(jnp.bfloat16), SEQ)
    proj = jnp.dot(source, local_w, preferred_element_type=jnp.float32)
    queries = (proj[:, :model_width] + local_b[0]).astype(jnp.bfloat16)
    keys_low = proj[:, model_width : 2 * model_width].astype(jnp.bfloat16)
    values_low = (proj[:, 2 * model_width :] + local_b[1]).astype(jnp.bfloat16)
    gproj = jnp.dot(source, glob_w[:, model_width:], preferred_element_type=jnp.float32)
    gkeys = gproj[:, :model_width].astype(jnp.bfloat16)
    gvalues = (gproj[:, model_width:] + glob_b[1]).astype(jnp.bfloat16)
    gqueries = (
        jnp.dot(global_rows, glob_w[:, :model_width], preferred_element_type=jnp.float32)
        + glob_b[0]
    ).astype(jnp.bfloat16)
    side_proj = jnp.dot(global_rows, local_w[:, model_width:], preferred_element_type=jnp.float32)
    extra_keys = (
        side_proj[:, :model_width].astype(jnp.bfloat16).reshape(glob_count, head_count, head_size)
    )
    extra_values = (
        (side_proj[:, model_width:] + local_b[1])
        .astype(jnp.bfloat16)
        .reshape(glob_count, head_count, head_size)
    )
    key_value = jnp.concatenate([keys_low, values_low], axis=1)
    widened = padded(key_value, ((SEQ, 0),), HALF)
    reach_rows = (widened.shape[0] - row_count) // 2
    wide_keys = widened[:, :model_width].reshape(-1, head_count, head_size)
    wide_values = widened[:, model_width:].reshape(-1, head_count, head_size)
    allowed = band_mask(first_row, row_count, reach_rows, length, positions, dilated)
    queries_h = queries.reshape(row_count, head_count, head_size)
    band_score = (
        jnp.einsum("qhd,khd->hqk", queries_h, wide_keys, preferred_element_type=jnp.float32)
        * score_scale
    )
    band_score = jnp.where(allowed, band_score, far_below)
    toward = (
        jnp.einsum("qhd,ghd->hqg", queries_h, extra_keys, preferred_element_type=jnp.float32)
        * score_scale
    )
    peak_score = jnp.maximum(jnp.max(band_score, axis=-1), jnp.max(toward, axis=-1))[..., None]
    band_exp = jnp.exp(band_score - peak_score)
    toward_exp = jnp.exp(toward - peak_score)
    totals = jnp.sum(band_exp, axis=-1, keepdims=True) + jnp.sum(toward_exp, axis=-1, keepdims=True)
    band_full = band_exp / totals
    toward_full = toward_exp / totals
    band_prob = band_full.astype(jnp.bfloat16)
    toward_prob = toward_full.astype(jnp.bfloat16)
    local_ctx = jnp.einsum(
        "hqk,khd->qhd", band_prob, wide_values, preferred_element_type=jnp.float32
    ) + jnp.einsum("hqg,ghd->qhd", toward_prob, extra_values, preferred_element_type=jnp.float32)
    gqueries_h = gqueries.reshape(glob_count, head_count, head_size)
    gkeys_h = gkeys.reshape(row_count, head_count, head_size)
    gvalues_h = gvalues.reshape(row_count, head_count, head_size)
    spread = (
        jnp.einsum("ghd,khd->hgk", gqueries_h, gkeys_h, preferred_element_type=jnp.float32)
        * score_scale
    )
    part_peak = jnp.max(spread, axis=-1)
    part_total = jnp.sum(jnp.exp(spread - part_peak[..., None]), axis=-1)
    glob_peak, glob_total = joined((part_peak, part_total), SEQ, join_stats)
    glob_full = jnp.exp(spread - glob_peak[..., None]) / glob_total[..., None]
    glob_prob = glob_full.astype(jnp.bfloat16)
    part_ctx = jnp.einsum("hgk,khd->ghd", glob_prob, gvalues_h, preferred_element_type=jnp.float32)
    glob_ctx = lax.psum(part_ctx.reshape(glob_count, model_width), SEQ)
    placed_ctx = jnp.dot(owner_full, glob_ctx, precision=lax.Precision.HIGHEST)
    context = jnp.where(is_global[:, None], placed_ctx, local_ctx.reshape(row_count, model_width))
    context_low = context.astype(jnp.bfloat16)
    attn_out = jnp.dot(context_low, out_w, preferred_element_type=jnp.float32) + out_b
    mixed, unit_one, scale_one = layer_norm(
        source.astype(jnp.float32) + attn_out, gains[0], shifts[0]
    )

    def feed_forward(hidden_in):
        pre_act = (
            jnp.dot(hidden_in.astype(jnp.bfloat16), up_w, preferred_element_type=jnp.float32) + up_b
        )
        lifted = jax.nn.gelu(pre_act, approximate=False).astype(jnp.bfloat16)
        return (
            pre_act,
            lifted,
            jnp.dot(lifted, down_w, preferred_element_type=jnp.float32) + down_b,
        )

    def skip_block(hidden_in):
        return (
            jnp.zeros((row_count, ff_width), jnp.float32),
            jnp.zeros((row_count, ff_width), jnp.bfloat16),
            jnp.zeros((row_count, model_width), jnp.float32),
        )

    pre_act, activated, branch = lax.cond(active, feed_forward, skip_block, mixed)
    result, unit_two, scale_two = layer_norm(mixed + branch, gains[1], shifts[1])
    return SimpleNamespace(
        source=source,
        owner_low=owner_low,
        owner_full=owner_full,
        is_global=is_global,
        queries_h=queries_h,
        wide_keys=wide_keys,
        wide_values=wide_values,
        extra_keys=extra_keys,
        extra_values=extra_values,
        band_full=band_full,
        toward_full=toward_full,
        band_prob=band_prob,
        toward_prob=toward_prob,
        gqueries_h=gqueries_h,
        gkeys_h=gkeys_h,
        gvalues_h=gvalues_h,
        glob_full=glob_full,
        glob_prob=glob_prob,
        context_low=context_low,
        unit_one=unit_one,
        scale_one=scale_one,
        mixed=mixed,
        pre_act=pre_act,
        activated=activated,
        unit_two=unit_two,
        scale_two=scale_two,
        result=result,
        reach_rows=reach_rows,
        score_scale=score_scale,
    )


def ffn_back(kept_values, weights, upstream, active):
    local_w, local_b, glob_w, glob_b, out_w, out_b, gains, shifts, up_w, up_b, down_w, down_b = (
        weights
    )
    d_second, gain_two, shift_two = norm_back(
        kept_values.unit_two, kept_values.scale_two, gains[1], upstream
    )
    d_branch = d_second.astype(jnp.bfloat16)

    def ffn_work(operands):
        pre_act, d_out = operands
        d_lifted = jnp.einsum("cd,fd->cf", d_out, down_w, preferred_element_type=jnp.float32)
        gelu_vals, gelu_back = jax.vjp(partial(jax.nn.gelu, approximate=False), pre_act)
        d_pre = gelu_back(d_lifted)[0].astype(jnp.bfloat16)
        d_hidden = jnp.einsum("cf,df->cd", d_pre, up_w, preferred_element_type=jnp.float32)
        return (d_hidden, d_pre)

    def ffn_spare(operands):
        return (
            jnp.zeros(upstream.shape, jnp.float32),
            jnp.zeros((upstream.shape[0], up_w.shape[1]), jnp.bfloat16),
        )

    d_hidden, d_pre = lax.cond(active, ffn_work, ffn_spare, (kept_values.pre_act, d_branch))
    return (d_second + d_hidden, d_pre, d_branch, (gain_two, shift_two))


def attention_back(kept_values, weights, d_mixed):
    local_w, local_b, glob_w, glob_b, out_w, out_b, gains, shifts, up_w, up_b, down_w, down_b = (
        weights
    )
    row_count, model_width = kept_values.source.shape
    queries_h = kept_values.queries_h
    head_count, head_size = (queries_h.shape[1], queries_h.shape[2])
    glob_count = kept_values.owner_full.shape[1]
    reach_rows = kept_values.reach_rows
    score_scale = kept_values.score_scale
    d_first, gain_one, shift_one = norm_back(
        kept_values.unit_one, kept_values.scale_one, gains[0], d_mixed
    )
    d_attn = d_first.astype(jnp.bfloat16)
    d_context = jnp.einsum("ce,de->cd", d_attn, out_w, preferred_element_type=jnp.float32).astype(
        jnp.bfloat16
    )
    glob_part = jnp.einsum(
        "cg,cd->gd", kept_values.owner_low, d_context, preferred_element_type=jnp.float32
    )
    d_glob_ctx = lax.psum(glob_part.astype(jnp.bfloat16), SEQ)
    d_local = jnp.where(kept_values.is_global[:, None], jnp.zeros_like(d_context), d_context)
    d_local = d_local.reshape(row_count, head_count, head_size)
    band_full = kept_values.band_full
    toward_full = kept_values.toward_full
    d_band = jnp.einsum(
        "qhd,khd->hqk", d_local, kept_values.wide_values, preferred_element_type=jnp.float32
    )
    d_toward = jnp.einsum(
        "qhd,ghd->hqg", d_local, kept_values.extra_values, preferred_element_type=jnp.float32
    )
    inner_sum = jnp.sum(band_full * d_band, axis=-1) + jnp.sum(toward_full * d_toward, axis=-1)
    grad_band = (band_full * (d_band - inner_sum[..., None])).astype(jnp.bfloat16)
    grad_toward = (toward_full * (d_toward - inner_sum[..., None])).astype(jnp.bfloat16)
    d_queries = (
        jnp.einsum(
            "hqk,khd->qhd", grad_band, kept_values.wide_keys, preferred_element_type=jnp.float32
        )
        + jnp.einsum(
            "hqg,ghd->qhd",
            grad_toward,
            kept_values.extra_keys,
            preferred_element_type=jnp.float32,
        )
    ) * score_scale
    d_wide_keys = (
        jnp.einsum("hqk,qhd->khd", grad_band, queries_h, preferred_element_type=jnp.float32)
        * score_scale
    )
    d_wide_values = jnp.einsum(
        "hqk,qhd->khd", kept_values.band_prob, d_local, preferred_element_type=jnp.float32
    )
    d_extra_keys = (
        jnp.einsum("hqg,qhd->ghd", grad_toward, queries_h, preferred_element_type=jnp.float32)
        * score_scale
    )
    d_extra_values = jnp.einsum(
        "hqg,qhd->ghd", kept_values.toward_prob, d_local, preferred_element_type=jnp.float32
    )
    glob_full = kept_values.glob_full
    d_glob_h = d_glob_ctx.reshape(glob_count, head_count, head_size)
    d_spread = jnp.einsum(
        "ghd,khd->hgk", d_glob_h, kept_values.gvalues_h, preferred_element_type=jnp.float32
    )
    part_inner = jnp.sum(glob_full * d_spread, axis=-1)
    glob_inner, sum_extra_keys, sum_extra_values = (
        lax.psum(part_inner.astype(jnp.bfloat16), SEQ).astype(jnp.float32),
        lax.psum(d_extra_keys.reshape(glob_count, model_width).astype(jnp.bfloat16), SEQ).astype(
            jnp.float32
        ),
        lax.psum(
            d_extra_values.reshape(glob_count, model_width).astype(jnp.bfloat16), SEQ
        ).astype(jnp.float32),
    )
    grad_spread = (glob_full * (d_spread - glob_inner[..., None])).astype(jnp.bfloat16)
    part_query = (
        jnp.einsum(
            "hgk,khd->ghd", grad_spread, kept_values.gkeys_h, preferred_element_type=jnp.float32
        )
        * score_scale
    )
    d_gkeys = (
        jnp.einsum(
            "hgk,ghd->khd",
            grad_spread,
            kept_values.gqueries_h,
            preferred_element_type=jnp.float32,
        )
        * score_scale
    )
    d_gvalues = jnp.einsum(
        "hgk,ghd->khd", kept_values.glob_prob, d_glob_h, preferred_element_type=jnp.float32
    )
    d_gqueries = lax.psum(
        part_query.reshape(glob_count, model_width).astype(jnp.bfloat16), SEQ
    ).astype(jnp.float32)
    d_wide = jnp.concatenate(
        [d_wide_keys.reshape(-1, model_width), d_wide_values.reshape(-1, model_width)], axis=1
    )
    rim_grads = jnp.concatenate([d_wide[:reach_rows], d_wide[reach_rows + row_count :]], axis=0)
    incoming = padded(rim_grads.astype(jnp.bfloat16), ((SEQ, 0),), HALF).astype(rim_grads.dtype)
    own_part = (
        d_wide[reach_rows : reach_rows + row_count]
        + incoming[:reach_rows]
        + incoming[3 * reach_rows :]
    )
    owner_full = kept_values.owner_full
    d_keys_low = (
        own_part[:, :model_width]
        + jnp.dot(owner_full, sum_extra_keys, precision=lax.Precision.HIGHEST)
    ).astype(jnp.bfloat16)
    d_values_low = (
        own_part[:, model_width:]
        + jnp.dot(owner_full, sum_extra_values, precision=lax.Precision.HIGHEST)
    ).astype(jnp.bfloat16)
    d_queries_low = d_queries.reshape(row_count, model_width).astype(jnp.bfloat16)
    d_proj = jnp.concatenate([d_queries_low, d_keys_low, d_values_low], axis=1)
    d_gq_rows = jnp.dot(owner_full, d_gqueries, precision=lax.Precision.HIGHEST).astype(
        jnp.bfloat16
    )
    d_gproj = jnp.concatenate(
        [
            d_gq_rows,
            d_gkeys.reshape(row_count, model_width).astype(jnp.bfloat16),
            d_gvalues.reshape(row_count, model_width).astype(jnp.bfloat16),
        ],
        axis=1,
    )
    d_source = (
        d_first
        + jnp.einsum("ce,de->cd", d_proj, local_w, preferred_element_type=jnp.float32)
        + jnp.einsum("ce,de->cd", d_gproj, glob_w, preferred_element_type=jnp.float32)
    )
    return (d_source, d_proj, d_gproj, d_attn, (gain_one, shift_one))


def ffn_terms(mixed_buf, pre_buf, act_buf, branch_buf, count):
    return (
        jnp.einsum(
            "mcd,mcf->df", mixed_buf[:count], pre_buf[:count], preferred_element_type=jnp.float32
        ),
        jnp.sum(pre_buf[:count].astype(jnp.float32), axis=(0, 1)),
        jnp.einsum(
            "mcf,mcd->fd", act_buf[:count], branch_buf[:count], preferred_element_type=jnp.float32
        ),
        jnp.sum(branch_buf[:count].astype(jnp.float32), axis=(0, 1)),
    )


def on_device(
    layer_in,
    cotangent,
    masked_rows,
    global_positions,
    local_weight,
    local_bias,
    global_weight,
    global_bias,
    out_weight,
    out_bias,
    norm_gain,
    norm_shift,
    up_weight,
    up_bias,
    down_weight,
    down_bias,
):
    weights = (
        local_weight[0],
        local_bias[0],
        global_weight[0],
        global_bias[0],
        out_weight[0],
        out_bias[0],
        norm_gain[0],
        norm_shift[0],
        up_weight[0],
        up_bias[0],
        down_weight[0],
        down_bias[0],
    )
    section_index = lax.axis_index(SECTION)
    seq_index = lax.axis_index(SEQ)
    micro_count = layer_in.shape[0]
    row_count = layer_in.shape[2]
    model_width = layer_in.shape[3]
    ff_width = up_weight.shape[2]
    length = row_count * lax.axis_size(SEQ)
    first_row = seq_index * row_count
    head_count = model_width // HEAD
    dilated = (jnp.arange(head_count) >= head_count - 2) & (section_index == 1)
    kept_inputs = jnp.zeros((micro_count, row_count, model_width), jnp.bfloat16)
    outputs = jnp.zeros_like(kept_inputs)
    arrived = jnp.zeros((row_count, model_width), jnp.bfloat16)
    for step_index in range(micro_count + 1):
        micro_index = step_index - section_index
        in_range = (micro_index >= 0) & (micro_index < micro_count)
        slot_index = jnp.clip(micro_index, 0, micro_count - 1)
        fresh = lax.dynamic_index_in_dim(layer_in, slot_index, 0, keepdims=False)[0]
        source = jnp.where(section_index == 0, fresh, arrived)
        positions = lax.dynamic_index_in_dim(global_positions, slot_index, 0, keepdims=False)[0]
        kept_values = forward_layer(
            source, positions, weights, first_row, length, dilated, in_range
        )
        result = kept_values.result.astype(jnp.bfloat16)
        kept_inputs = jnp.where(
            in_range,
            lax.dynamic_update_index_in_dim(kept_inputs, source, slot_index, 0),
            kept_inputs,
        )
        outputs = jnp.where(
            in_range, lax.dynamic_update_index_in_dim(outputs, result, slot_index, 0), outputs
        )
        if step_index < micro_count:
            arrived = shifted(result, SECTION, 1)
    slots = micro_count + 1
    proj_buf = jnp.zeros((slots, row_count, 3 * model_width), jnp.bfloat16)
    gproj_buf = jnp.zeros_like(proj_buf)
    ctx_buf = jnp.zeros((slots, row_count, model_width), jnp.bfloat16)
    attn_buf = jnp.zeros_like(ctx_buf)
    mixed_buf = jnp.zeros_like(ctx_buf)
    branch_buf = jnp.zeros_like(ctx_buf)
    pre_buf = jnp.zeros((slots, row_count, ff_width), jnp.bfloat16)
    act_buf = jnp.zeros_like(pre_buf)
    gain_total = jnp.zeros((2, model_width), jnp.float32)
    shift_total = jnp.zeros((2, model_width), jnp.float32)
    back_arrived = jnp.zeros((row_count, model_width), jnp.bfloat16)
    in_grads = jnp.zeros_like(kept_inputs)
    for step_index in range(micro_count + 1):
        micro_index = step_index - 1 + section_index
        in_range = (micro_index >= 0) & (micro_index < micro_count)
        slot_index = jnp.clip(micro_index, 0, micro_count - 1)
        store = jnp.where(in_range, micro_index, micro_count)
        source = lax.dynamic_index_in_dim(kept_inputs, slot_index, 0, keepdims=False)
        positions = lax.dynamic_index_in_dim(global_positions, slot_index, 0, keepdims=False)[0]
        picked_rows = lax.dynamic_index_in_dim(masked_rows, slot_index, 0, keepdims=False)[0]
        picked_grads = lax.dynamic_index_in_dim(cotangent, slot_index, 0, keepdims=False)[0]
        row_hit = ((first_row + jnp.arange(row_count))[:, None] == picked_rows[None, :]).astype(
            jnp.bfloat16
        )
        placed = jnp.dot(row_hit, picked_grads, preferred_element_type=jnp.float32)
        upstream = jnp.where(section_index == 1, placed, back_arrived.astype(jnp.float32))
        kept_values = forward_layer(
            source, positions, weights, first_row, length, dilated, in_range
        )
        d_mixed, d_pre, d_branch, norm_two = ffn_back(kept_values, weights, upstream, in_range)
        mixed_buf = lax.dynamic_update_index_in_dim(
            mixed_buf, kept_values.mixed.astype(jnp.bfloat16), store, 0
        )
        pre_buf = lax.dynamic_update_index_in_dim(pre_buf, d_pre, store, 0)
        act_buf = lax.dynamic_update_index_in_dim(act_buf, kept_values.activated, store, 0)
        branch_buf = lax.dynamic_update_index_in_dim(branch_buf, d_branch, store, 0)
        d_source, d_proj, d_gproj, d_attn, norm_one = attention_back(kept_values, weights, d_mixed)
        proj_buf = lax.dynamic_update_index_in_dim(proj_buf, d_proj, store, 0)
        gproj_buf = lax.dynamic_update_index_in_dim(gproj_buf, d_gproj, store, 0)
        ctx_buf = lax.dynamic_update_index_in_dim(ctx_buf, kept_values.context_low, store, 0)
        attn_buf = lax.dynamic_update_index_in_dim(attn_buf, d_attn, store, 0)
        gain_total = gain_total + jnp.where(in_range, jnp.stack([norm_one[0], norm_two[0]]), 0.0)
        shift_total = shift_total + jnp.where(in_range, jnp.stack([norm_one[1], norm_two[1]]), 0.0)
        d_low = d_source.astype(jnp.bfloat16)
        in_grads = jnp.where(
            in_range, lax.dynamic_update_index_in_dim(in_grads, d_low, slot_index, 0), in_grads
        )
        if step_index < micro_count:
            back_arrived = shifted(d_low, SECTION, -1)
    used_proj = proj_buf[:micro_count]
    used_gproj = gproj_buf[:micro_count]
    grad_local = jnp.einsum(
        "mcd,mce->de", kept_inputs, used_proj, preferred_element_type=jnp.float32
    )
    grad_glob = jnp.einsum(
        "mcd,mce->de", kept_inputs, used_gproj, preferred_element_type=jnp.float32
    )
    grad_out = jnp.einsum(
        "mcd,mce->de",
        ctx_buf[:micro_count],
        attn_buf[:micro_count],
        preferred_element_type=jnp.float32,
    )
    grad_out_b = jnp.sum(attn_buf[:micro_count].astype(jnp.float32), axis=(0, 1))
    local_b_grad = jnp.stack(
        [
            jnp.sum(used_proj[:, :, :model_width].astype(jnp.float32), axis=(0, 1)),
            jnp.sum(used_proj[:, :, 2 * model_width :].astype(jnp.float32), axis=(0, 1)),
        ]
    )
    glob_b_grad = jnp.stack(
        [
            jnp.sum(used_gproj[:, :, :model_width].astype(jnp.float32), axis=(0, 1)),
            jnp.sum(used_gproj[:, :, 2 * model_width :].astype(jnp.float32), axis=(0, 1)),
        ]
    )
    small_sums = lax.psum((local_b_grad, glob_b_grad, gain_total, shift_total), (SEQ, DP))
    ffn_parts = ffn_terms(mixed_buf, pre_buf, act_buf, branch_buf, micro_count)
    large_sums = (
        lax.psum_scatter(grad_local, (SEQ, DP), scatter_dimension=0, tiled=True),
        lax.psum_scatter(grad_glob, (SEQ, DP), scatter_dimension=0, tiled=True),
        lax.psum_scatter(grad_out, (SEQ, DP), scatter_dimension=0, tiled=True),
        lax.psum_scatter(grad_out_b, (SEQ, DP), scatter_dimension=0, tiled=True),
        lax.psum_scatter(ffn_parts[0], (SEQ, DP), scatter_dimension=0, tiled=True),
        lax.psum_scatter(ffn_parts[1], (SEQ, DP), scatter_dimension=0, tiled=True),
        lax.psum_scatter(ffn_parts[2], (SEQ, DP), scatter_dimension=0, tiled=True),
        lax.psum_scatter(ffn_parts[3], (SEQ, DP), scatter_dimension=0, tiled=True),
    )
    summed = (
        large_sums[0],
        small_sums[0],
        large_sums[1],
        small_sums[1],
        large_sums[2],
        large_sums[3],
        small_sums[2],
        small_sums[3],
        large_sums[4],
        large_sums[5],
        large_sums[6],
        large_sums[7],
    )
    return (outputs[None, :, None], in_grads[None, :, None]) + tuple(
        (member[None] for member in summed)
    )


bf16 = jnp.bfloat16
f32 = jnp.float32
VMEM_BYTES = 50 * 1024 * 1024


def nn(a, b):
    return jnp.dot(a, b, preferred_element_type=f32)


def nt(a, b):
    return lax.dot_general(a, b, (((1,), (1,)), ((), ())), preferred_element_type=f32)


def tn(a, b):
    return lax.dot_general(a, b, (((0,), (0,)), ((), ())), preferred_element_type=f32)


def owner_rows(prow, chunk, rows):
    at = lax.broadcasted_iota(jnp.int32, (rows, prow.shape[1]), 0) + chunk * rows
    return (at == prow[...]).astype(f32)


def owner_cols(pcol, chunk, rows):
    at = lax.broadcasted_iota(jnp.int32, (pcol.shape[0], rows), 1) + chunk * rows
    return (at == pcol[...]).astype(f32)


def is_dilated(layer, group, h):
    return ((3 * group + h >= 10) & (layer == 1)).astype(jnp.int32)


def band_masks(mask_s, dilated, rows):
    row = lax.broadcasted_iota(jnp.int32, (rows, rows), 0)
    col = lax.broadcasted_iota(jnp.int32, (rows, rows), 1)
    odd = ((row + col) % 2).astype(f32)
    level = odd * (dilated.astype(f32) * far_below)
    mask_s[0] = jnp.where(row >= col, level, far_below)
    mask_s[1] = level
    mask_s[2] = jnp.where(row <= col, level, far_below)


def neighbours(block, count):
    return [b for b in (block - 1, block, block + 1) if 0 <= b < count]


def cost(us):
    return pl.CostEstimate(
        flops=int(us * 1e9), transcendentals=0, bytes_accessed=int(us * 3.5e6)
    )


def start_all(copies):
    for copy in copies:
        copy.start()
    return copies


def wait_all(copies):
    for copy in copies:
        copy.wait()


def moves(pairs, sems, at=0):
    return [pltpu.make_async_copy(a, b, sems.at[at + i]) for i, (a, b) in enumerate(pairs)]


def choose(flag, first, second, target, sem):
    for value, source in ((0, first), (1, second)):

        @pl.when(flag == value)
        def _(source=source):
            pltpu.make_async_copy(source, target, sem).start()

    return pltpu.make_async_copy(first, target, sem)


def prepare_kernel(
    ids, lw, gw, lb, gb, ob, ng, ns, db, ub, own_o, send_o, pack_o, win_s, sems
):
    width = lw.shape[0]
    hw = width // 4
    sources = [(lw, 0), (lw, 1), (lw, 2), (gw, 1), (gw, 2), (gw, 0)]
    copies = []
    for t, group in enumerate((ids[1], ids[0])):
        for i, (ref, part) in enumerate(sources):
            start = pl.multiple_of(part * width + 128 * ((3 * group) // 2), 128)
            copies.append(
                pltpu.make_async_copy(
                    ref.at[:, pl.ds(start, 256)], win_s.at[t, i], sems.at[6 * t + i]
                )
            )
            copies[-1].start()
    pack_o[...] = jnp.zeros(pack_o.shape, bf16)
    at = 0
    for ref in (lb, gb, ob, ng, ns, db):
        pack_o[at : at + ref.shape[0], :] = ref[...]
        at += ref.shape[0]
    for i in range(ub.shape[1] // width):
        pack_o[at + i : at + i + 1, :] = ub[:, i * width : (i + 1) * width]
    for t, target in enumerate((send_o, own_o)):
        for i in range(6):
            copies[6 * t + i].wait()
        for odd in range(2):

            @pl.when(ids[6] == odd)
            def _(t=t, target=target, odd=odd):
                parts = [win_s[t, i][:, 64 * odd : 64 * odd + hw] for i in range(6)]
                target[...] = jnp.concatenate(parts, axis=1)


def prepare(ids, local_w, global_w, rows):
    width = local_w.shape[0]
    vm = pl.BlockSpec(memory_space=pltpu.VMEM)
    hbm = pl.BlockSpec(memory_space=pl.ANY)
    chosen = jax.ShapeDtypeStruct((width, 6 * width // 4), bf16)
    return pl.pallas_call(
        prepare_kernel,
        out_shape=[chosen, chosen, jax.ShapeDtypeStruct((16, width), bf16)],
        in_specs=[pl.BlockSpec(memory_space=pltpu.SMEM), hbm, hbm] + [vm] * 7,
        out_specs=[vm] * 3,
        scratch_shapes=[
            pltpu.VMEM((2, 6, width, 256), bf16),
            pltpu.SemaphoreType.DMA((12,)),
        ],
        compiler_params=pltpu.CompilerParams(vmem_limit_bytes=VMEM_BYTES),
        cost_estimate=cost(3),
        name="prepare",
    )(ids, local_w, global_w, *rows)


def attend_kernel(layer, *refs):
    count = 4
    sources = 7 if layer == 0 else 4
    ids, parts, refs = refs[0], refs[1 : 1 + sources], refs[1 + sources :]
    (
        w_a, w_b, pack_a, pack_b, prow, pcol,
        c0, c1, c2, c3, u_o, own_o, q_o, k_o, v_o, gk_o, gv_o, gq_o, kg_o, vg_o, lse_o,
        w_s, sem, vt_s, mask_s, ctx_s, gctx_s,
    ) = refs
    rows = c0.shape[0]
    heads = q_o.shape[0]
    hw = heads * HEAD
    scale = HEAD ** (-0.5)
    glob = prow.shape[1]
    group, core = ids[0], ids[4]
    w_copy = choose((core != layer).astype(jnp.int32), w_a, w_b, w_s, sem)
    if layer == 0:
        block = parts[0]
        half = rows // 2
        u_o[pl.ds(pl.multiple_of((2 * ids[5] + ids[6]) * rows, rows), rows), :] = block[ids[5]]
        places = (
            2 * ids[5] + 1 - ids[6],
            2 * (1 - ids[5]) + ids[6],
            2 * (1 - ids[5]) + 1 - ids[6],
        )
        for i, place in enumerate(places):
            for part, side in ((parts[1 + i], core), (parts[4 + i], 1 - core)):
                at = pl.multiple_of(place * rows + side * half, half)
                u_o[pl.ds(at, half), :] = part[...]
    else:
        for r in range(count):
            u_o[pl.ds(pl.multiple_of(ids[r] * rows, rows), rows), :] = parts[r][...]
    own_o[...] = u_o[pl.ds(pl.multiple_of(group * rows, rows), rows), :]
    pack = jnp.where(core == layer, pack_a[...].astype(f32), pack_b[...].astype(f32))[:4]
    hb = pack[:, :hw]
    for i in range(1, 4):
        hb = jnp.where(group == i, pack[:, i * hw : (i + 1) * hw], hb)
    kg_all = jnp.zeros((glob, hw), f32)
    vg_all = jnp.zeros((glob, hw), f32)
    ug_all = jnp.zeros((glob, u_o.shape[1]), f32)
    first = lax.broadcasted_iota(jnp.int32, (rows, HEAD), 1) == 0
    w_copy.wait()
    w = w_s
    for chunk in range(count):
        at = slice(chunk * rows, (chunk + 1) * rows)
        x = u_o[at, :]
        p = nn(x, w[:, : 5 * hw])
        queries = (p[:, :hw] + hb[0:1, :]).astype(bf16).astype(f32) * scale
        keys = p[:, hw : 2 * hw]
        values = p[:, 2 * hw : 3 * hw] + hb[1:2, :]
        gkeys = p[:, 3 * hw : 4 * hw]
        gvalues = p[:, 4 * hw : 5 * hw] + hb[3:4, :]
        is_global = jnp.max(owner_rows(prow, chunk, rows), axis=1, keepdims=True)
        tail_k = jnp.where(first, is_global * far_below, 0.0)
        tail_q = jnp.where(first, 1.0, 0.0)
        for h in range(heads):
            cut = slice(HEAD * h, HEAD * h + HEAD)
            q_o[h, at, :] = jnp.concatenate([queries[:, cut], tail_q], axis=1).astype(bf16)
            k_o[h, at, :] = jnp.concatenate([keys[:, cut], tail_k], axis=1).astype(bf16)
            v_o[h, at, :] = values[:, cut].astype(bf16)
            gk_o[h, at, :] = gkeys[:, cut].astype(bf16)
            gv_o[h, at, :] = gvalues[:, cut].astype(bf16)
            vt_s[h, chunk] = values[:, cut].T.astype(bf16)
        hit = owner_cols(pcol, chunk, rows).astype(bf16)
        kg_all += nn(hit, keys.astype(bf16))
        vg_all += nn(hit, values.astype(bf16))
        ug_all += nn(hit, x)
    gq_all = (nn(ug_all.astype(bf16), w[:, 5 * hw :]) + hb[2:3, :]).astype(bf16).astype(f32) * scale
    none = jnp.zeros((glob, HEAD), f32)
    for h in range(heads):
        cut = slice(HEAD * h, HEAD * h + HEAD)
        gq_o[h] = gq_all[:, cut].astype(bf16)
        kg_o[h] = jnp.concatenate([kg_all[:, cut], none], axis=1).astype(bf16)
        vg_o[h] = vg_all[:, cut].astype(bf16)

    def head(h, carry):
        band_masks(mask_s, is_dilated(layer, group, h), rows)
        kg = kg_o[h]
        vgt = vg_o[h].astype(f32).T.astype(bf16)
        for qb in range(count):
            q = q_o[h, qb * rows : (qb + 1) * rows, :]
            near = neighbours(qb, count)
            scores = [
                nt(k_o[h, kb * rows : (kb + 1) * rows, :], q) + mask_s[kb - qb + 1] for kb in near
            ]
            side = nt(kg, q)
            peak = jnp.max(side, axis=0, keepdims=True)
            for s in scores:
                peak = jnp.maximum(peak, jnp.max(s, axis=0, keepdims=True))
            side = jnp.exp(side - peak)
            scores = [jnp.exp(s - peak) for s in scores]
            total = jnp.sum(side, axis=0, keepdims=True)
            for s in scores:
                total += jnp.sum(s, axis=0, keepdims=True)
            inverse = 1.0 / total
            ctx = nn(vgt, (side * inverse).astype(bf16))
            for kb, s in zip(near, scores):
                ctx += nn(vt_s[h, kb], (s * inverse).astype(bf16))
            ctx_s[h, qb * rows : (qb + 1) * rows, :] = ctx.T
            lse_o[h, qb : qb + 1, :] = peak + jnp.log(total)
        spread = nt(gq_o[h], gk_o[h])
        e = jnp.exp(spread - jnp.max(spread, axis=1, keepdims=True))
        prob = (e / jnp.sum(e, axis=1, keepdims=True)).astype(bf16)
        gctx_s[h] = nn(prob, gv_o[h])
        return carry

    lax.fori_loop(0, heads, head, 0)
    gctx = jnp.concatenate([gctx_s[h] for h in range(heads)], axis=1).astype(bf16)
    for r, c_o in enumerate((c0, c1, c2, c3)):
        chunk = ids[r]
        at = pl.ds(pl.multiple_of(chunk * rows, rows), rows)
        hit = owner_rows(prow, chunk, rows)
        placed = nn(hit.astype(bf16), gctx)
        local = jnp.concatenate([ctx_s[h, at, :] for h in range(heads)], axis=1)
        c_o[...] = jnp.where(jnp.max(hit, axis=1, keepdims=True) > 0, placed, local).astype(bf16)


def attend(layer, ids, parts, weights, packs, prow, pcol):
    width = weights[0].shape[0]
    hw = weights[0].shape[1] // 6
    heads = hw // HEAD
    glob = prow.shape[1]
    rows = HALF
    full = 4 * rows
    sds = jax.ShapeDtypeStruct
    outs = [sds((rows, hw), bf16)] * 4 + [
        sds((full, width), bf16),
        sds((rows, width), bf16),
        sds((heads, full, 2 * HEAD), bf16),
        sds((heads, full, 2 * HEAD), bf16),
        sds((heads, full, HEAD), bf16),
        sds((heads, full, HEAD), bf16),
        sds((heads, full, HEAD), bf16),
        sds((heads, glob, HEAD), bf16),
        sds((heads, glob, 2 * HEAD), bf16),
        sds((heads, glob, HEAD), bf16),
        sds((heads, 4, rows), f32),
    ]
    vm = pl.BlockSpec(memory_space=pltpu.VMEM)
    hbm = pl.BlockSpec(memory_space=pl.ANY)
    res = pl.pallas_call(
        partial(attend_kernel, layer),
        out_shape=outs,
        in_specs=[pl.BlockSpec(memory_space=pltpu.SMEM)]
        + [vm] * len(parts)
        + [hbm] * 2
        + [vm] * 4,
        out_specs=[vm] * len(outs),
        scratch_shapes=[
            pltpu.VMEM(weights[0].shape, bf16),
            pltpu.SemaphoreType.DMA,
            pltpu.VMEM((heads, 4, HEAD, rows), bf16),
            pltpu.VMEM((3, rows, rows), f32),
            pltpu.VMEM((heads, full, HEAD), f32),
            pltpu.VMEM((heads, glob, HEAD), f32),
        ],
        compiler_params=pltpu.CompilerParams(vmem_limit_bytes=VMEM_BYTES),
        cost_estimate=cost(14),
        name="attend",
    )(ids, *parts, *weights, *packs, prow, pcol)
    return res[:4], res[4], res[5], res[6:]


def attend_back_kernel(
    layer, ids, d0, d1, d2, d3, q, k, v, gk, gv, gq, kg, vg, lse, prow, pcol, w_a, w_b,
    d_o, bias_o, p0, p1, p2, p3,
    w_s, sem, mask_s, do_s, dog_s, dq_s, dk_s, dv_s, dkg_s, dvg_s, dgk_s, dgv_s, dgq_s,
):
    rows = d0.shape[0]
    heads = q.shape[0]
    count = 4
    scale = HEAD ** (-0.5)
    glob = prow.shape[1]
    w_copy = choose((ids[4] != layer).astype(jnp.int32), w_a, w_b, w_s, sem)
    dg_all = jnp.zeros((glob, heads * HEAD), f32)
    for r, d in enumerate((d0, d1, d2, d3)):
        chunk = ids[r]
        at = pl.ds(pl.multiple_of(chunk * rows, rows), rows)
        dx = d[...]
        dg_all += nn(owner_cols(pcol, chunk, rows).astype(bf16), dx)
        is_global = jnp.max(owner_rows(prow, chunk, rows), axis=1, keepdims=True)
        local = jnp.where(is_global > 0, 0.0, dx.astype(f32))
        for h in range(heads):
            do_s[h, at, :] = local[:, HEAD * h : HEAD * h + HEAD].astype(bf16)
    for h in range(heads):
        dog_s[h] = dg_all[:, HEAD * h : HEAD * h + HEAD].astype(bf16)

    def head(h, carry):
        band_masks(mask_s, is_dilated(layer, ids[0], h), rows)
        kgh = kg[h]
        vgh = vg[h]
        kgt = kgh[:, :HEAD].astype(f32).T.astype(bf16)
        kt = [
            k[h, b * rows : (b + 1) * rows, :][:, :HEAD].astype(f32).T.astype(bf16)
            for b in range(count)
        ]
        dk = [jnp.zeros((rows, 2 * HEAD), f32) for _ in range(count)]
        dv = [jnp.zeros((rows, HEAD), f32) for _ in range(count)]
        dkg = jnp.zeros((glob, 2 * HEAD), f32)
        dvg = jnp.zeros((glob, HEAD), f32)
        for qb in range(count):
            span = slice(qb * rows, (qb + 1) * rows)
            qq = q[h, span, :]
            do = do_s[h, span, :]
            row = lse[h, qb : qb + 1, :]
            near = neighbours(qb, count)
            prob = [
                jnp.exp(nt(k[h, b * rows : (b + 1) * rows, :], qq) + mask_s[b - qb + 1] - row)
                for b in near
            ]
            side = jnp.exp(nt(kgh, qq) - row)
            dprob = [nt(v[h, b * rows : (b + 1) * rows, :], do) for b in near]
            dside = nt(vgh, do)
            inner = jnp.sum(side * dside, axis=0, keepdims=True)
            for p, dp in zip(prob, dprob):
                inner += jnp.sum(p * dp, axis=0, keepdims=True)
            ds = (side * (dside - inner)).astype(bf16)
            dvg += nn(side.astype(bf16), do)
            dkg += nn(ds, qq)
            dq = nn(kgt, ds)
            for b, p, dp in zip(near, prob, dprob):
                ds = (p * (dp - inner)).astype(bf16)
                dv[b] += nn(p.astype(bf16), do)
                dk[b] += nn(ds, qq)
                dq += nn(kt[b], ds)
            dq_s[h, span, :] = dq.T * scale
        for b in range(count):
            dk_s[h, b * rows : (b + 1) * rows, :] = dk[b][:, :HEAD]
            dv_s[h, b * rows : (b + 1) * rows, :] = dv[b]
        dkg_s[h] = dkg[:, :HEAD]
        dvg_s[h] = dvg
        spread = nt(gk[h], gq[h])
        e = jnp.exp(spread - jnp.max(spread, axis=0, keepdims=True))
        p = e / jnp.sum(e, axis=0, keepdims=True)
        dog = dog_s[h]
        dp = nt(gv[h], dog)
        ds = (p * (dp - jnp.sum(p * dp, axis=0, keepdims=True))).astype(bf16)
        dgv_s[h] = nn(p.astype(bf16), dog)
        dgk_s[h] = nn(ds, gq[h])
        dgq_s[h] = tn(ds, gk[h]) * scale
        return carry

    lax.fori_loop(0, heads, head, 0)

    def wide(ref, at=None):
        parts = [ref[h] if at is None else ref[h, at, :] for h in range(heads)]
        return jnp.concatenate(parts, axis=1)

    dkg_all = wide(dkg_s).astype(bf16)
    dvg_all = wide(dvg_s).astype(bf16)
    dgq_all = wide(dgq_s).astype(bf16)
    sums = [jnp.zeros((1, heads * HEAD), f32) for _ in range(4)]
    w_copy.wait()
    for r, p_o in enumerate((p0, p1, p2, p3)):
        chunk = ids[r]
        at = pl.ds(pl.multiple_of(chunk * rows, rows), rows)
        hit = owner_rows(prow, chunk, rows).astype(bf16)
        dq = wide(dq_s, at)
        dk = wide(dk_s, at) + nn(hit, dkg_all)
        dv = wide(dv_s, at) + nn(hit, dvg_all)
        dgk = wide(dgk_s, at)
        dgv = wide(dgv_s, at)
        dgq = nn(hit, dgq_all)
        joint = jnp.concatenate([dq, dk, dv, dgk, dgv, dgq], axis=1).astype(bf16)
        d_o[at, :] = joint
        p_o[...] = nt(joint, w_s[...]).astype(p_o.dtype)
        for i, part in enumerate((dq, dv, dgq, dgv)):
            sums[i] += jnp.sum(part, axis=0, keepdims=True)
    bias_o[...] = jnp.concatenate(sums, axis=0)


def attend_back(layer, ids, pieces, kept, prow, pcol, weights):
    rows, hw = pieces[0].shape
    width = weights[0].shape[0]
    heads = hw // HEAD
    glob = prow.shape[1]
    full = 4 * rows
    vm = pl.BlockSpec(memory_space=pltpu.VMEM)
    hbm = pl.BlockSpec(memory_space=pl.ANY)
    big = (heads, full, HEAD)
    small = (heads, glob, HEAD)
    res = pl.pallas_call(
        partial(attend_back_kernel, layer),
        out_shape=[
            jax.ShapeDtypeStruct((full, 6 * hw), bf16),
            jax.ShapeDtypeStruct((4, hw), f32),
        ]
        + [jax.ShapeDtypeStruct((rows, width), t) for t in (f32, bf16, f32, bf16)],
        in_specs=[pl.BlockSpec(memory_space=pltpu.SMEM)] + [vm] * 15 + [hbm] * 2,
        out_specs=[vm] * 6,
        scratch_shapes=[
            pltpu.VMEM(weights[0].shape, bf16),
            pltpu.SemaphoreType.DMA,
            pltpu.VMEM((3, rows, rows), f32),
            pltpu.VMEM(big, bf16),
            pltpu.VMEM(small, bf16),
            pltpu.VMEM(big, f32),
            pltpu.VMEM(big, f32),
            pltpu.VMEM(big, f32),
            pltpu.VMEM(small, f32),
            pltpu.VMEM(small, f32),
            pltpu.VMEM(big, f32),
            pltpu.VMEM(big, f32),
            pltpu.VMEM(small, f32),
        ],
        compiler_params=pltpu.CompilerParams(vmem_limit_bytes=VMEM_BYTES),
        cost_estimate=cost(18),
        name="attend_back",
    )(ids, *pieces, *kept, prow, pcol, *weights)
    return res[0], res[1], res[2:]


def fetch(first, second, use_second, pairs, sems):
    for flag, source in ((0, first), (1, second)):

        @pl.when(use_second.astype(jnp.int32) == flag)
        def _(source=source):
            for i, (pick, target) in enumerate(pairs):
                pltpu.make_async_copy(pick(source), target, sems.at[i]).start()

    def wait(i):
        pick, target = pairs[i]
        pltpu.make_async_copy(pick(first), target, sems.at[i]).wait()

    return wait


def weight_pairs(steps, cols, wo_s, wu_s, wd_s):
    pairs = [(lambda w: w[0], wo_s)]
    for j in range(steps):
        pairs.append((lambda w, j=j: w[1].at[:, pl.ds(j * cols, cols)], wu_s.at[j]))
        pairs.append((lambda w, j=j: w[2].at[pl.ds(j * cols, cols), :], wd_s.at[j]))
    return pairs


def row_norm(z):
    center = z - jnp.mean(z, axis=1, keepdims=True)
    scaled = lax.rsqrt(jnp.mean(center * center, axis=1, keepdims=True) + norm_eps)
    return center * scaled, scaled


def rows_kernel(
    layer, ids, c0, c1, c2, c3, u, pack_a, pack_b, wo_a, wo_b, wu_a, wu_b, wd_a, wd_b,
    y_o, fwd_o, slope_o, unit1_o, unit2_o, scale1_o, scale2_o,
    wo_s, wu_s, wd_s, sems,
):
    steps, cols = wu_s.shape[0], wu_s.shape[2]
    pairs = weight_pairs(steps, cols, wo_s, wu_s, wd_s)
    wait = fetch((wo_a, wu_a, wd_a), (wo_b, wu_b, wd_b), ids[4] != layer, pairs, sems)
    pack = jnp.where(ids[4] == layer, pack_a[...].astype(f32), pack_b[...].astype(f32))
    hw = c0.shape[1]
    width = 4 * hw
    pieces = [c[...] for c in (c0, c1, c2, c3)]
    for a in range(4):
        part = pieces[0]
        for r in range(1, 4):
            part = jnp.where(ids[r] == a, pieces[r].astype(f32), part.astype(f32))
        fwd_o[:, width + a * hw : width + (a + 1) * hw] = part.astype(bf16)
    wait(0)
    attn = nn(fwd_o[:, width : 2 * width], wo_s[...]) + pack[4:5, :]
    unit1, scale1 = row_norm(u[...].astype(f32) + attn)
    mixed = unit1 * pack[5:6, :] + pack[7:8, :]
    low = mixed.astype(bf16)
    fwd_o[:, :width] = low
    unit1_o[...] = unit1
    scale1_o[...] = jnp.broadcast_to(scale1, scale1_o.shape)
    branch = jnp.zeros(mixed.shape, f32)
    for j in range(steps):
        wait(1 + 2 * j)
        pre = nn(low, wu_s[j]) + pack[10 + j : 11 + j, :]
        gauss = 0.5 * (1.0 + lax.erf(pre * (2.0 ** -0.5)))
        act = (pre * gauss).astype(bf16)
        bell = jnp.exp(-0.5 * pre * pre) * ((2.0 * np.pi) ** -0.5)
        slope_o[:, j * cols : (j + 1) * cols] = (gauss + pre * bell).astype(bf16)
        fwd_o[:, 2 * width + j * cols : 2 * width + (j + 1) * cols] = act
        wait(2 + 2 * j)
        branch += nn(act, wd_s[j])
    unit2, scale2 = row_norm(mixed + (branch + pack[9:10, :]))
    unit2_o[...] = unit2
    scale2_o[...] = jnp.broadcast_to(scale2, scale2_o.shape)
    y_o[...] = (unit2 * pack[6:7, :] + pack[8:9, :]).astype(bf16)


def rows_forward(layer, ids, pieces, u, packs, own, other):
    rows, width = u.shape
    ff = own[1].shape[1]
    steps = ff // width
    vm = pl.BlockSpec(memory_space=pltpu.VMEM)
    hbm = pl.BlockSpec(memory_space=pl.ANY)
    sds = jax.ShapeDtypeStruct
    return pl.pallas_call(
        partial(rows_kernel, layer),
        out_shape=[
            sds((rows, width), bf16),
            sds((rows, 2 * width + ff), bf16),
            sds((rows, ff), bf16),
            sds((rows, width), f32),
            sds((rows, width), f32),
            sds((rows, 128), f32),
            sds((rows, 128), f32),
        ],
        in_specs=[pl.BlockSpec(memory_space=pltpu.SMEM)] + [vm] * 7 + [hbm] * 6,
        out_specs=[vm] * 7,
        scratch_shapes=[
            pltpu.VMEM((width, width), bf16),
            pltpu.VMEM((steps, width, width), bf16),
            pltpu.VMEM((steps, width, width), bf16),
            pltpu.SemaphoreType.DMA((1 + 2 * steps,)),
        ],
        compiler_params=pltpu.CompilerParams(vmem_limit_bytes=VMEM_BYTES),
        cost_estimate=cost(10),
        name="rows_forward",
    )(ids, *pieces, u, *packs, own[0], other[0], own[1], other[1], own[2], other[2])


def norm_inward(unit, scaled, gain, upstream):
    d_unit = upstream * gain
    return scaled * (
        d_unit
        - jnp.mean(d_unit, axis=1, keepdims=True)
        - unit * jnp.mean(d_unit * unit, axis=1, keepdims=True)
    )


def rows_back_kernel(
    layer, ids, up, unit1, unit2, scale1, scale2, slope, pack_a, pack_b, wo_a, wo_b, wu_a, wu_b, wd_a, wd_b,
    first_o, d0, d1, d2, d3, keep_o, send_o, small_o,
    wo_s, wu_s, wd_s, sems,
):
    steps, cols = wu_s.shape[0], wu_s.shape[2]
    pairs = weight_pairs(steps, cols, wo_s, wu_s, wd_s)
    wait = fetch((wo_a, wu_a, wd_a), (wo_b, wu_b, wd_b), ids[4] != layer, pairs, sems)
    pack = jnp.where(ids[4] == layer, pack_a[...].astype(f32), pack_b[...].astype(f32))
    side = ids[4]
    half = first_o.shape[1] // 2
    ffh = keep_o.shape[1] - 2 * half

    def split(value, at):
        for s in range(2):

            @pl.when(side == s)
            def _(s=s):
                keep_o[:, at : at + half] = value[:, s * half : (s + 1) * half]
                send_o[:, at : at + half] = value[:, (1 - s) * half : (2 - s) * half]

    def total(value):
        return jnp.sum(value, axis=0, keepdims=True)

    upstream = up[...].astype(f32)
    unit = unit2[...]
    small_o[0:1, :] = total(upstream * unit)
    small_o[1:2, :] = total(upstream)
    d_second = norm_inward(unit, scale2[:, :1], pack[6:7, :], upstream)
    d_branch = d_second.astype(bf16)
    split(d_branch, ffh)
    small_o[5:6, :] = total(d_branch.astype(f32))
    d_mixed = d_second
    for j in range(steps):
        wait(2 + 2 * j)
        d_act = nt(d_branch, wd_s[j])
        d_pre = (d_act * slope[:, j * cols : (j + 1) * cols].astype(f32)).astype(bf16)
        small_o[6 + j : 7 + j, :] = total(d_pre.astype(f32))
        place = slice((j % (steps // 2)) * cols, (j % (steps // 2) + 1) * cols)

        @pl.when(side == j // (steps // 2))
        def _(d_pre=d_pre, place=place):
            keep_o[:, place] = d_pre

        @pl.when(side != j // (steps // 2))
        def _(d_pre=d_pre, place=place):
            send_o[:, place] = d_pre

        wait(1 + 2 * j)
        d_mixed += nt(d_pre, wu_s[j])
    unit = unit1[...]
    small_o[2:3, :] = total(d_mixed * unit)
    small_o[3:4, :] = total(d_mixed)
    d_first = norm_inward(unit, scale1[:, :1], pack[5:6, :], d_mixed)
    first_o[...] = d_first
    d_attn = d_first.astype(bf16)
    split(d_attn, ffh + half)
    small_o[4:5, :] = total(d_attn.astype(f32))
    small_o[10:, :] = jnp.zeros((small_o.shape[0] - 10, small_o.shape[1]), f32)
    wait(0)
    d_ctx = nt(d_attn, wo_s[...])
    hw = d0.shape[1]
    parts = [d_ctx[:, a * hw : (a + 1) * hw] for a in range(4)]
    for r, d_o in enumerate((d0, d1, d2, d3)):
        part = parts[0]
        for a in range(1, 4):
            part = jnp.where(ids[r] == a, parts[a], part)
        d_o[...] = part.astype(bf16)


def rows_back(layer, ids, upstream, kept, packs, own, other):
    rows, width = upstream.shape
    ff = own[1].shape[1]
    steps = ff // width
    hw = width // 4
    unit1, unit2, scale1, scale2, slope = kept
    vm = pl.BlockSpec(memory_space=pltpu.VMEM)
    hbm = pl.BlockSpec(memory_space=pl.ANY)
    sds = jax.ShapeDtypeStruct
    return pl.pallas_call(
        partial(rows_back_kernel, layer),
        out_shape=[sds((rows, width), f32)]
        + [sds((rows, hw), bf16)] * 4
        + [sds((rows, ff // 2 + width), bf16)] * 2
        + [sds((16, width), f32)],
        in_specs=[pl.BlockSpec(memory_space=pltpu.SMEM)] + [vm] * 8 + [hbm] * 6,
        out_specs=[vm] * 8,
        scratch_shapes=[
            pltpu.VMEM((width, width), bf16),
            pltpu.VMEM((steps, width, width), bf16),
            pltpu.VMEM((steps, width, width), bf16),
            pltpu.SemaphoreType.DMA((1 + 2 * steps,)),
        ],
        compiler_params=pltpu.CompilerParams(vmem_limit_bytes=VMEM_BYTES),
        cost_estimate=cost(11),
        name="rows_back",
    )(
        ids, upstream, unit1, unit2, scale1, scale2, slope, *packs,
        own[0], other[0], own[1], other[1], own[2], other[2],
    )


def rows_ahead(ids, pieces, u, pack, wait, weights, fwd_s, slope_s):
    wo_s, wu_s, wd_s = weights
    steps, cols = wu_s.shape[0], wu_s.shape[2]
    hw = pieces[0].shape[1]
    width = 4 * hw
    values = [c[...].astype(f32) for c in pieces]
    for a in range(4):
        part = values[0]
        for r in range(1, 4):
            part = jnp.where(ids[r] == a, values[r], part)
        fwd_s[:, width + a * hw : width + (a + 1) * hw] = part.astype(bf16)
    wait(0)
    attn = nn(fwd_s[:, width : 2 * width], wo_s[...]) + pack[4:5, :]
    unit1, scale1 = row_norm(u[...].astype(f32) + attn)
    mixed = unit1 * pack[5:6, :] + pack[7:8, :]
    low = mixed.astype(bf16)
    fwd_s[:, :width] = low
    branch = jnp.zeros(mixed.shape, f32)
    for j in range(steps):
        wait(1 + 2 * j)
        pre = nn(low, wu_s[j]) + pack[10 + j : 11 + j, :]
        gauss = 0.5 * (1.0 + lax.erf(pre * (2.0 ** -0.5)))
        act = (pre * gauss).astype(bf16)
        bell = jnp.exp(-0.5 * pre * pre) * ((2.0 * np.pi) ** -0.5)
        slope_s[:, j * cols : (j + 1) * cols] = (gauss + pre * bell).astype(bf16)
        fwd_s[:, 2 * width + j * cols : 2 * width + (j + 1) * cols] = act
        wait(2 + 2 * j)
        branch += nn(act, wd_s[j])
    unit2, scale2 = row_norm(mixed + (branch + pack[9:10, :]))
    return unit2 * pack[6:7, :] + pack[8:9, :], (unit1, scale1), (unit2, scale2)


def rows_behind(ids, upstream, norm1, norm2, pack, wait, weights, slope_s, outs):
    first_o, pieces, keep_s, send_s, small_o = outs
    wo_s, wu_s, wd_s = weights
    steps, cols = wu_s.shape[0], wu_s.shape[2]
    side = ids[4]
    half = first_o.shape[1] // 2
    ffh = keep_s.shape[1] - 2 * half

    def split(value, at):
        for s in range(2):

            @pl.when(side == s)
            def _(s=s):
                keep_s[:, at : at + half] = value[:, s * half : (s + 1) * half]
                send_s[:, at : at + half] = value[:, (1 - s) * half : (2 - s) * half]

    def total(value):
        return jnp.sum(value, axis=0, keepdims=True)

    unit, scaled = norm2
    small_o[0:1, :] = total(upstream * unit)
    small_o[1:2, :] = total(upstream)
    d_second = norm_inward(unit, scaled, pack[6:7, :], upstream)
    d_branch = d_second.astype(bf16)
    split(d_branch, ffh)
    small_o[5:6, :] = total(d_branch.astype(f32))
    d_mixed = d_second
    for j in range(steps):
        wait(2 + 2 * j)
        d_act = nt(d_branch, wd_s[j])
        d_pre = (d_act * slope_s[:, j * cols : (j + 1) * cols].astype(f32)).astype(bf16)
        small_o[6 + j : 7 + j, :] = total(d_pre.astype(f32))
        place = slice((j % (steps // 2)) * cols, (j % (steps // 2) + 1) * cols)

        @pl.when(side == j // (steps // 2))
        def _(d_pre=d_pre, place=place):
            keep_s[:, place] = d_pre

        @pl.when(side != j // (steps // 2))
        def _(d_pre=d_pre, place=place):
            send_s[:, place] = d_pre

        wait(1 + 2 * j)
        d_mixed += nt(d_pre, wu_s[j])
    unit, scaled = norm1
    small_o[2:3, :] = total(d_mixed * unit)
    small_o[3:4, :] = total(d_mixed)
    d_first = norm_inward(unit, scaled, pack[5:6, :], d_mixed)
    first_o[...] = d_first
    d_attn = d_first.astype(bf16)
    split(d_attn, ffh + half)
    small_o[4:5, :] = total(d_attn.astype(f32))
    small_o[10:, :] = jnp.zeros((small_o.shape[0] - 10, small_o.shape[1]), f32)
    wait(0)
    d_ctx = nt(d_attn, wo_s[...])
    hw = pieces[0].shape[1]
    parts = [d_ctx[:, a * hw : (a + 1) * hw] for a in range(4)]
    for r, d_o in enumerate(pieces):
        part = parts[0]
        for a in range(1, 4):
            part = jnp.where(ids[r] == a, parts[a], part)
        d_o[...] = part.astype(bf16)


def own_pack(layer, ids, pack_a, pack_b):
    return jnp.where(ids[4] == layer, pack_a[...].astype(f32), pack_b[...].astype(f32))


def rows_both_kernel(
    ids, c0, c1, c2, c3, u, up, pack_a, pack_b, wo_a, wo_b, wu_a, wu_b, wd_a, wd_b,
    y_o, first_o, d0, d1, d2, d3, small_o, keep_o, send_o, fwd_h,
    fwd_s, slope_s, out_sem, wo_s, wu_s, wd_s, sems,
):
    steps, cols = wu_s.shape[0], wu_s.shape[2]
    pairs = weight_pairs(steps, cols, wo_s, wu_s, wd_s)
    wait = fetch((wo_a, wu_a, wd_a), (wo_b, wu_b, wd_b), ids[4] != 1, pairs, sems)
    pack = own_pack(1, ids, pack_a, pack_b)
    weights = (wo_s, wu_s, wd_s)
    y, norm1, norm2 = rows_ahead(ids, (c0, c1, c2, c3), u, pack, wait, weights, fwd_s, slope_s)
    out = pltpu.make_async_copy(fwd_s, fwd_h, out_sem)
    out.start()
    y_o[...] = y.astype(bf16)
    rows_behind(
        ids, up[...].astype(f32), norm1, norm2, pack, lambda i: None, weights, slope_s,
        (first_o, (d0, d1, d2, d3), keep_o, send_o, small_o),
    )
    out.wait()


def rows_both(ids, pieces, u, upstream, packs, own, other):
    rows, width = u.shape
    ff = own[1].shape[1]
    steps = ff // width
    vm = pl.BlockSpec(memory_space=pltpu.VMEM)
    hbm = pl.BlockSpec(memory_space=pl.ANY)
    sds = jax.ShapeDtypeStruct
    res = pl.pallas_call(
        rows_both_kernel,
        out_shape=[sds((rows, width), bf16), sds((rows, width), f32)]
        + [sds((rows, width // 4), bf16)] * 4
        + [sds((16, width), f32)]
        + [sds((rows, ff // 2 + width), bf16)] * 2
        + [sds((rows, 2 * width + ff), bf16)],
        in_specs=[pl.BlockSpec(memory_space=pltpu.SMEM)] + [vm] * 8 + [hbm] * 6,
        out_specs=[vm] * 9 + [hbm],
        scratch_shapes=[
            pltpu.VMEM((rows, 2 * width + ff), bf16),
            pltpu.VMEM((rows, ff), bf16),
            pltpu.SemaphoreType.DMA,
            pltpu.VMEM((width, width), bf16),
            pltpu.VMEM((steps, width, width), bf16),
            pltpu.VMEM((steps, width, width), bf16),
            pltpu.SemaphoreType.DMA((1 + 2 * steps,)),
        ],
        compiler_params=pltpu.CompilerParams(vmem_limit_bytes=VMEM_BYTES),
        cost_estimate=cost(15),
        name="rows_both",
    )(
        ids, *pieces, u, upstream, *packs, own[0], other[0], own[1], other[1], own[2], other[2],
    )
    return res[0], res[9], res[1:9]


def grads_kernel(layer, ids, f0, f1, k0, k1, *refs):
    count = 1 if layer == 1 else 6
    targets, outs, (f, b, in_sems, out_sems) = refs[:count], refs[count : 2 * count], refs[2 * count :]
    rows = f0.shape[0]
    part = f0.shape[1] // 12
    width = 2 * part
    ffh = k0.shape[1] - width
    ins = []
    for at, n in [(None, None), (0, 2 * width)] + [(width * (2 + i), width) for i in range(4)]:
        for side, (fx, kx) in enumerate(((f0, k0), (f1, k1))):
            to = pl.ds(side * rows, rows)
            pair = (kx, b.at[to, :]) if at is None else (fx.at[:, pl.ds(at, n)], f.at[to, pl.ds(at, n)])
            ins += start_all(moves([pair], in_sems, len(ins)))
    wait_all(ins[:4])
    pre, branch, attn = b[:, :ffh], b[:, ffh : ffh + part], b[:, ffh + part :]
    if layer == 1:
        out, out_h = outs[0], targets[0]
        few, many = width // 16, 8 * part // 16
        blocks = ffh // part
        for j in range(2):
            at = j * part
            up = tn(f[:, at : at + part], pre).astype(bf16)
            last = tn(f[:, width + at : width + at + part], attn).astype(bf16)
            for s in range(8):
                cut = slice(s * few, (s + 1) * few)
                for i in range(blocks):
                    out[8 * j + s, i * few : (i + 1) * few, :] = up[cut, i * part : (i + 1) * part]
                out[8 * j + s, blocks * few : (blocks + 1) * few, :] = last[cut]
        sent = []
        for j in range(8):
            if j % 2 == 0:
                wait_all(ins[4 + j : 6 + j])
            at = 2 * width + j * part
            down = tn(f[:, at : at + part], branch).astype(bf16)
            for s in range(2):
                out[2 * j + s, (blocks + 1) * few :, :] = down[s * many : (s + 1) * many]
            pair = pl.ds(2 * j, 2)
            sent += start_all(moves([(out.at[pair], out_h.at[pair])], out_sems, j))
        wait_all(sent)
        return
    ua_o, ub_o, uk_o, da_o, db_o, dk_o = outs
    ua = ua_o.shape[1]
    small = dk_o.shape[1]
    sub = small // 2

    def rows_at(at):
        return f[:, pl.ds(pl.multiple_of(at, 128), part)]

    start = (1 - ids[5]) * part
    up = tn(rows_at(start), pre).astype(bf16)
    ua_o[...] = up[:, :ua]
    ub_o[:, : ffh - ua] = up[:, ua:]
    ub_o[:, ffh - ua :] = tn(rows_at(start + width), attn).astype(bf16)
    sent = start_all(moves(list(zip(outs[:2], targets[:2])), out_sems))
    start = ids[5] * part
    uk_o[:, :ffh] = tn(rows_at(start), pre).astype(bf16)
    uk_o[:, ffh:] = tn(rows_at(start + width), attn).astype(bf16)
    sent += start_all(moves([(uk_o, targets[2])], out_sems, 2))
    for j in range(8):
        if j % 2 == 0:
            wait_all(ins[4 + j : 6 + j])
        at = 2 * width + 2 * small * j
        down = tn(f[:, at : at + 2 * small], branch).astype(bf16)
        for low in range(2):
            block = down[small * low : small * (low + 1)]
            share = 2 * j + low
            place, mine = (share // 8) * 4 + share % 4, ids[6] == (share // 4) % 2

            @pl.when(mine)
            def _(block=block, place=place):
                dk_o[place] = block

            @pl.when(jnp.logical_not(mine))
            def _(block=block, place=place):
                da_o[place] = block[:sub]
                db_o[place] = block[sub:]

    wait_all(sent + start_all(moves(list(zip(outs[3:], targets[3:])), out_sems, 3)))


def grads(layer, ids, fwd, fwd_other, keep, got):
    width = HEAD * 12
    ff = 2 * (keep.shape[1] - width)
    part = width // 2
    ua = 1024
    small = ff // 16
    hbm = pl.BlockSpec(memory_space=pltpu.HBM)
    shapes = [
        (part, ua),
        (part, ff // 2 + part - ua),
        (part, ff // 2 + part),
        (8, small // 2, part),
        (8, small // 2, part),
        (8, small, part),
    ]
    if layer == 1:
        shapes = [(16, (ff // 2 // part + 1) * width // 16 + ff // 16, part)]
    return pl.pallas_call(
        partial(grads_kernel, layer),
        out_shape=[jax.ShapeDtypeStruct(shape, bf16) for shape in shapes],
        in_specs=[pl.BlockSpec(memory_space=pltpu.SMEM)] + [hbm] * 4,
        out_specs=[hbm] * len(shapes),
        scratch_shapes=[pltpu.VMEM(shape, bf16) for shape in shapes]
        + [
            pltpu.VMEM((2 * fwd.shape[0], fwd.shape[1]), bf16),
            pltpu.VMEM((2 * keep.shape[0], keep.shape[1]), bf16),
            pltpu.SemaphoreType.DMA((12,)),
            pltpu.SemaphoreType.DMA((8,)),
        ],
        compiler_params=pltpu.CompilerParams(vmem_limit_bytes=VMEM_BYTES),
        cost_estimate=cost(5),
        name="grads",
    )(ids, fwd, fwd_other, keep, got)


def proj_grads_kernel(ids, u_h, d_h, ra_h, rb_h, rk_h, u, d, ra_o, rb_o, rk_o, sems):
    wait_all(start_all(moves([(u_h, u), (d_h, d)], sems)))
    part = rk_o.shape[0]
    ra = ra_o.shape[1]
    rows = tn(u[:, pl.ds(pl.multiple_of((1 - ids[5]) * part, 128), part)], d[...]).astype(bf16)
    ra_o[...] = rows[:, :ra]
    rb_o[...] = rows[:, ra:]
    out = start_all(moves([(ra_o, ra_h), (rb_o, rb_h)], sems, 2))
    rk_o[...] = tn(u[:, pl.ds(pl.multiple_of(ids[5] * part, 128), part)], d[...]).astype(bf16)
    wait_all(out + start_all(moves([(rk_o, rk_h)], sems, 4)))


def proj_grads(ids, u, d):
    part = u.shape[1] // 2
    cols = d.shape[1]
    hbm = pl.BlockSpec(memory_space=pltpu.HBM)
    shapes = [(part, n) for n in (640, cols - 640, cols)]
    return pl.pallas_call(
        proj_grads_kernel,
        out_shape=[jax.ShapeDtypeStruct(shape, bf16) for shape in shapes],
        in_specs=[pl.BlockSpec(memory_space=pltpu.SMEM)] + [hbm] * 2,
        out_specs=[hbm] * 3,
        scratch_shapes=[pltpu.VMEM(shape, bf16) for shape in [u.shape, d.shape] + shapes]
        + [pltpu.SemaphoreType.DMA((5,))],
        compiler_params=pltpu.CompilerParams(vmem_limit_bytes=VMEM_BYTES),
        cost_estimate=cost(4),
        name="proj_grads",
    )(ids, u, d)


def assemble_kernel(sizes, ids, fk, fg, ak, ag, up_o, out_o, down_o, local_o, glob_o):
    share_w, share_f, ff, width = sizes
    part, hw = width // 2, width // 4
    core, x = ids[4], ids[6]
    for side in range(2):

        @pl.when(core == side)
        def _(side=side):
            halves = (fk, fg) if side == 0 else (fg, fk)
            for c, ref in enumerate(halves):
                for i in range(4):
                    to = c * (ff // 2) + i * part
                    up_o[:, to : to + part] = ref[i * share_w : (i + 1) * share_w, :]
                out_o[:, c * part : (c + 1) * part] = ref[4 * share_w : 5 * share_w, :]
                down_o[:, c * part : (c + 1) * part] = ref[5 * share_w :, :]

    held = []
    for group in range(4):
        pair = [jnp.where(core == group // 2, ak[i].astype(f32), ag[i].astype(f32)) for i in range(2)]
        held.append(jnp.where(x == group % 2, pair[0], pair[1]))
    for target, kinds in ((local_o, (0, 1, 2)), (glob_o, (5, 3, 4))):
        target[...] = jnp.concatenate(
            [held[g][:, k * hw : (k + 1) * hw] for k in kinds for g in range(4)], axis=1
        )


def assemble(ids, ffn_keep, ffn_got, att_keep, att_got, sizes):
    share_w, share_f, ff, width = sizes
    vm = pl.BlockSpec(memory_space=pltpu.VMEM)
    shapes = [(share_w, ff), (share_w, width), (share_f, width)] + [(share_w, 3 * width)] * 2
    return pl.pallas_call(
        partial(assemble_kernel, sizes),
        out_shape=[jax.ShapeDtypeStruct(shape, f32) for shape in shapes],
        in_specs=[pl.BlockSpec(memory_space=pltpu.SMEM)] + [vm] * 4,
        out_specs=[vm] * 5,
        compiler_params=pltpu.CompilerParams(vmem_limit_bytes=VMEM_BYTES),
        name="assemble",
    )(ids, ffn_keep, ffn_got, att_keep, att_got)


def core_flip(v):
    return lax.ppermute(v, SECTION, [(0, 1), (1, 0)])


def seq_flip(v, by):
    return lax.ppermute(v, SEQ, [(i, i ^ by) for i in range(4)])


def core_x_flip(v):
    return lax.ppermute(v, BOTH, [(i, i ^ 5) for i in range(8)])


def dp_flip(v, by):
    return lax.ppermute(v, DP, [(i, i ^ by) for i in range(lax.axis_size(DP))])


def pick(which, options):
    result = options[-1]
    for i in range(len(options) - 2, -1, -1):
        result = jnp.where(which == i, options[i], result)
    return result


def to_section(v, layer):
    near = [(y_ * 4 + 2 * y_ + x_, layer * 4 + 2 * y_ + x_) for y_ in (0, 1) for x_ in (0, 1)]
    far = [
        ((1 - y_) * 4 + 2 * y_ + x_, layer * 4 + 2 * (1 - y_) + x_) for y_ in (0, 1) for x_ in (0, 1)
    ]
    return lax.ppermute(v, BOTH, near), lax.ppermute(v, BOTH, far)


def by_micro(first, lower, upper, y):
    mine = jnp.where(first, lower[0], upper[0])
    away = jnp.where(first, lower[1], upper[1])
    return jnp.where(y == 0, jnp.stack([mine, away]), jnp.stack([away, mine]))


def two_chips(
    layer_in, cotangent, masked_rows, global_positions, local_weight, local_bias, global_weight,
    global_bias, out_weight, out_bias, norm_gain, norm_shift, up_weight, up_bias, down_weight,
    down_bias,
):
    c = lax.axis_index(SECTION)
    q = lax.axis_index(SEQ)
    z = lax.axis_index(DP)
    dp = lax.axis_size(DP)
    y, x = q // 2, q % 2
    g = 2 * c + x
    g_other = 2 * (1 - c) + x
    rows, width = layer_in.shape[2:]
    hw = width // 4
    ff = up_weight.shape[2]
    heads = hw // HEAD
    half_rows = rows // 2
    same = c == y
    first = c == 0

    block = layer_in[:, 0]

    def half_of(micro):
        return lax.dynamic_slice(block, (micro, c * half_rows, 0), (1, half_rows, width))[0]

    mine_part, away_part = half_of(y), half_of(1 - y)
    got = [seq_flip(mine_part, 1), seq_flip(away_part, 2), seq_flip(away_part, 3)]

    cot = cotangent[:, 0]
    marks = masked_rows[:, 0]

    def of_micro(v, micro):
        return lax.dynamic_index_in_dim(v, micro, 0, keepdims=False)

    cot_away = seq_flip(of_micro(cot, 1 - y), 2)
    marks_away = seq_flip(of_micro(marks, 1 - y), 2)

    ids = jnp.stack([g, g_other, 2 * c + 1 - x, 2 * (1 - c) + 1 - x, c, y, x, z]).astype(jnp.int32)
    ids, _ = lax.optimization_barrier((ids, (mine_part, away_part)))
    w_own, w_send, pack = prepare(
        ids,
        local_weight[0],
        global_weight[0],
        (local_bias[0], global_bias[0], out_bias, norm_gain[0], norm_shift[0], down_bias, up_bias),
    )
    own = (out_weight[0], up_weight[0], down_weight[0])
    other_up = core_flip(own[1])
    (w_own, w_send, pack), (got, other_up) = lax.optimization_barrier(
        ((w_own, w_send, pack), (got, other_up))
    )
    weights = (w_own, core_flip(w_send))
    packs = (pack, core_flip(pack))
    positions = of_micro(global_positions[:, 0], y)
    prow = positions[None, :]
    pcol = positions[:, None]
    parts = [block] + got + [core_flip(v) for v in got]
    own_late, _ = lax.optimization_barrier(((own[0], own[2]), (parts, weights, packs)))
    other_out, other_down = [core_flip(w) for w in own_late]
    other = (other_out, other_up, other_down)

    def exchange(pieces):
        return [pieces[0], core_flip(pieces[1]), seq_flip(pieces[2], 1), core_x_flip(pieces[3])]

    saved = []
    for layer in range(2):
        ctx, u_all, u_own, kept = attend(layer, ids, parts, weights, packs, prow, pcol)
        if layer == 0:
            ctx, other = lax.optimization_barrier((ctx, other))
        pieces = exchange(ctx)
        if layer == 0:
            res = rows_forward(layer, ids, pieces, u_own, packs, own, other)
            y_low, fwd, slope, *row_kept = res
            row_kept.append(slope)
            across = seq_flip(y_low, 1)
            across, (cot_away, marks_away, fwd_other) = lax.optimization_barrier(
                (across, (cot_away, marks_away, core_flip(fwd)))
            )
            parts = [y_low, core_flip(y_low), across, core_flip(across)]
            saved_low = y_low
            saved.append((u_all, kept, fwd, fwd_other, row_kept))
        else:
            pieces, out0 = lax.optimization_barrier((pieces, to_section(saved_low, 0)))
            cot_rows = jnp.where(same, of_micro(cot, y), cot_away)
            cot_marks = jnp.where(same, of_micro(marks, y), marks_away)
            row_hit = (g * rows + jnp.arange(rows))[:, None] == cot_marks[None, :]
            upstream = nn(row_hit.astype(bf16), cot_rows).astype(bf16)
            y_low, fwd, back = rows_both(ids, pieces, u_own, upstream, packs, own, other)

    flip_x = partial(seq_flip, by=1)
    flip_y = partial(seq_flip, by=2)
    flip_z1 = partial(dp_flip, by=1)
    flip_z2 = partial(dp_flip, by=2)
    low_z, high_z = z % 2, z // 2

    def after(value, others):
        return lax.optimization_barrier((value, others))

    def cut(value, axis, bit):
        return of_axis(value, axis, 1 - bit).astype(bf16), of_axis(value, axis, bit)

    def of_axis(value, axis, index):
        return lax.dynamic_index_in_dim(value, index, axis, keepdims=False)

    def plus(keep, got):
        return keep.astype(f32) + got.astype(f32)

    def bias_rows(small, bias):
        placed = jnp.concatenate([jnp.where(g == i, bias, 0.0) for i in range(4)], axis=1)
        return jnp.concatenate([small[:10], placed], axis=0)

    def inward(partials):
        low = [core_flip(partials[1]), core_flip(partials[3])]
        return plus(partials[0], low[0]), plus(partials[2], low[1]).astype(bf16)

    ua = 1024
    share_w = width // (4 * dp)
    share_f = ff // (4 * dp)
    sub = share_f // 2
    part = width // 2

    d_first, pieces, (small, keep, send) = back[0], exchange(back[1:5]), back[5:]
    gr = grads(1, ids, fwd, core_flip(fwd), keep, core_flip(send))
    pieces, gr = after(pieces, gr)
    ffn1 = lax.psum_scatter(gr[0], SEQ, scatter_dimension=0, tiled=True)
    res = attend_back(1, ids, pieces, kept, prow, pcol, weights)
    d_all, bias, partials = res
    small1 = bias_rows(small, bias)
    summed, send = inward(partials)
    across = flip_x(send)
    d_all, send = after(d_all, send)
    gr = proj_grads(ids, u_all, d_all)
    across, gr = after(across, gr)
    r1a, r1b, r1k = gr
    d_upper = (d_first + summed + across.astype(f32)).astype(bf16)

    got_r1a = flip_y(r1a)
    u_all, kept, fwd, fwd_other, row_kept = saved[0]
    res = rows_back(0, ids, d_upper, row_kept, packs, own, other)
    res, got_r1a = after(res, got_r1a)
    d_first, pieces, (keep, send, small) = res[0], exchange(res[1:5]), res[5:]
    got_r1b = flip_y(r1b)
    gr = grads(0, ids, fwd, fwd_other, keep, core_flip(send))
    pieces, gr = after(pieces, gr)
    u0a, u0b, u0k, d0a, d0b, d0k = gr
    got_u0a, got_d0a, got_u0b, got_d0b = flip_y(u0a), flip_x(d0a), flip_y(u0b), flip_x(d0b)
    res = attend_back(0, ids, pieces, kept, prow, pcol, weights)
    (res, y_low, d_upper), (got_u0a, got_d0a, got_r1b, ffn1) = after(
        (res, y_low, d_upper), (got_u0a, got_d0a, got_r1b, ffn1)
    )
    ffn1 = lax.psum_scatter(ffn1, DP, scatter_dimension=0, tiled=True)[0]
    d_all, bias, partials = res
    small0 = bias_rows(small, bias)

    def step(flights):
        sends = lax.optimization_barrier([send for _, send in flights])
        return [flip(send) for (flip, _), send in zip(flights, sends)]

    def end(got, *more):
        return lax.optimization_barrier((got, more))

    swapped = partial(jnp.where, first)
    small_keep, small_send = swapped(small0, small1), swapped(small1, small0)
    small = small_keep + core_flip(small_send)
    r1 = plus(r1k, jnp.concatenate([got_r1a, got_r1b], axis=1)).astype(bf16)
    r1_send, r1_keep = cut(r1.reshape(2, 2, 2, share_w, -1), 2, low_z)
    summed, d_send = inward(partials)
    got = step([(flip_x, d_send), (flip_z1, r1_send), (flip_x, small)])
    gr = proj_grads(ids, u_all, d_all)
    got, ends = end(got, got_u0b, got_d0b, gr)
    got_u0b, got_d0b, (r0a, r0b, r0k) = ends

    d_lower = (d_first + summed + got[0].astype(f32)).astype(bf16)
    u0 = plus(u0k, jnp.concatenate([got_u0a, got_u0b], axis=1)).astype(bf16)
    u0_send, u0_keep = cut(u0.reshape(2, 2, 2, share_w, -1), 2, low_z)
    r1_send, r1_keep = cut(plus(r1_keep, got[1]).astype(bf16), 1, high_z)
    small = small + got[2]
    got = step([(flip_y, r0a), (flip_z1, u0_send), (flip_y, r0b), (flip_z2, r1_send)])
    d0 = plus(d0k, jnp.concatenate([got_d0a, got_d0b], axis=1)).astype(bf16)
    d0_send, d0_keep = cut(d0.reshape(2, 2, 2, share_f, part), 0, y)
    got, ends = end(got, d0_send)
    d0_send = ends[0]

    u0_send, u0_keep = cut(plus(u0_keep, got[1]).astype(bf16), 1, high_z)
    r0 = plus(r0k, jnp.concatenate([got[0], got[2]], axis=1)).astype(bf16)
    r0_send, r0_keep = cut(r0.reshape(2, 2, 2, share_w, -1), 2, low_z)
    r1_send, r1_keep = cut(plus(r1_keep, got[3]).astype(bf16), 0, x)
    got = step([(flip_z2, u0_send), (flip_y, d0_send), (flip_z1, r0_send), (flip_z1, small)])
    in0 = to_section(d_lower, 0)
    got, ends = end(got, in0, ffn1)
    (near0, far0), ffn1 = ends

    u0_send, u0_keep = cut(plus(u0_keep, got[0]).astype(bf16), 0, x)
    d0_send, d0_keep = cut(plus(d0_keep, got[1]).astype(bf16), 1, low_z)
    r0_send, r0_keep = cut(plus(r0_keep, got[2]).astype(bf16), 1, high_z)
    small = small + got[3]
    got = step([(flip_z2, r0_send), (flip_z1, d0_send), (flip_x, u0_send), (flip_y, small), (flip_x, r1_send)])
    upper = to_section(jnp.stack([y_low, d_upper]), 1)
    got, ends = end(got, upper)
    out1, (near1, far1) = [(ends[0][0][i], ends[0][1][i]) for i in range(2)]
    r1_got = got[4]

    few = 5 * share_w
    one0 = plus(u0_keep, got[2])
    d0_send, d0_keep = cut(plus(d0_keep, got[1]).astype(bf16), 0, high_z)
    r0_send, r0_keep = cut(plus(r0_keep, got[0]).astype(bf16), 0, x)
    small = small + got[3]
    got = step([(flip_z2, d0_send), (flip_x, r0_send), (flip_z2, small)])
    got = end(got)[0]
    two0 = plus(d0_keep, got[0])
    small = small + got[2]

    lower = jnp.concatenate(
        [one0[:, i * part : (i + 1) * part] for i in range(5)] + [two0], axis=0
    )
    upper = ffn1.astype(f32)
    ffn_keep, ffn_send = swapped(lower, upper), swapped(upper, lower)
    att0, att1 = jnp.stack([r0_keep, got[1]]), jnp.stack([r1_keep, r1_got])
    att_keep, att_send = swapped(att0, att1), swapped(att1, att0)
    ffn_got, att_got = core_flip(ffn_send), core_flip(att_send)
    grad_up, grad_out, grad_down, grad_local, grad_glob = assemble(
        ids, ffn_keep, ffn_got, att_keep, att_got, (share_w, share_f, ff, width)
    )

    at = q * dp + z
    piece = partial(lax.dynamic_slice_in_dim, axis=0)
    outs = (
        grad_local,
        jnp.stack([small[10], small[11]]),
        grad_glob,
        jnp.stack([small[12], small[13]]),
        grad_out,
        piece(small[4], at * share_w, share_w),
        jnp.stack([small[2], small[0]]),
        jnp.stack([small[3], small[1]]),
        grad_up,
        piece(small[6:10].reshape(ff), at * (ff // (4 * dp)), ff // (4 * dp)),
        grad_down,
        piece(small[5], at * share_w, share_w),
    )
    layer_outputs = by_micro(first, out0, out1, y)
    in_grads = by_micro(first, (near0, far0), (near1, far1), y)
    return (layer_outputs[None, :, None], in_grads[None, :, None]) + tuple(o[None] for o in outs)


def fits_two_chips(mesh, layer_in):
    sizes = dict(mesh.shape)
    micro, _, length, width = layer_in.shape
    dp = sizes[DP]
    return (
        sizes[SECTION] == 2
        and sizes[SEQ] == 4
        and micro == 2
        and dp == 4
        and length == 4 * HALF
        and width == 12 * HEAD
    )


def solution(mesh):
    in_specs = (
        P(None, DP, SEQ, None),
        P(None, DP, SEQ, None),
        P(None, DP, SEQ),
        P(None, DP, None),
        P(SECTION, None, None),
        P(SECTION, None, None),
        P(SECTION, None, None),
        P(SECTION, None, None),
        P(SECTION, None, None),
        P(SECTION, None),
        P(SECTION, None, None),
        P(SECTION, None, None),
        P(SECTION, None, None),
        P(SECTION, None),
        P(SECTION, None, None),
        P(SECTION, None),
    )
    out_specs = (
        P(SECTION, None, DP, SEQ, None),
        P(SECTION, None, DP, SEQ, None),
        P(SECTION, (SEQ, DP), None),
        P(SECTION, None, None),
        P(SECTION, (SEQ, DP), None),
        P(SECTION, None, None),
        P(SECTION, (SEQ, DP), None),
        P(SECTION, (SEQ, DP)),
        P(SECTION, None, None),
        P(SECTION, None, None),
        P(SECTION, (SEQ, DP), None),
        P(SECTION, (SEQ, DP)),
        P(SECTION, (SEQ, DP), None),
        P(SECTION, (SEQ, DP)),
    )

    def run(layer_in, *rest):
        body = two_chips if fits_two_chips(mesh, layer_in) else on_device
        return jax.shard_map(
            body, mesh=mesh, in_specs=in_specs, out_specs=out_specs, check_vma=False
        )(layer_in, *rest)

    return run
```

profile of v0, /device:TPU:0, one launch (start us, length us, event | category | flops | bytes accessed | tf_op | source)
XLA Modules:
  0.0 373.2 jit_solution(7537972370778237719)
XLA Ops:
  8.8 2.6 collective-permute-start.1
  11.4 1.4 collective-permute-start.2
  17.9 3.4 prepare.1
  23.7 3.5 collective-permute-done.8.refs_11_.pack_b.refs_8_
  28.5 15.1 %attend.2 = (bf16[256,192]{1,0:T(8,128)(2,1)S(1)}, bf16[256,192]{1,0:T(8,128)(2,1)S(1)}, bf16[256,192]{1,0:T(8,128)(2,1)S(1)}, bf16[256,192]{1,0:T(8,128)(2,1)S(...) custom-call(s32[8]{0:T(128)S(1)} %stack.98.ids.refs_0_, ...), custom_call_target="tpu_custom_call" | custom-call | flops 14000000000 | bytes 49000000 | tf_op jit(solution)/shard_map/attend/pallas_call | solution.py:845
  45.6 1.9 collective-permute-start.12
  47.6 4.3 %collective-permute-done.12.c2 = bf16[256,192]{1,0:T(8,128)(2,1)S(1)} collective-permute-done((bf16[256,192]{1,0:T(8,128)(2,1)S(1)}, bf16[256,192]{1,0:T(8,128)(2,1)S(1)}, u32[]{:S(2)}, u32[]{:S(2)}) %collective-permute-start.12) | collective-permute-done | bytes 98336 | tf_op jit(solution)/shard_map/ppermute | solution.py:1576
  51.9 2.1 collective-permute-done.13.c3
  54.0 8.9 %rows_forward.1 = (bf16[256,768]{1,0:T(8,128)(2,1)S(1)}, bf16[256,4608]{1,0:T(8,128)(2,1)}, bf16[256,3072]{1,0:T(8,128)(2,1)}, f32[256,768]{1,0:T(8,128)S(1)}, f...) custom-call(s32[8]{0:T(128)S(1)} %stack.98.ids.refs_0_, ...), custom_call_target="tpu_custom_call" | custom-call | flops 10000000000 | bytes 35000000 | tf_op jit(solution)/shard_map/rows_forward/pallas_call | solution.py:1095
  65.0 1.7 collective-permute-start.15
  67.0 1.6 collective-permute-start.16
  69.1 3.0 collective-permute-done.17
  72.1 4.1 %collective-permute-done.15.refs_3_ = bf16[256,768]{1,0:T(8,128)(2,1)S(1)} collective-permute-done((bf16[256,768]{1,0:T(8,128)(2,1)S(1)}, bf16[256,768]{1,0:T(8,128)(2,1)S(1)}, u32[]{:S(2)}, u32[]{:S(2)}) %collective-permute-start.15) | collective-permute-done | bytes 393248 | tf_op jit(solution)/shard_map/ppermute | solution.py:1576
  77.0 1.5 collective-permute-start.24
  78.6 14.6 %attend.3 = (bf16[256,192]{1,0:T(8,128)(2,1)S(1)}, bf16[256,192]{1,0:T(8,128)(2,1)S(1)}, bf16[256,192]{1,0:T(8,128)(2,1)S(1)}, bf16[256,192]{1,0:T(8,128)(2,1)S(...) custom-call(s32[8]{0:T(128)S(1)} %stack.98.ids.refs_0_, ...), custom_call_target="tpu_custom_call" | custom-call | flops 14000000000 | bytes 49000000 | tf_op jit(solution)/shard_map/attend/pallas_call | solution.py:845
  94.1 2.9 collective-permute-start.20
  97.0 1.5 collective-permute-start.21
  98.9 4.5 %collective-permute-done.21.c2 = bf16[256,192]{1,0:T(8,128)(2,1)S(1)} collective-permute-done((bf16[256,192]{1,0:T(8,128)(2,1)S(1)}, bf16[256,192]{1,0:T(8,128)(2,1)S(1)}, u32[]{:S(2)}, u32[]{:S(2)}) %collective-permute-start.21) | collective-permute-done | bytes 98336 | tf_op jit(solution)/shard_map/ppermute | solution.py:1576
  104.3 27.3 %rows_both.1 = (bf16[256,768]{1,0:T(8,128)(2,1)S(1)}, f32[256,768]{1,0:T(8,128)S(1)}, bf16[256,192]{1,0:T(8,128)(2,1)S(1)}, bf16[256,192]{1,0:T(8,128)(2,1)S(1)}...) custom-call(s32[8]{0:T(128)S(1)} %stack.98.ids.refs_0_, ...), custom_call_target="tpu_custom_call" | custom-call | flops 15000000512 | bytes 52500000 | tf_op jit(solution)/shard_map/rows_both/pallas_call | solution.py:1359
  133.5 1.5 collective-permute-start.26
  135.0 4.2 %collective-permute-done.29.k1 = bf16[256,2304]{1,0:T(8,128)(2,1)S(1)} collective-permute-done((bf16[256,2304]{1,0:T(8,128)(2,1)}, bf16[256,2304]{1,0:T(8,128)(2,1)S(1)}, u32[]{:S(2)}, u32[]{:S(2)}) %collective-permute-start.29) | collective-permute-done | bytes 1179680 | tf_op jit(solution)/shard_map/ppermute | solution.py:1572
  139.2 1.5 copy-done.56
  142.0 7.7 %grads.2 = bf16[16,432,384]{2,1,0:T(8,128)(2,1)} custom-call(s32[8]{0:T(128)S(1)} %stack.98.ids.refs_0_, bf16[256,4608]{1,0:T(8,128)(2,1)} %get-tuple-element.263.f0, bf16[256,4608]{1,0:T(8,128)(2,1)} %copy-done.56, bf16[256,2304]{1,0:T(8,128)(2,1)S(1)} %copy-done.17, bf16[256,2304]{1,0:T(8,128)(2,1)S(1)} %collective-permute-done.29.k1), custom_call_target="tpu_custom_call" | custom-call | flops 5000000000 | bytes 17500000 | tf_op jit(solution)/shard_map/grads/pallas_call | solution.py:1483
  150.8 18.0 %attend_back.2 = (bf16[1024,1152]{1,0:T(8,128)(2,1)}, f32[4,192]{1,0:T(4,128)S(1)}, f32[256,768]{1,0:T(8,128)S(1)}, bf16[256,768]{1,0:T(8,128)(2,1)S(1)}, f32[25...) custom-call(s32[8]{0:T(128)S(1)} %stack.98.ids.refs_0_, bf16[256,192]{1,0:T(8,128)(2,1)S(1)} %get-tuple-element.266.d0, ...), custom_call_target="tpu_custom_call" | custom-call | flops 17999998976 | bytes 63000000 | tf_op jit(solution)/shard_map/attend_back/pallas_call | solution.py:986
  170.7 1.6 collective-permute-start.32
  172.3 5.7 %proj_grads.2 = (bf16[384,640]{1,0:T(8,128)(2,1)S(1)}, bf16[384,512]{1,0:T(8,128)(2,1)}, bf16[384,1152]{1,0:T(8,128)(2,1)S(1)}) custom-call(s32[8]{0:T(128)S(1)} %stack.98.ids.refs_0_, bf16[1024,768]{1,0:T(8,128)(2,1)S(1)} %copy-done.19, bf16[1024,1152]{1,0:T(8,128)(2,1)} %get-tuple-element.285.d_h), custom_call_target="tpu_custom_call" | custom-call | flops 4000000000 | bytes 14000000 | tf_op jit(solution)/shard_map/proj_grads/pallas_call | solution.py:1518
  178.1 12.9 %collective-permute-done.32 = bf16[256,768]{1,0:T(8,128)(2,1)S(1)} collective-permute-done((bf16[256,768]{1,0:T(8,128)(2,1)S(1)}, bf16[256,768]{1,0:T(8,128)(2,1)S(1)}, u32[]{:S(2)}, u32[]{:S(2)}) %collective-permute-start.32) | collective-permute-done | bytes 393248 | tf_op jit(solution)/shard_map/ppermute | solution.py:1576
  191.7 11.1 %rows_back.1 = (f32[256,768]{1,0:T(8,128)S(1)}, bf16[256,192]{1,0:T(8,128)(2,1)S(1)}, bf16[256,192]{1,0:T(8,128)(2,1)S(1)}, bf16[256,192]{1,0:T(8,128)(2,1)S(1)}...) custom-call(s32[8]{0:T(128)S(1)} %stack.98.ids.refs_0_, ...), custom_call_target="tpu_custom_call" | custom-call | flops 11000000512 | bytes 38500000 | tf_op jit(solution)/shard_map/rows_back/pallas_call | solution.py:1208
  204.6 1.5 collective-permute-start.40
  206.3 1.4 collective-permute-start.35
  208.0 9.6 %grads.3 = (bf16[384,1024]{1,0:T(8,128)(2,1)S(1)}, bf16[384,896]{1,0:T(8,128)(2,1)}, bf16[384,1920]{1,0:T(8,128)(2,1)}, bf16[8,96,384]{2,1,0:T(8,128)(2,1)S(1)},...) custom-call(s32[8]{0:T(128)S(1)} %stack.98.ids.refs_0_, bf16[256,4608]{1,0:T(8,128)(2,1)} %get-tuple-element.244.f0, ...), custom_call_target="tpu_custom_call" | custom-call | flops 5000000000 | bytes 17500000 | tf_op jit(solution)/shard_map/grads/pallas_call | solution.py:1483
  217.6 2.6 collective-permute-done.36.d3
  220.8 1.5 collective-permute-start.39
  224.3 18.0 %attend_back.3 = (bf16[1024,1152]{1,0:T(8,128)(2,1)}, f32[4,192]{1,0:T(4,128)S(1)}, f32[256,768]{1,0:T(8,128)S(1)}, bf16[256,768]{1,0:T(8,128)(2,1)S(1)}, f32[25...) custom-call(s32[8]{0:T(128)S(1)} %stack.98.ids.refs_0_, bf16[256,192]{1,0:T(8,128)(2,1)S(1)} %get-tuple-element.317.d0, ...), custom_call_target="tpu_custom_call" | custom-call | flops 17999998976 | bytes 63000000 | tf_op jit(solution)/shard_map/attend_back/pallas_call | solution.py:986
  246.9 1.4 add_convert_fusion.3
  250.1 1.5 collective-permute-start.44
  251.7 1.4 collective-permute-start.43
  253.8 1.4 copy-done.18
  255.2 5.9 %proj_grads.3 = (bf16[384,640]{1,0:T(8,128)(2,1)S(1)}, bf16[384,512]{1,0:T(8,128)(2,1)S(1)}, bf16[384,1152]{1,0:T(8,128)(2,1)S(1)}) custom-call(s32[8]{0:T(128)S(1)} %stack.98.ids.refs_0_, bf16[1024,768]{1,0:T(8,128)(2,1)S(1)} %copy-done.18, bf16[1024,1152]{1,0:T(8,128)(2,1)} %get-tuple-element.356.d_h), custom_call_target="tpu_custom_call" | custom-call | flops 4000000000 | bytes 14000000 | tf_op jit(solution)/shard_map/proj_grads/pallas_call | solution.py:1518
  261.2 2.5 collective-permute-done.45
  263.7 3.9 %collective-permute-done.44 = bf16[2,2,48,1152]{3,2,0,1:T(8,128)(2,1)S(1)} collective-permute-done((bf16[2,2,48,1152]{3,2,0,1:T(8,128)(2,1)}, bf16[2,2,48,1152]{3,2,0,1:T(8,128)(2,1)S(1)}, u32[]{:S(2)}, u32[]{:S(2)}) %collective-permute-start.44) | collective-permute-done | bytes 442400 | tf_op jit(solution)/shard_map/ppermute | solution.py:1584
  267.7 1.8 add_convert_fusion
  271.8 2.0 collective-permute-start.50
  273.8 1.4 add_convert_fusion.1
  275.5 6.1 %collective-permute-start.51 = (bf16[2,48,1152]{2,1,0:T(8,128)(2,1)S(1)}, bf16[2,48,1152]{2,1,0:T(8,128)(2,1)S(1)}, u32[]{:S(2)}, u32[]{:S(2)}) collective-permute-start(bf16[2,48,1152]{2,1,0:T(8,128)(2,1)S(1)} %dynamic-slice_bitcast_fusion.3), channel_id=1, source_target_pairs={{0,2},{1,3},{2,0},{3,1},{4,6},{5,7},{6,4},{7,5},{8,10},{9,11},{10,... | collective-permute-start | bytes 663560 | tf_op jit(solution)/shard_map/ppermute | solution.py:1584
  282.4 21.2 %collective-permute-done.51 = bf16[2,48,1152]{2,1,0:T(8,128)(2,1)S(1)} collective-permute-done((bf16[2,48,1152]{2,1,0:T(8,128)(2,1)S(1)}, bf16[2,48,1152]{2,1,0:T(8,128)(2,1)S(1)}, u32[]{:S(2)}, u32[]{:S(2)}) %collective-permute-start.51) | collective-permute-done | bytes 221216 | tf_op jit(solution)/shard_map/ppermute | solution.py:1584
  303.6 1.5 collective-permute-start.58
  305.7 2.7 collective-permute-start.53
  308.4 3.5 collective-permute-start.54
  311.9 2.0 collective-permute-start.55
  314.6 2.2 collective-permute-done.58
  316.8 2.2 collective-permute-start.64
  319.0 10.9 %collective-permute-done.55 = f32[14,768]{1,0:T(8,128)S(1)} collective-permute-done((f32[14,768]{1,0:T(8,128)S(1)}, f32[14,768]{1,0:T(8,128)S(1)}, u32[]{:S(2)}, u32[]{:S(2)}) %collective-permute-start.55) | collective-permute-done | bytes 43040 | tf_op jit(solution)/shard_map/ppermute | solution.py:1584
  329.9 1.5 collective-permute-start.65
  333.9 1.8 collective-permute-start.60
  335.8 1.5 collective-permute-start.61
  337.9 4.8 %collective-permute-start.62 = (f32[14,768]{1,0:T(8,128)S(1)}, f32[14,768]{1,0:T(8,128)S(1)}, u32[]{:S(2)}, u32[]{:S(2)}) collective-permute-start(f32[14,768]{1,0:T(8,128)S(1)} %add.228), channel_id=1, source_target_pairs={{0,8},{4,12},{8,0},{12,4},{1,9},{5,13},{9,1},{13,5},{2,10},{6,14},... | collective-permute-start | bytes 129032 | tf_op jit(solution)/shard_map/ppermute | solution.py:1576
  342.7 2.1 collective-permute-done.62
  345.7 1.8 collective-permute-done.59
  348.3 2.9 collective-permute-start.66
  351.2 1.5 collective-permute-start.67
  353.0 1.5 fusion.8
  356.5 4.1 %collective-permute-done.68 = f32[14,768]{1,0:T(8,128)S(1)} collective-permute-done((f32[14,768]{1,0:T(8,128)S(1)}, f32[14,768]{1,0:T(8,128)S(1)}, u32[]{:S(2)}, u32[]{:S(2)}) %collective-permute-start.68) | collective-permute-done | bytes 43040 | tf_op jit(solution)/shard_map/ppermute | solution.py:1584
  364.0 2.1 assemble.1
  (285 shorter events, 51.8 us)
Async XLA Ops:
  7.2 239.0 %reduce-scatter.3.cloned.1.call-start = ((), (), s32[]{:S(2)}) async-start(), calls=%async_computation.2 | async-start | bytes 6635520 | tf_op jit(solution)/shard_map/reduce_scatter | solution.py:1731
  7.2 15.3 %collective-permute-start.3 = (bf16[768,3072]{1,0:T(8,128)(2,1)}, bf16[768,3072]{1,0:T(8,128)(2,1)}, u32[]{:S(2)}, u32[]{:S(2)}) collective-permute-start(bf16[768,3072]{1,0:T(8,128)(2,1)} %bitcast.178), channel_id=1, source_target_pairs={{0,16},{16,0},{1,17},{17,1},{2,18},{18,2},{3,19},{19,3},{4,20},{20... | collective-permute-start | bytes 14155784 | tf_op jit(solution)/shard_map/ppermute | solution.py:1572
  8.8 13.7 %collective-permute-start.1 = (bf16[128,768]{1,0:T(8,128)(2,1)S(1)}, bf16[128,768]{1,0:T(8,128)(2,1)S(1)}, u32[]{:S(2)}, u32[]{:S(2)}) collective-permute-start(bf16[128,768]{1,0:T(8,128)(2,1)S(1)} %get-tuple-element.436), channel_id=1, source_target_pairs={{0,8},{4,12},{8,0},{12,4},{1,9},{5,13},{9,1},{13,5},{2,10},{6,14},... | collective-permute-start | bytes 589832 | tf_op jit(solution)/shard_map/ppermute | solution.py:1576
  11.4 11.1 %collective-permute-start.2 = (bf16[128,768]{1,0:T(8,128)(2,1)S(1)}, bf16[128,768]{1,0:T(8,128)(2,1)S(1)}, u32[]{:S(2)}, u32[]{:S(2)}) collective-permute-start(bf16[128,768]{1,0:T(8,128)(2,1)S(1)} %get-tuple-element.436), channel_id=1, source_target_pairs={{0,12},{4,8},{8,4},{12,0},{1,13},{5,9},{9,5},{13,1},{2,14},{6,10},... | collective-permute-start | bytes 589832 | tf_op jit(solution)/shard_map/ppermute | solution.py:1576
  12.9 9.6 %collective-permute-start = (bf16[128,768]{1,0:T(8,128)(2,1)S(1)}, bf16[128,768]{1,0:T(8,128)(2,1)S(1)}, u32[]{:S(2)}, u32[]{:S(2)}) collective-permute-start(bf16[128,768]{1,0:T(8,128)(2,1)S(1)} %get-tuple-element.437), channel_id=1, source_target_pairs={{0,4},{4,0},{8,12},{12,8},{1,5},{5,1},{9,13},{13,9},{2,6},{6,2},{1... | collective-permute-start | bytes 589832 | tf_op jit(solution)/shard_map/ppermute | solution.py:1576
  22.5 4.7 %collective-permute-start.7 = (bf16[768,1152]{1,0:T(8,128)(2,1)S(1)}, bf16[768,1152]{1,0:T(8,128)(2,1)S(1)}, u32[]{:S(2)}, u32[]{:S(2)}) collective-permute-start(bf16[768,1152]{1,0:T(8,128)(2,1)S(1)} %get-tuple-element.226), channel_id=1, source_target_pairs={{0,16},{16,0},{1,17},{17,1},{2,18},{18,2},{3,19},{19,3},{4,20},{20... | collective-permute-start | bytes 5308424 | tf_op jit(solution)/shard_map/ppermute | solution.py:1572
  22.6 4.6 %collective-permute-start.4 = (bf16[128,768]{1,0:T(8,128)(2,1)S(1)}, bf16[128,768]{1,0:T(8,128)(2,1)S(1)}, u32[]{:S(2)}, u32[]{:S(2)}) collective-permute-start(bf16[128,768]{1,0:T(8,128)(2,1)S(1)} %collective-permute-done.refs_2_), channel_id=1, source_target_pairs={{0,16},{16,0},{1,17},{17,1},{2,18},{18,2},{3,19},{19,3},{4,20},{20... | collective-permute-start | bytes 589832 | tf_op jit(solution)/shard_map/ppermute | solution.py:1572
  23.1 4.1 %collective-permute-start.5 = (bf16[128,768]{1,0:T(8,128)(2,1)S(1)}, bf16[128,768]{1,0:T(8,128)(2,1)S(1)}, u32[]{:S(2)}, u32[]{:S(2)}) collective-permute-start(bf16[128,768]{1,0:T(8,128)(2,1)S(1)} %collective-permute-done.1.refs_3_), channel_id=1, source_target_pairs={{0,16},{16,0},{1,17},{17,1},{2,18},{18,2},{3,19},{19,3},{4,20},{20... | collective-permute-start | bytes 589832 | tf_op jit(solution)/shard_map/ppermute | solution.py:1572
  23.2 4.0 %collective-permute-start.6 = (bf16[128,768]{1,0:T(8,128)(2,1)S(1)}, bf16[128,768]{1,0:T(8,128)(2,1)S(1)}, u32[]{:S(2)}, u32[]{:S(2)}) collective-permute-start(bf16[128,768]{1,0:T(8,128)(2,1)S(1)} %collective-permute-done.2.refs_4_), channel_id=1, source_target_pairs={{0,16},{16,0},{1,17},{17,1},{2,18},{18,2},{3,19},{19,3},{4,20},{20... | collective-permute-start | bytes 589832 | tf_op jit(solution)/shard_map/ppermute | solution.py:1572
  23.6 3.5 collective-permute-start.8
  27.2 18.2 %collective-permute-start.10 = (bf16[3072,768]{1,0:T(8,128)(2,1)}, bf16[3072,768]{1,0:T(8,128)(2,1)}, u32[]{:S(2)}, u32[]{:S(2)}) collective-permute-start(bf16[3072,768]{1,0:T(8,128)(2,1)} %bitcast.21.wd_a), channel_id=1, source_target_pairs={{0,16},{16,0},{1,17},{17,1},{2,18},{18,2},{3,19},{19,3},{4,20},{20... | collective-permute-start | bytes 14155784 | tf_op jit(solution)/shard_map/ppermute | solution.py:1572
  27.5 17.9 %collective-permute-start.9 = (bf16[768,768]{1,0:T(8,128)(2,1)}, bf16[768,768]{1,0:T(8,128)(2,1)S(1)}, u32[]{:S(2)}, u32[]{:S(2)}) collective-permute-start(bf16[768,768]{1,0:T(8,128)(2,1)} %bitcast.184), channel_id=1, source_target_pairs={{0,16},{16,0},{1,17},{17,1},{2,18},{18,2},{3,19},{19,3},{4,20},{20... | collective-permute-start | bytes 3538952 | tf_op jit(solution)/shard_map/ppermute | solution.py:1572
  45.6 6.3 %collective-permute-start.12 = (bf16[256,192]{1,0:T(8,128)(2,1)S(1)}, bf16[256,192]{1,0:T(8,128)(2,1)S(1)}, u32[]{:S(2)}, u32[]{:S(2)}) collective-permute-start(bf16[256,192]{1,0:T(8,128)(2,1)S(1)} %get-tuple-element.237), channel_id=1, source_target_pairs={{0,4},{4,0},{8,12},{12,8},{1,5},{5,1},{9,13},{13,9},{2,6},{6,2},{1... | collective-permute-start | bytes 294920 | tf_op jit(solution)/shard_map/ppermute | solution.py:1576
  47.6 6.5 %collective-permute-start.13 = (bf16[256,192]{1,0:T(8,128)(2,1)S(1)}, bf16[256,192]{1,0:T(8,128)(2,1)S(1)}, u32[]{:S(2)}, u32[]{:S(2)}) collective-permute-start(bf16[256,192]{1,0:T(8,128)(2,1)S(1)} %get-tuple-element.238), channel_id=1, source_target_pairs={{0,20},{4,16},{8,28},{12,24},{16,4},{20,0},{24,12},{28,8},{1,21},{... | collective-permute-start | bytes 294920 | tf_op jit(solution)/shard_map/ppermute | solution.py:1580
  64.7 11.5 %collective-permute-start.18 = (bf16[256,4608]{1,0:T(8,128)(2,1)}, bf16[256,4608]{1,0:T(8,128)(2,1)}, u32[]{:S(2)}, u32[]{:S(2)}) collective-permute-start(bf16[256,4608]{1,0:T(8,128)(2,1)} %get-tuple-element.244.f0), channel_id=1, source_target_pairs={{0,16},{16,0},{1,17},{17,1},{2,18},{18,2},{3,19},{19,3},{4,20},{20... | collective-permute-start | bytes 7077896 | tf_op jit(solution)/shard_map/ppermute | solution.py:1572
  65.0 11.2 %collective-permute-start.15 = (bf16[256,768]{1,0:T(8,128)(2,1)S(1)}, bf16[256,768]{1,0:T(8,128)(2,1)S(1)}, u32[]{:S(2)}, u32[]{:S(2)}) collective-permute-start(bf16[256,768]{1,0:T(8,128)(2,1)S(1)} %get-tuple-element.243.refs_1_), channel_id=1, source_target_pairs={{0,4},{4,0},{8,12},{12,8},{1,5},{5,1},{9,13},{13,9},{2,6},{6,2},{1... | collective-permute-start | bytes 1179656 | tf_op jit(solution)/shard_map/ppermute | solution.py:1576
  67.0 5.1 %collective-permute-start.16 = (bf16[38,768]{1,0:T(8,128)(2,1)S(1)}, bf16[38,768]{1,0:T(8,128)(2,1)S(1)}, u32[]{:S(2)}, u32[]{:S(2)}) collective-permute-start(bf16[38,768]{1,0:T(8,128)(2,1)S(1)} %bitcast.176), channel_id=1, source_target_pairs={{0,8},{4,12},{8,0},{12,4},{1,9},{5,13},{9,1},{13,5},{2,10},{6,14},... | collective-permute-start | bytes 175112 | tf_op jit(solution)/shard_map/ppermute | solution.py:1576
  69.1 9.4 %collective-permute-start.14 = (bf16[256,768]{1,0:T(8,128)(2,1)S(1)}, bf16[256,768]{1,0:T(8,128)(2,1)S(1)}, u32[]{:S(2)}, u32[]{:S(2)}) collective-permute-start(bf16[256,768]{1,0:T(8,128)(2,1)S(1)} %get-tuple-element.243.refs_1_), channel_id=1, source_target_pairs={{0,16},{16,0},{1,17},{17,1},{2,18},{18,2},{3,19},{19,3},{4,20},{20... | collective-permute-start | bytes 1179656 | tf_op jit(solution)/shard_map/ppermute | solution.py:1572
  76.3 22.6 %collective-permute-start.23 = (bf16[256,768]{1,0:T(8,128)(2,1)S(1)}, bf16[256,768]{1,0:T(8,128)(2,1)S(1)}, u32[]{:S(2)}, u32[]{:S(2)}) collective-permute-start(bf16[256,768]{1,0:T(8,128)(2,1)S(1)} %get-tuple-element.243.refs_1_), channel_id=1, source_target_pairs={{0,0},{4,4},{24,8},{28,12},{1,1},{5,5},{25,9},{29,13},{2,2},{6,6},... | collective-permute-start | bytes 1179656 | tf_op jit(solution)/shard_map/ppermute | solution.py:1599
  77.0 21.9 %collective-permute-start.24 = (bf16[256,768]{1,0:T(8,128)(2,1)S(1)}, bf16[256,768]{1,0:T(8,128)(2,1)S(1)}, u32[]{:S(2)}, u32[]{:S(2)}) collective-permute-start(bf16[256,768]{1,0:T(8,128)(2,1)S(1)} %get-tuple-element.243.refs_1_), channel_id=1, source_target_pairs={{16,8},{20,12},{8,0},{12,4},{17,9},{21,13},{9,1},{13,5},{18,10},{2... | collective-permute-start | bytes 1179656 | tf_op jit(solution)/shard_map/ppermute | solution.py:1599
  94.1 4.8 %collective-permute-start.20 = (bf16[256,192]{1,0:T(8,128)(2,1)S(1)}, bf16[256,192]{1,0:T(8,128)(2,1)S(1)}, u32[]{:S(2)}, u32[]{:S(2)}) collective-permute-start(bf16[256,192]{1,0:T(8,128)(2,1)S(1)} %get-tuple-element.247), channel_id=1, source_target_pairs={{0,16},{16,0},{1,17},{17,1},{2,18},{18,2},{3,19},{19,3},{4,20},{20... | collective-permute-start | bytes 294920 | tf_op jit(solution)/shard_map/ppermute | solution.py:1572
  97.0 6.3 %collective-permute-start.21 = (bf16[256,192]{1,0:T(8,128)(2,1)S(1)}, bf16[256,192]{1,0:T(8,128)(2,1)S(1)}, u32[]{:S(2)}, u32[]{:S(2)}) collective-permute-start(bf16[256,192]{1,0:T(8,128)(2,1)S(1)} %get-tuple-element.248), channel_id=1, source_target_pairs={{0,4},{4,0},{8,12},{12,8},{1,5},{5,1},{9,13},{13,9},{2,6},{6,2},{1... | collective-permute-start | bytes 294920 | tf_op jit(solution)/shard_map/ppermute | solution.py:1576
  98.5 5.8 %collective-permute-start.22 = (bf16[256,192]{1,0:T(8,128)(2,1)S(1)}, bf16[256,192]{1,0:T(8,128)(2,1)S(1)}, u32[]{:S(2)}, u32[]{:S(2)}) collective-permute-start(bf16[256,192]{1,0:T(8,128)(2,1)S(1)} %get-tuple-element.249), channel_id=1, source_target_pairs={{0,20},{4,16},{8,28},{12,24},{16,4},{20,0},{24,12},{28,8},{1,21},{... | collective-permute-start | bytes 294920 | tf_op jit(solution)/shard_map/ppermute | solution.py:1580
  132.3 6.9 %collective-permute-start.28 = (bf16[256,4608]{1,0:T(8,128)(2,1)}, bf16[256,4608]{1,0:T(8,128)(2,1)S(1)}, u32[]{:S(2)}, u32[]{:S(2)}) collective-permute-start(bf16[256,4608]{1,0:T(8,128)(2,1)} %get-tuple-element.263.f0), channel_id=1, source_target_pairs={{0,16},{16,0},{1,17},{17,1},{2,18},{18,2},{3,19},{19,3},{4,20},{20... | collective-permute-start | bytes 7077896 | tf_op jit(solution)/shard_map/ppermute | solution.py:1572
  132.9 6.2 %collective-permute-start.29 = (bf16[256,2304]{1,0:T(8,128)(2,1)}, bf16[256,2304]{1,0:T(8,128)(2,1)S(1)}, u32[]{:S(2)}, u32[]{:S(2)}) collective-permute-start(bf16[256,2304]{1,0:T(8,128)(2,1)} %get-tuple-element.265), channel_id=1, source_target_pairs={{0,16},{16,0},{1,17},{17,1},{2,18},{18,2},{3,19},{19,3},{4,20},{20... | collective-permute-start | bytes 3538952 | tf_op jit(solution)/shard_map/ppermute | solution.py:1572
  133.0 16.7 %collective-permute-start.25 = (bf16[256,192]{1,0:T(8,128)(2,1)S(1)}, bf16[256,192]{1,0:T(8,128)(2,1)S(1)}, u32[]{:S(2)}, u32[]{:S(2)}) collective-permute-start(bf16[256,192]{1,0:T(8,128)(2,1)S(1)} %get-tuple-element.260), channel_id=1, source_target_pairs={{0,16},{16,0},{1,17},{17,1},{2,18},{18,2},{3,19},{19,3},{4,20},{20... | collective-permute-start | bytes 294920 | tf_op jit(solution)/shard_map/ppermute | solution.py:1572
  133.5 16.2 %collective-permute-start.26 = (bf16[256,192]{1,0:T(8,128)(2,1)S(1)}, bf16[256,192]{1,0:T(8,128)(2,1)S(1)}, u32[]{:S(2)}, u32[]{:S(2)}) collective-permute-start(bf16[256,192]{1,0:T(8,128)(2,1)S(1)} %get-tuple-element.261), channel_id=1, source_target_pairs={{0,4},{4,0},{8,12},{12,8},{1,5},{5,1},{9,13},{13,9},{2,6},{6,2},{1... | collective-permute-start | bytes 294920 | tf_op jit(solution)/shard_map/ppermute | solution.py:1576
  135.0 14.7 %collective-permute-start.27 = (bf16[256,192]{1,0:T(8,128)(2,1)S(1)}, bf16[256,192]{1,0:T(8,128)(2,1)S(1)}, u32[]{:S(2)}, u32[]{:S(2)}) collective-permute-start(bf16[256,192]{1,0:T(8,128)(2,1)S(1)} %get-tuple-element.262), channel_id=1, source_target_pairs={{0,20},{4,16},{8,28},{12,24},{16,4},{20,0},{24,12},{28,8},{1,21},{... | collective-permute-start | bytes 294920 | tf_op jit(solution)/shard_map/ppermute | solution.py:1580
  149.7 182.5 %reduce-scatter.5.cloned.1.call-start = ((), (), s32[]{:S(2)}) async-start(), calls=%async_computation.3 | async-start | bytes 1658880 | tf_op jit(solution)/shard_map/reduce_scatter | solution.py:1757
  170.7 20.2 %collective-permute-start.32 = (bf16[256,768]{1,0:T(8,128)(2,1)S(1)}, bf16[256,768]{1,0:T(8,128)(2,1)S(1)}, u32[]{:S(2)}, u32[]{:S(2)}) collective-permute-start(bf16[256,768]{1,0:T(8,128)(2,1)S(1)} %add_convert_fusion.7), channel_id=1, source_target_pairs={{0,4},{4,0},{8,12},{12,8},{1,5},{5,1},{9,13},{13,9},{2,6},{6,2},{1... | collective-permute-start | bytes 1179656 | tf_op jit(solution)/shard_map/ppermute | solution.py:1576
  172.3 19.3 %collective-permute-start.30 = (bf16[256,768]{1,0:T(8,128)(2,1)S(1)}, bf16[256,768]{1,0:T(8,128)(2,1)S(1)}, u32[]{:S(2)}, u32[]{:S(2)}) collective-permute-start(bf16[256,768]{1,0:T(8,128)(2,1)S(1)} %get-tuple-element.280), channel_id=1, source_target_pairs={{0,16},{16,0},{1,17},{17,1},{2,18},{18,2},{3,19},{19,3},{4,20},{20... | collective-permute-start | bytes 1179656 | tf_op jit(solution)/shard_map/ppermute | solution.py:1572
  190.9 12.8 %collective-permute-start.33 = (bf16[384,640]{1,0:T(8,128)(2,1)S(1)}, bf16[384,640]{1,0:T(8,128)(2,1)S(1)}, u32[]{:S(2)}, u32[]{:S(2)}) collective-permute-start(bf16[384,640]{1,0:T(8,128)(2,1)S(1)} %get-tuple-element.303), channel_id=1, source_target_pairs={{0,8},{4,12},{8,0},{12,4},{1,9},{5,13},{9,1},{13,5},{2,10},{6,14},... | collective-permute-start | bytes 1474568 | tf_op jit(solution)/shard_map/ppermute | solution.py:1576
  204.6 40.0 %collective-permute-start.40 = (bf16[384,512]{1,0:T(8,128)(2,1)}, bf16[384,512]{1,0:T(8,128)(2,1)S(1)}, u32[]{:S(2)}, u32[]{:S(2)}) collective-permute-start(bf16[384,512]{1,0:T(8,128)(2,1)} %get-tuple-element.339), channel_id=1, source_target_pairs={{0,8},{4,12},{8,0},{12,4},{1,9},{5,13},{9,1},{13,5},{2,10},{6,14},... | collective-permute-start | bytes 1179656 | tf_op jit(solution)/shard_map/ppermute | solution.py:1576
  206.1 11.4 %collective-permute-start.34 = (bf16[256,192]{1,0:T(8,128)(2,1)S(1)}, bf16[256,192]{1,0:T(8,128)(2,1)S(1)}, u32[]{:S(2)}, u32[]{:S(2)}) collective-permute-start(bf16[256,192]{1,0:T(8,128)(2,1)S(1)} %get-tuple-element.305), channel_id=1, source_target_pairs={{0,16},{16,0},{1,17},{17,1},{2,18},{18,2},{3,19},{19,3},{4,20},{20... | collective-permute-start | bytes 294920 | tf_op jit(solution)/shard_map/ppermute | solution.py:1572
  206.3 11.2 %collective-permute-start.35 = (bf16[256,192]{1,0:T(8,128)(2,1)S(1)}, bf16[256,192]{1,0:T(8,128)(2,1)S(1)}, u32[]{:S(2)}, u32[]{:S(2)}) collective-permute-start(bf16[256,192]{1,0:T(8,128)(2,1)S(1)} %get-tuple-element.306), channel_id=1, source_target_pairs={{0,4},{4,0},{8,12},{12,8},{1,5},{5,1},{9,13},{13,9},{2,6},{6,2},{1... | collective-permute-start | bytes 294920 | tf_op jit(solution)/shard_map/ppermute | solution.py:1576
  207.8 12.4 %collective-permute-start.36 = (bf16[256,192]{1,0:T(8,128)(2,1)S(1)}, bf16[256,192]{1,0:T(8,128)(2,1)S(1)}, u32[]{:S(2)}, u32[]{:S(2)}) collective-permute-start(bf16[256,192]{1,0:T(8,128)(2,1)S(1)} %get-tuple-element.307), channel_id=1, source_target_pairs={{0,20},{4,16},{8,28},{12,24},{16,4},{20,0},{24,12},{28,8},{1,21},{... | collective-permute-start | bytes 294920 | tf_op jit(solution)/shard_map/ppermute | solution.py:1580
  220.2 26.0 %collective-permute-start.38 = (bf16[384,1024]{1,0:T(8,128)(2,1)S(1)}, bf16[384,1024]{1,0:T(8,128)(2,1)}, u32[]{:S(2)}, u32[]{:S(2)}) collective-permute-start(bf16[384,1024]{1,0:T(8,128)(2,1)S(1)} %get-tuple-element.337), channel_id=1, source_target_pairs={{0,8},{4,12},{8,0},{12,4},{1,9},{5,13},{9,1},{13,5},{2,10},{6,14},... | collective-permute-start | bytes 2359304 | tf_op jit(solution)/shard_map/ppermute | solution.py:1576
  220.8 23.8 %collective-permute-start.39 = (bf16[8,96,384]{2,1,0:T(8,128)(2,1)S(1)}, bf16[8,96,384]{2,1,0:T(8,128)(2,1)S(1)}, u32[]{:S(2)}, u32[]{:S(2)}) collective-permute-start(bf16[8,96,384]{2,1,0:T(8,128)(2,1)S(1)} %get-tuple-element.338), channel_id=1, source_target_pairs={{0,4},{4,0},{8,12},{12,8},{1,5},{5,1},{9,13},{13,9},{2,6},{6,2},{1... | collective-permute-start | bytes 1769480 | tf_op jit(solution)/shard_map/ppermute | solution.py:1576
  222.3 38.9 %collective-permute-start.46 = (bf16[384,896]{1,0:T(8,128)(2,1)}, bf16[384,896]{1,0:T(8,128)(2,1)}, u32[]{:S(2)}, u32[]{:S(2)}) collective-permute-start(bf16[384,896]{1,0:T(8,128)(2,1)} %get-tuple-element.353), channel_id=1, source_target_pairs={{0,8},{4,12},{8,0},{12,4},{1,9},{5,13},{9,1},{13,5},{2,10},{6,14},... | collective-permute-start | bytes 2064392 | tf_op jit(solution)/shard_map/ppermute | solution.py:1576
  223.7 37.4 %collective-permute-start.47 = (bf16[8,96,384]{2,1,0:T(8,128)(2,1)}, bf16[8,96,384]{2,1,0:T(8,128)(2,1)}, u32[]{:S(2)}, u32[]{:S(2)}) collective-permute-start(bf16[8,96,384]{2,1,0:T(8,128)(2,1)} %get-tuple-element.354), channel_id=1, source_target_pairs={{0,4},{4,0},{8,12},{12,8},{1,5},{5,1},{9,13},{13,9},{2,6},{6,2},{1... | collective-permute-start | bytes 1769480 | tf_op jit(solution)/shard_map/ppermute | solution.py:1576
  250.1 17.6 %collective-permute-start.44 = (bf16[2,2,48,1152]{3,2,0,1:T(8,128)(2,1)}, bf16[2,2,48,1152]{3,2,0,1:T(8,128)(2,1)S(1)}, u32[]{:S(2)}, u32[]{:S(2)}) collective-permute-start(bf16[2,2,48,1152]{3,2,0,1:T(8,128)(2,1)} %bitcast.151), channel_id=1, source_target_pairs={{0,1},{1,0},{2,3},{3,2},{4,5},{5,4},{6,7},{7,6},{8,9},{9,8},{10,11... | collective-permute-start | bytes 1327112 | tf_op jit(solution)/shard_map/ppermute | solution.py:1584
  251.7 12.1 %collective-permute-start.43 = (bf16[256,768]{1,0:T(8,128)(2,1)}, bf16[256,768]{1,0:T(8,128)(2,1)S(1)}, u32[]{:S(2)}, u32[]{:S(2)}) collective-permute-start(bf16[256,768]{1,0:T(8,128)(2,1)} %add_convert_fusion.5), channel_id=1, source_target_pairs={{0,4},{4,0},{8,12},{12,8},{1,5},{5,1},{9,13},{13,9},{2,6},{6,2},{1... | collective-permute-start | bytes 1179656 | tf_op jit(solution)/shard_map/ppermute | solution.py:1576
  253.1 10.6 %collective-permute-start.45 = (f32[14,768]{1,0:T(8,128)S(1)}, f32[14,768]{1,0:T(8,128)S(1)}, u32[]{:S(2)}, u32[]{:S(2)}) collective-permute-start(f32[14,768]{1,0:T(8,128)S(1)} %select_add_fusion), channel_id=1, source_target_pairs={{0,4},{4,0},{8,12},{12,8},{1,5},{5,1},{9,13},{13,9},{2,6},{6,2},{1... | collective-permute-start | bytes 129032 | tf_op jit(solution)/shard_map/ppermute | solution.py:1576
  261.1 20.4 %collective-permute-start.56 = (bf16[256,768]{1,0:T(8,128)(2,1)S(1)}, bf16[256,768]{1,0:T(8,128)(2,1)S(1)}, u32[]{:S(2)}, u32[]{:S(2)}) collective-permute-start(bf16[256,768]{1,0:T(8,128)(2,1)S(1)} %copy-done.7), channel_id=1, source_target_pairs={{0,16},{16,0},{1,17},{17,1},{2,18},{18,2},{3,19},{19,3},{4,20},{20... | collective-permute-start | bytes 1179656 | tf_op jit(solution)/shard_map/ppermute | solution.py:1572
  269.8 35.3 %collective-permute-start.49 = (bf16[2,2,48,1920]{3,2,0,1:T(8,128)(2,1)S(1)}, bf16[2,2,48,1920]{3,2,0,1:T(8,128)(2,1)S(1)}, u32[]{:S(2)}, u32[]{:S(2)}) collective-permute-start(bf16[2,2,48,1920]{3,2,0,1:T(8,128)(2,1)S(1)} %bitcast.169), channel_id=1, source_target_pairs={{0,1},{1,0},{2,3},{3,2},{4,5},{5,4},{6,7},{7,6},{8,9},{9,8},{10,11... | collective-permute-start | bytes 2211848 | tf_op jit(solution)/shard_map/ppermute | solution.py:1584
  271.8 33.3 %collective-permute-start.48 = (bf16[384,640]{1,0:T(8,128)(2,1)S(1)}, bf16[384,640]{1,0:T(8,128)(2,1)S(1)}, u32[]{:S(2)}, u32[]{:S(2)}) collective-permute-start(bf16[384,640]{1,0:T(8,128)(2,1)S(1)} %get-tuple-element.367), channel_id=1, source_target_pairs={{0,8},{4,12},{8,0},{12,4},{1,9},{5,13},{9,1},{13,5},{2,10},{6,14},... | collective-permute-start | bytes 1474568 | tf_op jit(solution)/shard_map/ppermute | solution.py:1576
  271.8 33.3 %collective-permute-start.50 = (bf16[384,512]{1,0:T(8,128)(2,1)S(1)}, bf16[384,512]{1,0:T(8,128)(2,1)S(1)}, u32[]{:S(2)}, u32[]{:S(2)}) collective-permute-start(bf16[384,512]{1,0:T(8,128)(2,1)S(1)} %get-tuple-element.369), channel_id=1, source_target_pairs={{0,8},{4,12},{8,0},{12,4},{1,9},{5,13},{9,1},{13,5},{2,10},{6,14},... | collective-permute-start | bytes 1179656 | tf_op jit(solution)/shard_map/ppermute | solution.py:1576
  275.5 28.1 %collective-permute-start.51 = (bf16[2,48,1152]{2,1,0:T(8,128)(2,1)S(1)}, bf16[2,48,1152]{2,1,0:T(8,128)(2,1)S(1)}, u32[]{:S(2)}, u32[]{:S(2)}) collective-permute-start(bf16[2,48,1152]{2,1,0:T(8,128)(2,1)S(1)} %dynamic-slice_bitcast_fusion.3), channel_id=1, source_target_pairs={{0,2},{1,3},{2,0},{3,1},{4,6},{5,7},{6,4},{7,5},{8,10},{9,11},{10,... | collective-permute-start | bytes 663560 | tf_op jit(solution)/shard_map/ppermute | solution.py:1584
  281.7 30.2 %collective-permute-start.57 = (bf16[256,768]{1,0:T(8,128)(2,1)S(1)}, bf16[256,768]{1,0:T(8,128)(2,1)S(1)}, u32[]{:S(2)}, u32[]{:S(2)}) collective-permute-start(bf16[256,768]{1,0:T(8,128)(2,1)S(1)} %add_convert_fusion.4), channel_id=1, source_target_pairs={{0,0},{4,4},{24,8},{28,12},{1,1},{5,5},{25,9},{29,13},{2,2},{6,6},... | collective-permute-start | bytes 1179656 | tf_op jit(solution)/shard_map/ppermute | solution.py:1599
  303.6 13.3 %collective-permute-start.58 = (bf16[256,768]{1,0:T(8,128)(2,1)S(1)}, bf16[256,768]{1,0:T(8,128)(2,1)S(1)}, u32[]{:S(2)}, u32[]{:S(2)}) collective-permute-start(bf16[256,768]{1,0:T(8,128)(2,1)S(1)} %add_convert_fusion.4), channel_id=1, source_target_pairs={{16,8},{20,12},{8,0},{12,4},{17,9},{21,13},{9,1},{13,5},{18,10},{2... | collective-permute-start | bytes 1179656 | tf_op jit(solution)/shard_map/ppermute | solution.py:1599
  305.7 26.6 %collective-permute-start.53 = (bf16[2,2,192,384]{3,2,0,1:T(8,128)(2,1)S(1)}, bf16[2,2,192,384]{3,2,0,1:T(8,128)(2,1)S(1)}, u32[]{:S(2)}, u32[]{:S(2)}) collective-permute-start(bf16[2,2,192,384]{3,2,0,1:T(8,128)(2,1)S(1)} %bitcast.170), channel_id=1, source_target_pairs={{0,8},{4,12},{8,0},{12,4},{1,9},{5,13},{9,1},{13,5},{2,10},{6,14},... | collective-permute-start | bytes 1769480 | tf_op jit(solution)/shard_map/ppermute | solution.py:1576
  308.4 23.1 %collective-permute-start.54 = (bf16[2,2,48,1152]{3,2,0,1:T(8,128)(2,1)S(1)}, bf16[2,2,48,1152]{3,2,0,1:T(8,128)(2,1)S(1)}, u32[]{:S(2)}, u32[]{:S(2)}) collective-permute-start(bf16[2,2,48,1152]{3,2,0,1:T(8,128)(2,1)S(1)} %bitcast.171), channel_id=1, source_target_pairs={{0,1},{1,0},{2,3},{3,2},{4,5},{5,4},{6,7},{7,6},{8,9},{9,8},{10,11... | collective-permute-start | bytes 1327112 | tf_op jit(solution)/shard_map/ppermute | solution.py:1584
  311.9 19.6 %collective-permute-start.52 = (bf16[2,48,1920]{2,1,0:T(8,128)(2,1)S(1)}, bf16[2,48,1920]{2,1,0:T(8,128)(2,1)S(1)}, u32[]{:S(2)}, u32[]{:S(2)}) collective-permute-start(bf16[2,48,1920]{2,1,0:T(8,128)(2,1)S(1)} %dynamic-slice_bitcast_fusion), channel_id=1, source_target_pairs={{0,2},{1,3},{2,0},{3,1},{4,6},{5,7},{6,4},{7,5},{8,10},{9,11},{10,... | collective-permute-start | bytes 1105928 | tf_op jit(solution)/shard_map/ppermute | solution.py:1584
  311.9 18.0 %collective-permute-start.55 = (f32[14,768]{1,0:T(8,128)S(1)}, f32[14,768]{1,0:T(8,128)S(1)}, u32[]{:S(2)}, u32[]{:S(2)}) collective-permute-start(f32[14,768]{1,0:T(8,128)S(1)} %add.219), channel_id=1, source_target_pairs={{0,1},{1,0},{2,3},{3,2},{4,5},{5,4},{6,7},{7,6},{8,9},{9,8},{10,11... | collective-permute-start | bytes 129032 | tf_op jit(solution)/shard_map/ppermute | solution.py:1584
  316.8 20.5 %collective-permute-start.64 = (bf16[2,256,768]{2,1,0:T(8,128)(2,1)}, bf16[2,256,768]{2,1,0:T(8,128)(2,1)}, u32[]{:S(2)}, u32[]{:S(2)}) collective-permute-start(bf16[2,256,768]{2,1,0:T(8,128)(2,1)} %pad_maximum_fusion), channel_id=1, source_target_pairs={{0,16},{4,20},{24,24},{28,28},{1,17},{5,21},{25,25},{29,29},{2,18}... | collective-permute-start | bytes 2359304 | tf_op jit(solution)/shard_map/ppermute | solution.py:1599
  329.9 7.9 %collective-permute-start.65 = (bf16[2,256,768]{2,1,0:T(8,128)(2,1)}, bf16[2,256,768]{2,1,0:T(8,128)(2,1)}, u32[]{:S(2)}, u32[]{:S(2)}) collective-permute-start(bf16[2,256,768]{2,1,0:T(8,128)(2,1)} %pad_maximum_fusion), channel_id=1, source_target_pairs={{16,24},{20,28},{8,16},{12,20},{17,25},{21,29},{9,17},{13,21},{18,... | collective-permute-start | bytes 2359304 | tf_op jit(solution)/shard_map/ppermute | solution.py:1599
  333.9 14.2 %collective-permute-start.60 = (bf16[2,192,384]{2,1,0:T(8,128)(2,1)S(1)}, bf16[2,192,384]{2,1,0:T(8,128)(2,1)S(1)}, u32[]{:S(2)}, u32[]{:S(2)}) collective-permute-start(bf16[2,192,384]{2,1,0:T(8,128)(2,1)S(1)} %dynamic-slice_bitcast_fusion.1), channel_id=1, source_target_pairs={{0,1},{1,0},{2,3},{3,2},{4,5},{5,4},{6,7},{7,6},{8,9},{9,8},{10,11... | collective-permute-start | bytes 884744 | tf_op jit(solution)/shard_map/ppermute | solution.py:1584
  335.7 11.9 %collective-permute-start.59 = (bf16[2,48,1152]{2,1,0:T(8,128)(2,1)S(1)}, bf16[2,48,1152]{2,1,0:T(8,128)(2,1)S(1)}, u32[]{:S(2)}, u32[]{:S(2)}) collective-permute-start(bf16[2,48,1152]{2,1,0:T(8,128)(2,1)S(1)} %dynamic-slice_bitcast_fusion.2), channel_id=1, source_target_pairs={{0,2},{1,3},{2,0},{3,1},{4,6},{5,7},{6,4},{7,5},{8,10},{9,11},{10,... | collective-permute-start | bytes 663560 | tf_op jit(solution)/shard_map/ppermute | solution.py:1584
  335.8 9.9 %collective-permute-start.61 = (bf16[48,1920]{1,0:T(8,128)(2,1)S(1)}, bf16[48,1920]{1,0:T(8,128)(2,1)S(1)}, u32[]{:S(2)}, u32[]{:S(2)}) collective-permute-start(bf16[48,1920]{1,0:T(8,128)(2,1)S(1)} %dynamic-slice_bitcast_fusion.6), channel_id=1, source_target_pairs={{0,4},{4,0},{8,12},{12,8},{1,5},{5,1},{9,13},{13,9},{2,6},{6,2},{1... | collective-permute-start | bytes 552968 | tf_op jit(solution)/shard_map/ppermute | solution.py:1576
  337.3 8.4 %collective-permute-start.63 = (bf16[48,1152]{1,0:T(8,128)(2,1)S(1)}, bf16[48,1152]{1,0:T(8,128)(2,1)S(1)}, u32[]{:S(2)}, u32[]{:S(2)}) collective-permute-start(bf16[48,1152]{1,0:T(8,128)(2,1)S(1)} %copy-done.51), channel_id=1, source_target_pairs={{0,4},{4,0},{8,12},{12,8},{1,5},{5,1},{9,13},{13,9},{2,6},{6,2},{1... | collective-permute-start | bytes 331784 | tf_op jit(solution)/shard_map/ppermute | solution.py:1576
  337.9 6.9 %collective-permute-start.62 = (f32[14,768]{1,0:T(8,128)S(1)}, f32[14,768]{1,0:T(8,128)S(1)}, u32[]{:S(2)}, u32[]{:S(2)}) collective-permute-start(f32[14,768]{1,0:T(8,128)S(1)} %add.228), channel_id=1, source_target_pairs={{0,8},{4,12},{8,0},{12,4},{1,9},{5,13},{9,1},{13,5},{2,10},{6,14},... | collective-permute-start | bytes 129032 | tf_op jit(solution)/shard_map/ppermute | solution.py:1576
  348.3 12.3 %collective-permute-start.66 = (bf16[192,384]{1,0:T(8,128)(2,1)S(1)}, bf16[192,384]{1,0:T(8,128)(2,1)S(1)}, u32[]{:S(2)}, u32[]{:S(2)}) collective-permute-start(bf16[192,384]{1,0:T(8,128)(2,1)S(1)} %dynamic-slice_bitcast_fusion.7), channel_id=1, source_target_pairs={{0,2},{1,3},{2,0},{3,1},{4,6},{5,7},{6,4},{7,5},{8,10},{9,11},{10,... | collective-permute-start | bytes 442376 | tf_op jit(solution)/shard_map/ppermute | solution.py:1584
  351.2 9.4 %collective-permute-start.67 = (bf16[48,1152]{1,0:T(8,128)(2,1)S(1)}, bf16[48,1152]{1,0:T(8,128)(2,1)S(1)}, u32[]{:S(2)}, u32[]{:S(2)}) collective-permute-start(bf16[48,1152]{1,0:T(8,128)(2,1)S(1)} %get-tuple-element.410), channel_id=1, source_target_pairs={{0,4},{4,0},{8,12},{12,8},{1,5},{5,1},{9,13},{13,9},{2,6},{6,2},{1... | collective-permute-start | bytes 331784 | tf_op jit(solution)/shard_map/ppermute | solution.py:1576
  352.8 7.9 %collective-permute-start.68 = (f32[14,768]{1,0:T(8,128)S(1)}, f32[14,768]{1,0:T(8,128)S(1)}, u32[]{:S(2)}, u32[]{:S(2)}) collective-permute-start(f32[14,768]{1,0:T(8,128)S(1)} %add.234), channel_id=1, source_target_pairs={{0,2},{1,3},{2,0},{3,1},{4,6},{5,7},{6,4},{7,5},{8,10},{9,11},{10,... | collective-permute-start | bytes 129032 | tf_op jit(solution)/shard_map/ppermute | solution.py:1584
  (68 other events, 415.7 us)
Sparse Core Ops, SparseCore 0:
  149.9 81.7 reduce-scatter.2
  253.2 44.1 reduce-scatter.4
where the time goes:
time: 378 us; the launch traced here: 373 us
  Pallas kernels  147 us (39%)
  waiting for transfers between devices  93.9 us (25%)
  starting transfers between devices  73.7 us (19%)
  local copies, waits for them, and re-layouts  29.2 us (8%)
  between operations  15.4 us (4%)
  other arithmetic  13.4 us (4%)
    ppermute x10, waiting for transfers between devices, dp_flip(): return lax.ppermute(v, DP, [(i, i ^ by) for i in range(lax.axis_size(DP))])  42.4 us
    ppermute x26, starting transfers between devices, seq_flip(): return lax.ppermute(v, SEQ, [(i, i ^ by) for i in range(4)])  37.3 us
    pallas_call x2, Pallas kernels, attend_back(): pl.pallas_call(partial(attend_back_kernel, layer), out_shape=[jax.ShapeDt...  36 us
    ppermute x26, waiting for transfers between devices, seq_flip(): return lax.ppermute(v, SEQ, [(i, i ^ by) for i in range(4)])  34.4 us
    pallas_call x2, Pallas kernels, attend(): pl.pallas_call(partial(attend_kernel, layer), out_shape=outs, in_specs=[p...  29.7 us
    pallas_call x1, Pallas kernels, rows_both(): pl.pallas_call(rows_both_kernel, out_shape=[sds((rows, width), bf16), sds...  27.3 us
    unnamed x124, local copies, waits for them, and re-layouts  23.6 us
    ppermute x10, starting transfers between devices, dp_flip(): return lax.ppermute(v, DP, [(i, i ^ by) for i in range(lax.axis_size(DP))])  19.1 us
  transfers between devices with their start and end apart: 73, of which 21 were waited for; matrix products, arithmetic and copies ran while one was open for 5% of the time, Pallas kernels for 29%

commit v1 on v0

--- a/solution.py
+++ b/solution.py
@@ -664,13 +664,13 @@
                 )
             )
             copies[-1].start()
-    pack_o[...] = jnp.zeros(pack_o.shape, bf16)
+    pack_o[...] = jnp.zeros(pack_o.shape, f32)
     at = 0
     for ref in (lb, gb, ob, ng, ns, db):
-        pack_o[at : at + ref.shape[0], :] = ref[...]
+        pack_o[at : at + ref.shape[0], :] = ref[...].astype(f32)
         at += ref.shape[0]
     for i in range(ub.shape[1] // width):
-        pack_o[at + i : at + i + 1, :] = ub[:, i * width : (i + 1) * width]
+        pack_o[at + i : at + i + 1, :] = ub[:, i * width : (i + 1) * width].astype(f32)
     for t, target in enumerate((send_o, own_o)):
         for i in range(6):
             copies[6 * t + i].wait()
@@ -689,7 +689,7 @@
     chosen = jax.ShapeDtypeStruct((width, 6 * width // 4), bf16)
     return pl.pallas_call(
         prepare_kernel,
-        out_shape=[chosen, chosen, jax.ShapeDtypeStruct((16, width), bf16)],
+        out_shape=[chosen, chosen, jax.ShapeDtypeStruct((16, width), f32)],
         in_specs=[pl.BlockSpec(memory_space=pltpu.SMEM), hbm, hbm] + [vm] * 7,
         out_specs=[vm] * 3,
         scratch_shapes=[
@@ -735,7 +735,7 @@
         for r in range(count):
             u_o[pl.ds(pl.multiple_of(ids[r] * rows, rows), rows), :] = parts[r][...]
     own_o[...] = u_o[pl.ds(pl.multiple_of(group * rows, rows), rows), :]
-    pack = jnp.where(core == layer, pack_a[...].astype(f32), pack_b[...].astype(f32))[:4]
+    pack = jnp.where(core == layer, pack_a[...], pack_b[...])[:4]
     hb = pack[:, :hw]
     for i in range(1, 4):
         hb = jnp.where(group == i, pack[:, i * hw : (i + 1) * hw], hb)
@@ -1051,7 +1051,7 @@
     steps, cols = wu_s.shape[0], wu_s.shape[2]
     pairs = weight_pairs(steps, cols, wo_s, wu_s, wd_s)
     wait = fetch((wo_a, wu_a, wd_a), (wo_b, wu_b, wd_b), ids[4] != layer, pairs, sems)
-    pack = jnp.where(ids[4] == layer, pack_a[...].astype(f32), pack_b[...].astype(f32))
+    pack = jnp.where(ids[4] == layer, pack_a[...], pack_b[...])
     hw = c0.shape[1]
     width = 4 * hw
     pieces = [c[...] for c in (c0, c1, c2, c3)]
@@ -1134,7 +1134,7 @@
     steps, cols = wu_s.shape[0], wu_s.shape[2]
     pairs = weight_pairs(steps, cols, wo_s, wu_s, wd_s)
     wait = fetch((wo_a, wu_a, wd_a), (wo_b, wu_b, wd_b), ids[4] != layer, pairs, sems)
-    pack = jnp.where(ids[4] == layer, pack_a[...].astype(f32), pack_b[...].astype(f32))
+    pack = jnp.where(ids[4] == layer, pack_a[...], pack_b[...])
     side = ids[4]
     half = first_o.shape[1] // 2
     ffh = keep_o.shape[1] - 2 * half
@@ -1325,7 +1325,7 @@
 
 
 def own_pack(layer, ids, pack_a, pack_b):
-    return jnp.where(ids[4] == layer, pack_a[...].astype(f32), pack_b[...].astype(f32))
+    return jnp.where(ids[4] == layer, pack_a[...], pack_b[...])
 
 
 def rows_both_kernel(
@@ -1469,7 +1469,7 @@
     part = width // 2
     ua = 1024
     small = ff // 16
-    hbm = pl.BlockSpec(memory_space=pltpu.HBM)
+    hbm = pl.BlockSpec(memory_space=pl.ANY)
     shapes = [
         (part, ua),
         (part, ff // 2 + part - ua),
@@ -1513,7 +1513,7 @@
 def proj_grads(ids, u, d):
     part = u.shape[1] // 2
     cols = d.shape[1]
-    hbm = pl.BlockSpec(memory_space=pltpu.HBM)
+    hbm = pl.BlockSpec(memory_space=pl.ANY)
     shapes = [(part, n) for n in (640, cols - 640, cols)]
     return pl.pallas_call(
         proj_grads_kernel,

time: 378 us -> 378 us (level)
  no operation moved by 1% of the time
where the time goes in v1:
time: 378 us; the launch traced here: 373 us
  Pallas kernels  147 us (39%)
  waiting for transfers between devices  93.7 us (25%)
  starting transfers between devices  73.8 us (20%)
  local copies, waits for them, and re-layouts  29.2 us (8%)
  between operations  15.4 us (4%)
  other arithmetic  13.4 us (4%)
    ppermute x10, waiting for transfers between devices, dp_flip(): return lax.ppermute(v, DP, [(i, i ^ by) for i in range(lax.axis_size(DP))])  42.3 us
    ppermute x26, starting transfers between devices, seq_flip(): return lax.ppermute(v, SEQ, [(i, i ^ by) for i in range(4)])  37.4 us
    pallas_call x2, Pallas kernels, attend_back(): pl.pallas_call(partial(attend_back_kernel, layer), out_shape=[jax.ShapeDt...  35.9 us
    ppermute x26, waiting for transfers between devices, seq_flip(): return lax.ppermute(v, SEQ, [(i, i ^ by) for i in range(4)])  34.4 us
    pallas_call x2, Pallas kernels, attend(): pl.pallas_call(partial(attend_kernel, layer), out_shape=outs, in_specs=[p...  29.8 us
    pallas_call x1, Pallas kernels, rows_both(): pl.pallas_call(rows_both_kernel, out_shape=[sds((rows, width), bf16), sds...  27.3 us
    unnamed x124, local copies, waits for them, and re-layouts  23.6 us
    ppermute x10, starting transfers between devices, dp_flip(): return lax.ppermute(v, DP, [(i, i ^ by) for i in range(lax.axis_size(DP))])  19.2 us
  transfers between devices with their start and end apart: 73, of which 21 were waited for; matrix products, arithmetic and copies ran while one was open for 5% of the time, Pallas kernels for 29%

profile of v1, /device:TPU:0, one launch (start us, length us, event | category | flops | bytes accessed | tf_op | source)
XLA Modules:
  0.0 373.2 jit_solution(2353281032749785650)
XLA Ops:
  8.8 2.6 collective-permute-start.1
  11.4 1.4 collective-permute-start.2
  17.9 3.4 prepare.1
  23.7 3.5 collective-permute-done.8.refs_11_.pack_b.refs_8_
  28.5 15.1 %attend.2 = (bf16[256,192]{1,0:T(8,128)(2,1)S(1)}, bf16[256,192]{1,0:T(8,128)(2,1)S(1)}, bf16[256,192]{1,0:T(8,128)(2,1)S(1)}, bf16[256,192]{1,0:T(8,128)(2,1)S(...) custom-call(s32[8]{0:T(128)S(1)} %stack.98.ids.refs_0_, ...), custom_call_target="tpu_custom_call" | custom-call | flops 14000000000 | bytes 49000000 | tf_op jit(solution)/shard_map/attend/pallas_call | solution.py:845
  45.7 1.9 collective-permute-start.12
  47.7 4.4 %collective-permute-done.12.c2 = bf16[256,192]{1,0:T(8,128)(2,1)S(1)} collective-permute-done((bf16[256,192]{1,0:T(8,128)(2,1)S(1)}, bf16[256,192]{1,0:T(8,128)(2,1)S(1)}, u32[]{:S(2)}, u32[]{:S(2)}) %collective-permute-start.12) | collective-permute-done | bytes 98336 | tf_op jit(solution)/shard_map/ppermute | solution.py:1576
  52.0 2.1 collective-permute-done.13.c3
  54.1 8.9 %rows_forward.1 = (bf16[256,768]{1,0:T(8,128)(2,1)S(1)}, bf16[256,4608]{1,0:T(8,128)(2,1)}, bf16[256,3072]{1,0:T(8,128)(2,1)}, f32[256,768]{1,0:T(8,128)S(1)}, f...) custom-call(s32[8]{0:T(128)S(1)} %stack.98.ids.refs_0_, ...), custom_call_target="tpu_custom_call" | custom-call | flops 10000000000 | bytes 35000000 | tf_op jit(solution)/shard_map/rows_forward/pallas_call | solution.py:1095
  65.1 1.7 collective-permute-start.15
  67.1 1.6 collective-permute-start.16
  69.2 3.0 collective-permute-done.17
  72.2 4.1 %collective-permute-done.15.refs_3_ = bf16[256,768]{1,0:T(8,128)(2,1)S(1)} collective-permute-done((bf16[256,768]{1,0:T(8,128)(2,1)S(1)}, bf16[256,768]{1,0:T(8,128)(2,1)S(1)}, u32[]{:S(2)}, u32[]{:S(2)}) %collective-permute-start.15) | collective-permute-done | bytes 393248 | tf_op jit(solution)/shard_map/ppermute | solution.py:1576
  77.0 1.5 collective-permute-start.24
  78.6 14.6 %attend.3 = (bf16[256,192]{1,0:T(8,128)(2,1)S(1)}, bf16[256,192]{1,0:T(8,128)(2,1)S(1)}, bf16[256,192]{1,0:T(8,128)(2,1)S(1)}, bf16[256,192]{1,0:T(8,128)(2,1)S(...) custom-call(s32[8]{0:T(128)S(1)} %stack.98.ids.refs_0_, ...), custom_call_target="tpu_custom_call" | custom-call | flops 14000000000 | bytes 49000000 | tf_op jit(solution)/shard_map/attend/pallas_call | solution.py:845
  94.2 3.0 collective-permute-start.20
  97.1 1.5 collective-permute-start.21
  99.0 4.5 %collective-permute-done.21.c2 = bf16[256,192]{1,0:T(8,128)(2,1)S(1)} collective-permute-done((bf16[256,192]{1,0:T(8,128)(2,1)S(1)}, bf16[256,192]{1,0:T(8,128)(2,1)S(1)}, u32[]{:S(2)}, u32[]{:S(2)}) %collective-permute-start.21) | collective-permute-done | bytes 98336 | tf_op jit(solution)/shard_map/ppermute | solution.py:1576
  104.4 27.3 %rows_both.1 = (bf16[256,768]{1,0:T(8,128)(2,1)S(1)}, f32[256,768]{1,0:T(8,128)S(1)}, bf16[256,192]{1,0:T(8,128)(2,1)S(1)}, bf16[256,192]{1,0:T(8,128)(2,1)S(1)}...) custom-call(s32[8]{0:T(128)S(1)} %stack.98.ids.refs_0_, ...), custom_call_target="tpu_custom_call" | custom-call | flops 15000000512 | bytes 52500000 | tf_op jit(solution)/shard_map/rows_both/pallas_call | solution.py:1359
  133.6 1.5 collective-permute-start.26
  135.0 4.2 %collective-permute-done.29.k1 = bf16[256,2304]{1,0:T(8,128)(2,1)S(1)} collective-permute-done((bf16[256,2304]{1,0:T(8,128)(2,1)}, bf16[256,2304]{1,0:T(8,128)(2,1)S(1)}, u32[]{:S(2)}, u32[]{:S(2)}) %collective-permute-start.29) | collective-permute-done | bytes 1179680 | tf_op jit(solution)/shard_map/ppermute | solution.py:1572
  139.3 1.5 copy-done.56
  142.0 7.7 %grads.2 = bf16[16,432,384]{2,1,0:T(8,128)(2,1)} custom-call(s32[8]{0:T(128)S(1)} %stack.98.ids.refs_0_, bf16[256,4608]{1,0:T(8,128)(2,1)} %get-tuple-element.263.f0, bf16[256,4608]{1,0:T(8,128)(2,1)} %copy-done.56, bf16[256,2304]{1,0:T(8,128)(2,1)S(1)} %copy-done.17, bf16[256,2304]{1,0:T(8,128)(2,1)S(1)} %collective-permute-done.29.k1), custom_call_target="tpu_custom_call" | custom-call | flops 5000000000 | bytes 17500000 | tf_op jit(solution)/shard_map/grads/pallas_call | solution.py:1483
  150.9 18.0 %attend_back.2 = (bf16[1024,1152]{1,0:T(8,128)(2,1)}, f32[4,192]{1,0:T(4,128)S(1)}, f32[256,768]{1,0:T(8,128)S(1)}, bf16[256,768]{1,0:T(8,128)(2,1)S(1)}, f32[25...) custom-call(s32[8]{0:T(128)S(1)} %stack.98.ids.refs_0_, bf16[256,192]{1,0:T(8,128)(2,1)S(1)} %get-tuple-element.266.d0, ...), custom_call_target="tpu_custom_call" | custom-call | flops 17999998976 | bytes 63000000 | tf_op jit(solution)/shard_map/attend_back/pallas_call | solution.py:986
  170.8 1.6 collective-permute-start.32
  172.4 5.7 %proj_grads.2 = (bf16[384,640]{1,0:T(8,128)(2,1)S(1)}, bf16[384,512]{1,0:T(8,128)(2,1)}, bf16[384,1152]{1,0:T(8,128)(2,1)S(1)}) custom-call(s32[8]{0:T(128)S(1)} %stack.98.ids.refs_0_, bf16[1024,768]{1,0:T(8,128)(2,1)S(1)} %copy-done.19, bf16[1024,1152]{1,0:T(8,128)(2,1)} %get-tuple-element.285.d_h), custom_call_target="tpu_custom_call" | custom-call | flops 4000000000 | bytes 14000000 | tf_op jit(solution)/shard_map/proj_grads/pallas_call | solution.py:1518
  178.2 12.9 %collective-permute-done.32 = bf16[256,768]{1,0:T(8,128)(2,1)S(1)} collective-permute-done((bf16[256,768]{1,0:T(8,128)(2,1)S(1)}, bf16[256,768]{1,0:T(8,128)(2,1)S(1)}, u32[]{:S(2)}, u32[]{:S(2)}) %collective-permute-start.32) | collective-permute-done | bytes 393248 | tf_op jit(solution)/shard_map/ppermute | solution.py:1576
  191.8 11.1 %rows_back.1 = (f32[256,768]{1,0:T(8,128)S(1)}, bf16[256,192]{1,0:T(8,128)(2,1)S(1)}, bf16[256,192]{1,0:T(8,128)(2,1)S(1)}, bf16[256,192]{1,0:T(8,128)(2,1)S(1)}...) custom-call(s32[8]{0:T(128)S(1)} %stack.98.ids.refs_0_, ...), custom_call_target="tpu_custom_call" | custom-call | flops 11000000512 | bytes 38500000 | tf_op jit(solution)/shard_map/rows_back/pallas_call | solution.py:1208
  204.7 1.5 collective-permute-start.40
  206.4 1.5 collective-permute-start.35
  208.1 9.6 %grads.3 = (bf16[384,1024]{1,0:T(8,128)(2,1)S(1)}, bf16[384,896]{1,0:T(8,128)(2,1)}, bf16[384,1920]{1,0:T(8,128)(2,1)}, bf16[8,96,384]{2,1,0:T(8,128)(2,1)S(1)},...) custom-call(s32[8]{0:T(128)S(1)} %stack.98.ids.refs_0_, bf16[256,4608]{1,0:T(8,128)(2,1)} %get-tuple-element.244.f0, ...), custom_call_target="tpu_custom_call" | custom-call | flops 5000000000 | bytes 17500000 | tf_op jit(solution)/shard_map/grads/pallas_call | solution.py:1483
  217.7 2.6 collective-permute-done.36.d3
  220.8 1.5 collective-permute-start.39
  222.4 1.4 collective-permute-start.46
  224.4 18.0 %attend_back.3 = (bf16[1024,1152]{1,0:T(8,128)(2,1)}, f32[4,192]{1,0:T(4,128)S(1)}, f32[256,768]{1,0:T(8,128)S(1)}, bf16[256,768]{1,0:T(8,128)(2,1)S(1)}, f32[25...) custom-call(s32[8]{0:T(128)S(1)} %stack.98.ids.refs_0_, bf16[256,192]{1,0:T(8,128)(2,1)S(1)} %get-tuple-element.317.d0, ...), custom_call_target="tpu_custom_call" | custom-call | flops 17999998976 | bytes 63000000 | tf_op jit(solution)/shard_map/attend_back/pallas_call | solution.py:986
  250.2 1.5 collective-permute-start.44
  251.7 1.5 collective-permute-start.43
  253.8 1.4 copy-done.18
  255.2 5.9 %proj_grads.3 = (bf16[384,640]{1,0:T(8,128)(2,1)S(1)}, bf16[384,512]{1,0:T(8,128)(2,1)S(1)}, bf16[384,1152]{1,0:T(8,128)(2,1)S(1)}) custom-call(s32[8]{0:T(128)S(1)} %stack.98.ids.refs_0_, bf16[1024,768]{1,0:T(8,128)(2,1)S(1)} %copy-done.18, bf16[1024,1152]{1,0:T(8,128)(2,1)} %get-tuple-element.356.d_h), custom_call_target="tpu_custom_call" | custom-call | flops 4000000000 | bytes 14000000 | tf_op jit(solution)/shard_map/proj_grads/pallas_call | solution.py:1518
  261.2 2.5 collective-permute-done.45
  263.8 4.1 %collective-permute-done.44 = bf16[2,2,48,1152]{3,2,0,1:T(8,128)(2,1)S(1)} collective-permute-done((bf16[2,2,48,1152]{3,2,0,1:T(8,128)(2,1)}, bf16[2,2,48,1152]{3,2,0,1:T(8,128)(2,1)S(1)}, u32[]{:S(2)}, u32[]{:S(2)}) %collective-permute-start.44) | collective-permute-done | bytes 442400 | tf_op jit(solution)/shard_map/ppermute | solution.py:1584
  267.8 1.7 add_convert_fusion
  272.0 2.0 collective-permute-start.50
  274.0 1.4 add_convert_fusion.1
  275.6 6.1 %collective-permute-start.51 = (bf16[2,48,1152]{2,1,0:T(8,128)(2,1)S(1)}, bf16[2,48,1152]{2,1,0:T(8,128)(2,1)S(1)}, u32[]{:S(2)}, u32[]{:S(2)}) collective-permute-start(bf16[2,48,1152]{2,1,0:T(8,128)(2,1)S(1)} %dynamic-slice_bitcast_fusion.3), channel_id=1, source_target_pairs={{0,2},{1,3},{2,0},{3,1},{4,6},{5,7},{6,4},{7,5},{8,10},{9,11},{10,... | collective-permute-start | bytes 663560 | tf_op jit(solution)/shard_map/ppermute | solution.py:1584
  282.6 21.0 %collective-permute-done.51 = bf16[2,48,1152]{2,1,0:T(8,128)(2,1)S(1)} collective-permute-done((bf16[2,48,1152]{2,1,0:T(8,128)(2,1)S(1)}, bf16[2,48,1152]{2,1,0:T(8,128)(2,1)S(1)}, u32[]{:S(2)}, u32[]{:S(2)}) %collective-permute-start.51) | collective-permute-done | bytes 221216 | tf_op jit(solution)/shard_map/ppermute | solution.py:1584
  303.6 1.5 collective-permute-start.58
  305.7 2.7 collective-permute-start.53
  308.4 3.5 collective-permute-start.54
  312.0 2.0 collective-permute-start.55
  314.7 2.2 collective-permute-done.58
  316.9 2.2 collective-permute-start.64
  319.1 10.9 %collective-permute-done.55 = f32[14,768]{1,0:T(8,128)S(1)} collective-permute-done((f32[14,768]{1,0:T(8,128)S(1)}, f32[14,768]{1,0:T(8,128)S(1)}, u32[]{:S(2)}, u32[]{:S(2)}) %collective-permute-start.55) | collective-permute-done | bytes 43040 | tf_op jit(solution)/shard_map/ppermute | solution.py:1584
  330.0 1.5 collective-permute-start.65
  333.9 1.8 collective-permute-start.60
  335.9 1.5 collective-permute-start.61
  337.9 4.8 %collective-permute-start.62 = (f32[14,768]{1,0:T(8,128)S(1)}, f32[14,768]{1,0:T(8,128)S(1)}, u32[]{:S(2)}, u32[]{:S(2)}) collective-permute-start(f32[14,768]{1,0:T(8,128)S(1)} %add.228), channel_id=1, source_target_pairs={{0,8},{4,12},{8,0},{12,4},{1,9},{5,13},{9,1},{13,5},{2,10},{6,14},... | collective-permute-start | bytes 129032 | tf_op jit(solution)/shard_map/ppermute | solution.py:1576
  342.7 2.1 collective-permute-done.62
  345.8 1.8 collective-permute-done.59
  348.3 3.0 collective-permute-start.66
  351.3 1.6 collective-permute-start.67
  353.1 1.5 fusion.8
  356.6 4.1 %collective-permute-done.68 = f32[14,768]{1,0:T(8,128)S(1)} collective-permute-done((f32[14,768]{1,0:T(8,128)S(1)}, f32[14,768]{1,0:T(8,128)S(1)}, u32[]{:S(2)}, u32[]{:S(2)}) %collective-permute-start.68) | collective-permute-done | bytes 43040 | tf_op jit(solution)/shard_map/ppermute | solution.py:1584
  364.0 2.1 assemble.1
  (285 shorter events, 51.4 us)
Async XLA Ops:
  7.2 239.1 %reduce-scatter.3.cloned.1.call-start = ((), (), s32[]{:S(2)}) async-start(), calls=%async_computation.2 | async-start | bytes 6635520 | tf_op jit(solution)/shard_map/reduce_scatter | solution.py:1731
  7.2 15.3 %collective-permute-start.3 = (bf16[768,3072]{1,0:T(8,128)(2,1)}, bf16[768,3072]{1,0:T(8,128)(2,1)}, u32[]{:S(2)}, u32[]{:S(2)}) collective-permute-start(bf16[768,3072]{1,0:T(8,128)(2,1)} %bitcast.178), channel_id=1, source_target_pairs={{0,16},{16,0},{1,17},{17,1},{2,18},{18,2},{3,19},{19,3},{4,20},{20... | collective-permute-start | bytes 14155784 | tf_op jit(solution)/shard_map/ppermute | solution.py:1572
  8.8 13.7 %collective-permute-start.1 = (bf16[128,768]{1,0:T(8,128)(2,1)S(1)}, bf16[128,768]{1,0:T(8,128)(2,1)S(1)}, u32[]{:S(2)}, u32[]{:S(2)}) collective-permute-start(bf16[128,768]{1,0:T(8,128)(2,1)S(1)} %get-tuple-element.436), channel_id=1, source_target_pairs={{0,8},{4,12},{8,0},{12,4},{1,9},{5,13},{9,1},{13,5},{2,10},{6,14},... | collective-permute-start | bytes 589832 | tf_op jit(solution)/shard_map/ppermute | solution.py:1576
  11.4 11.1 %collective-permute-start.2 = (bf16[128,768]{1,0:T(8,128)(2,1)S(1)}, bf16[128,768]{1,0:T(8,128)(2,1)S(1)}, u32[]{:S(2)}, u32[]{:S(2)}) collective-permute-start(bf16[128,768]{1,0:T(8,128)(2,1)S(1)} %get-tuple-element.436), channel_id=1, source_target_pairs={{0,12},{4,8},{8,4},{12,0},{1,13},{5,9},{9,5},{13,1},{2,14},{6,10},... | collective-permute-start | bytes 589832 | tf_op jit(solution)/shard_map/ppermute | solution.py:1576
  12.9 9.6 %collective-permute-start = (bf16[128,768]{1,0:T(8,128)(2,1)S(1)}, bf16[128,768]{1,0:T(8,128)(2,1)S(1)}, u32[]{:S(2)}, u32[]{:S(2)}) collective-permute-start(bf16[128,768]{1,0:T(8,128)(2,1)S(1)} %get-tuple-element.437), channel_id=1, source_target_pairs={{0,4},{4,0},{8,12},{12,8},{1,5},{5,1},{9,13},{13,9},{2,6},{6,2},{1... | collective-permute-start | bytes 589832 | tf_op jit(solution)/shard_map/ppermute | solution.py:1576
  22.5 4.7 %collective-permute-start.7 = (bf16[768,1152]{1,0:T(8,128)(2,1)S(1)}, bf16[768,1152]{1,0:T(8,128)(2,1)S(1)}, u32[]{:S(2)}, u32[]{:S(2)}) collective-permute-start(bf16[768,1152]{1,0:T(8,128)(2,1)S(1)} %get-tuple-element.226), channel_id=1, source_target_pairs={{0,16},{16,0},{1,17},{17,1},{2,18},{18,2},{3,19},{19,3},{4,20},{20... | collective-permute-start | bytes 5308424 | tf_op jit(solution)/shard_map/ppermute | solution.py:1572
  22.6 4.6 %collective-permute-start.4 = (bf16[128,768]{1,0:T(8,128)(2,1)S(1)}, bf16[128,768]{1,0:T(8,128)(2,1)S(1)}, u32[]{:S(2)}, u32[]{:S(2)}) collective-permute-start(bf16[128,768]{1,0:T(8,128)(2,1)S(1)} %collective-permute-done.refs_2_), channel_id=1, source_target_pairs={{0,16},{16,0},{1,17},{17,1},{2,18},{18,2},{3,19},{19,3},{4,20},{20... | collective-permute-start | bytes 589832 | tf_op jit(solution)/shard_map/ppermute | solution.py:1572
  23.1 4.1 %collective-permute-start.5 = (bf16[128,768]{1,0:T(8,128)(2,1)S(1)}, bf16[128,768]{1,0:T(8,128)(2,1)S(1)}, u32[]{:S(2)}, u32[]{:S(2)}) collective-permute-start(bf16[128,768]{1,0:T(8,128)(2,1)S(1)} %collective-permute-done.1.refs_3_), channel_id=1, source_target_pairs={{0,16},{16,0},{1,17},{17,1},{2,18},{18,2},{3,19},{19,3},{4,20},{20... | collective-permute-start | bytes 589832 | tf_op jit(solution)/shard_map/ppermute | solution.py:1572
  23.2 4.0 %collective-permute-start.6 = (bf16[128,768]{1,0:T(8,128)(2,1)S(1)}, bf16[128,768]{1,0:T(8,128)(2,1)S(1)}, u32[]{:S(2)}, u32[]{:S(2)}) collective-permute-start(bf16[128,768]{1,0:T(8,128)(2,1)S(1)} %collective-permute-done.2.refs_4_), channel_id=1, source_target_pairs={{0,16},{16,0},{1,17},{17,1},{2,18},{18,2},{3,19},{19,3},{4,20},{20... | collective-permute-start | bytes 589832 | tf_op jit(solution)/shard_map/ppermute | solution.py:1572
  23.6 3.6 collective-permute-start.8
  27.2 18.3 %collective-permute-start.10 = (bf16[3072,768]{1,0:T(8,128)(2,1)}, bf16[3072,768]{1,0:T(8,128)(2,1)}, u32[]{:S(2)}, u32[]{:S(2)}) collective-permute-start(bf16[3072,768]{1,0:T(8,128)(2,1)} %bitcast.21.wd_a), channel_id=1, source_target_pairs={{0,16},{16,0},{1,17},{17,1},{2,18},{18,2},{3,19},{19,3},{4,20},{20... | collective-permute-start | bytes 14155784 | tf_op jit(solution)/shard_map/ppermute | solution.py:1572
  27.5 18.0 %collective-permute-start.9 = (bf16[768,768]{1,0:T(8,128)(2,1)}, bf16[768,768]{1,0:T(8,128)(2,1)S(1)}, u32[]{:S(2)}, u32[]{:S(2)}) collective-permute-start(bf16[768,768]{1,0:T(8,128)(2,1)} %bitcast.184), channel_id=1, source_target_pairs={{0,16},{16,0},{1,17},{17,1},{2,18},{18,2},{3,19},{19,3},{4,20},{20... | collective-permute-start | bytes 3538952 | tf_op jit(solution)/shard_map/ppermute | solution.py:1572
  45.7 6.3 %collective-permute-start.12 = (bf16[256,192]{1,0:T(8,128)(2,1)S(1)}, bf16[256,192]{1,0:T(8,128)(2,1)S(1)}, u32[]{:S(2)}, u32[]{:S(2)}) collective-permute-start(bf16[256,192]{1,0:T(8,128)(2,1)S(1)} %get-tuple-element.237), channel_id=1, source_target_pairs={{0,4},{4,0},{8,12},{12,8},{1,5},{5,1},{9,13},{13,9},{2,6},{6,2},{1... | collective-permute-start | bytes 294920 | tf_op jit(solution)/shard_map/ppermute | solution.py:1576
  47.7 6.4 %collective-permute-start.13 = (bf16[256,192]{1,0:T(8,128)(2,1)S(1)}, bf16[256,192]{1,0:T(8,128)(2,1)S(1)}, u32[]{:S(2)}, u32[]{:S(2)}) collective-permute-start(bf16[256,192]{1,0:T(8,128)(2,1)S(1)} %get-tuple-element.238), channel_id=1, source_target_pairs={{0,20},{4,16},{8,28},{12,24},{16,4},{20,0},{24,12},{28,8},{1,21},{... | collective-permute-start | bytes 294920 | tf_op jit(solution)/shard_map/ppermute | solution.py:1580
  64.8 11.5 %collective-permute-start.18 = (bf16[256,4608]{1,0:T(8,128)(2,1)}, bf16[256,4608]{1,0:T(8,128)(2,1)}, u32[]{:S(2)}, u32[]{:S(2)}) collective-permute-start(bf16[256,4608]{1,0:T(8,128)(2,1)} %get-tuple-element.244.f0), channel_id=1, source_target_pairs={{0,16},{16,0},{1,17},{17,1},{2,18},{18,2},{3,19},{19,3},{4,20},{20... | collective-permute-start | bytes 7077896 | tf_op jit(solution)/shard_map/ppermute | solution.py:1572
  65.1 11.2 %collective-permute-start.15 = (bf16[256,768]{1,0:T(8,128)(2,1)S(1)}, bf16[256,768]{1,0:T(8,128)(2,1)S(1)}, u32[]{:S(2)}, u32[]{:S(2)}) collective-permute-start(bf16[256,768]{1,0:T(8,128)(2,1)S(1)} %get-tuple-element.243.refs_1_), channel_id=1, source_target_pairs={{0,4},{4,0},{8,12},{12,8},{1,5},{5,1},{9,13},{13,9},{2,6},{6,2},{1... | collective-permute-start | bytes 1179656 | tf_op jit(solution)/shard_map/ppermute | solution.py:1576
  67.1 5.1 %collective-permute-start.16 = (bf16[38,768]{1,0:T(8,128)(2,1)S(1)}, bf16[38,768]{1,0:T(8,128)(2,1)S(1)}, u32[]{:S(2)}, u32[]{:S(2)}) collective-permute-start(bf16[38,768]{1,0:T(8,128)(2,1)S(1)} %bitcast.176), channel_id=1, source_target_pairs={{0,8},{4,12},{8,0},{12,4},{1,9},{5,13},{9,1},{13,5},{2,10},{6,14},... | collective-permute-start | bytes 175112 | tf_op jit(solution)/shard_map/ppermute | solution.py:1576
  69.2 9.4 %collective-permute-start.14 = (bf16[256,768]{1,0:T(8,128)(2,1)S(1)}, bf16[256,768]{1,0:T(8,128)(2,1)S(1)}, u32[]{:S(2)}, u32[]{:S(2)}) collective-permute-start(bf16[256,768]{1,0:T(8,128)(2,1)S(1)} %get-tuple-element.243.refs_1_), channel_id=1, source_target_pairs={{0,16},{16,0},{1,17},{17,1},{2,18},{18,2},{3,19},{19,3},{4,20},{20... | collective-permute-start | bytes 1179656 | tf_op jit(solution)/shard_map/ppermute | solution.py:1572
  76.3 22.6 %collective-permute-start.23 = (bf16[256,768]{1,0:T(8,128)(2,1)S(1)}, bf16[256,768]{1,0:T(8,128)(2,1)S(1)}, u32[]{:S(2)}, u32[]{:S(2)}) collective-permute-start(bf16[256,768]{1,0:T(8,128)(2,1)S(1)} %get-tuple-element.243.refs_1_), channel_id=1, source_target_pairs={{0,0},{4,4},{24,8},{28,12},{1,1},{5,5},{25,9},{29,13},{2,2},{6,6},... | collective-permute-start | bytes 1179656 | tf_op jit(solution)/shard_map/ppermute | solution.py:1599
  77.0 21.9 %collective-permute-start.24 = (bf16[256,768]{1,0:T(8,128)(2,1)S(1)}, bf16[256,768]{1,0:T(8,128)(2,1)S(1)}, u32[]{:S(2)}, u32[]{:S(2)}) collective-permute-start(bf16[256,768]{1,0:T(8,128)(2,1)S(1)} %get-tuple-element.243.refs_1_), channel_id=1, source_target_pairs={{16,8},{20,12},{8,0},{12,4},{17,9},{21,13},{9,1},{13,5},{18,10},{2... | collective-permute-start | bytes 1179656 | tf_op jit(solution)/shard_map/ppermute | solution.py:1599
  94.2 4.8 %collective-permute-start.20 = (bf16[256,192]{1,0:T(8,128)(2,1)S(1)}, bf16[256,192]{1,0:T(8,128)(2,1)S(1)}, u32[]{:S(2)}, u32[]{:S(2)}) collective-permute-start(bf16[256,192]{1,0:T(8,128)(2,1)S(1)} %get-tuple-element.247), channel_id=1, source_target_pairs={{0,16},{16,0},{1,17},{17,1},{2,18},{18,2},{3,19},{19,3},{4,20},{20... | collective-permute-start | bytes 294920 | tf_op jit(solution)/shard_map/ppermute | solution.py:1572
  97.1 6.3 %collective-permute-start.21 = (bf16[256,192]{1,0:T(8,128)(2,1)S(1)}, bf16[256,192]{1,0:T(8,128)(2,1)S(1)}, u32[]{:S(2)}, u32[]{:S(2)}) collective-permute-start(bf16[256,192]{1,0:T(8,128)(2,1)S(1)} %get-tuple-element.248), channel_id=1, source_target_pairs={{0,4},{4,0},{8,12},{12,8},{1,5},{5,1},{9,13},{13,9},{2,6},{6,2},{1... | collective-permute-start | bytes 294920 | tf_op jit(solution)/shard_map/ppermute | solution.py:1576
  98.6 5.8 %collective-permute-start.22 = (bf16[256,192]{1,0:T(8,128)(2,1)S(1)}, bf16[256,192]{1,0:T(8,128)(2,1)S(1)}, u32[]{:S(2)}, u32[]{:S(2)}) collective-permute-start(bf16[256,192]{1,0:T(8,128)(2,1)S(1)} %get-tuple-element.249), channel_id=1, source_target_pairs={{0,20},{4,16},{8,28},{12,24},{16,4},{20,0},{24,12},{28,8},{1,21},{... | collective-permute-start | bytes 294920 | tf_op jit(solution)/shard_map/ppermute | solution.py:1580
  132.4 6.9 %collective-permute-start.28 = (bf16[256,4608]{1,0:T(8,128)(2,1)}, bf16[256,4608]{1,0:T(8,128)(2,1)S(1)}, u32[]{:S(2)}, u32[]{:S(2)}) collective-permute-start(bf16[256,4608]{1,0:T(8,128)(2,1)} %get-tuple-element.263.f0), channel_id=1, source_target_pairs={{0,16},{16,0},{1,17},{17,1},{2,18},{18,2},{3,19},{19,3},{4,20},{20... | collective-permute-start | bytes 7077896 | tf_op jit(solution)/shard_map/ppermute | solution.py:1572
  133.0 6.2 %collective-permute-start.29 = (bf16[256,2304]{1,0:T(8,128)(2,1)}, bf16[256,2304]{1,0:T(8,128)(2,1)S(1)}, u32[]{:S(2)}, u32[]{:S(2)}) collective-permute-start(bf16[256,2304]{1,0:T(8,128)(2,1)} %get-tuple-element.265), channel_id=1, source_target_pairs={{0,16},{16,0},{1,17},{17,1},{2,18},{18,2},{3,19},{19,3},{4,20},{20... | collective-permute-start | bytes 3538952 | tf_op jit(solution)/shard_map/ppermute | solution.py:1572
  133.0 16.7 %collective-permute-start.25 = (bf16[256,192]{1,0:T(8,128)(2,1)S(1)}, bf16[256,192]{1,0:T(8,128)(2,1)S(1)}, u32[]{:S(2)}, u32[]{:S(2)}) collective-permute-start(bf16[256,192]{1,0:T(8,128)(2,1)S(1)} %get-tuple-element.260), channel_id=1, source_target_pairs={{0,16},{16,0},{1,17},{17,1},{2,18},{18,2},{3,19},{19,3},{4,20},{20... | collective-permute-start | bytes 294920 | tf_op jit(solution)/shard_map/ppermute | solution.py:1572
  133.6 16.2 %collective-permute-start.26 = (bf16[256,192]{1,0:T(8,128)(2,1)S(1)}, bf16[256,192]{1,0:T(8,128)(2,1)S(1)}, u32[]{:S(2)}, u32[]{:S(2)}) collective-permute-start(bf16[256,192]{1,0:T(8,128)(2,1)S(1)} %get-tuple-element.261), channel_id=1, source_target_pairs={{0,4},{4,0},{8,12},{12,8},{1,5},{5,1},{9,13},{13,9},{2,6},{6,2},{1... | collective-permute-start | bytes 294920 | tf_op jit(solution)/shard_map/ppermute | solution.py:1576
  135.0 14.7 %collective-permute-start.27 = (bf16[256,192]{1,0:T(8,128)(2,1)S(1)}, bf16[256,192]{1,0:T(8,128)(2,1)S(1)}, u32[]{:S(2)}, u32[]{:S(2)}) collective-permute-start(bf16[256,192]{1,0:T(8,128)(2,1)S(1)} %get-tuple-element.262), channel_id=1, source_target_pairs={{0,20},{4,16},{8,28},{12,24},{16,4},{20,0},{24,12},{28,8},{1,21},{... | collective-permute-start | bytes 294920 | tf_op jit(solution)/shard_map/ppermute | solution.py:1580
  149.8 182.5 %reduce-scatter.5.cloned.1.call-start = ((), (), s32[]{:S(2)}) async-start(), calls=%async_computation.3 | async-start | bytes 1658880 | tf_op jit(solution)/shard_map/reduce_scatter | solution.py:1757
  170.8 20.2 %collective-permute-start.32 = (bf16[256,768]{1,0:T(8,128)(2,1)S(1)}, bf16[256,768]{1,0:T(8,128)(2,1)S(1)}, u32[]{:S(2)}, u32[]{:S(2)}) collective-permute-start(bf16[256,768]{1,0:T(8,128)(2,1)S(1)} %add_convert_fusion.7), channel_id=1, source_target_pairs={{0,4},{4,0},{8,12},{12,8},{1,5},{5,1},{9,13},{13,9},{2,6},{6,2},{1... | collective-permute-start | bytes 1179656 | tf_op jit(solution)/shard_map/ppermute | solution.py:1576
  172.4 19.2 %collective-permute-start.30 = (bf16[256,768]{1,0:T(8,128)(2,1)S(1)}, bf16[256,768]{1,0:T(8,128)(2,1)S(1)}, u32[]{:S(2)}, u32[]{:S(2)}) collective-permute-start(bf16[256,768]{1,0:T(8,128)(2,1)S(1)} %get-tuple-element.280), channel_id=1, source_target_pairs={{0,16},{16,0},{1,17},{17,1},{2,18},{18,2},{3,19},{19,3},{4,20},{20... | collective-permute-start | bytes 1179656 | tf_op jit(solution)/shard_map/ppermute | solution.py:1572
  191.0 12.8 %collective-permute-start.33 = (bf16[384,640]{1,0:T(8,128)(2,1)S(1)}, bf16[384,640]{1,0:T(8,128)(2,1)S(1)}, u32[]{:S(2)}, u32[]{:S(2)}) collective-permute-start(bf16[384,640]{1,0:T(8,128)(2,1)S(1)} %get-tuple-element.303), channel_id=1, source_target_pairs={{0,8},{4,12},{8,0},{12,4},{1,9},{5,13},{9,1},{13,5},{2,10},{6,14},... | collective-permute-start | bytes 1474568 | tf_op jit(solution)/shard_map/ppermute | solution.py:1576
  204.7 40.0 %collective-permute-start.40 = (bf16[384,512]{1,0:T(8,128)(2,1)}, bf16[384,512]{1,0:T(8,128)(2,1)S(1)}, u32[]{:S(2)}, u32[]{:S(2)}) collective-permute-start(bf16[384,512]{1,0:T(8,128)(2,1)} %get-tuple-element.339), channel_id=1, source_target_pairs={{0,8},{4,12},{8,0},{12,4},{1,9},{5,13},{9,1},{13,5},{2,10},{6,14},... | collective-permute-start | bytes 1179656 | tf_op jit(solution)/shard_map/ppermute | solution.py:1576
  206.2 11.5 %collective-permute-start.34 = (bf16[256,192]{1,0:T(8,128)(2,1)S(1)}, bf16[256,192]{1,0:T(8,128)(2,1)S(1)}, u32[]{:S(2)}, u32[]{:S(2)}) collective-permute-start(bf16[256,192]{1,0:T(8,128)(2,1)S(1)} %get-tuple-element.305), channel_id=1, source_target_pairs={{0,16},{16,0},{1,17},{17,1},{2,18},{18,2},{3,19},{19,3},{4,20},{20... | collective-permute-start | bytes 294920 | tf_op jit(solution)/shard_map/ppermute | solution.py:1572
  206.4 11.3 %collective-permute-start.35 = (bf16[256,192]{1,0:T(8,128)(2,1)S(1)}, bf16[256,192]{1,0:T(8,128)(2,1)S(1)}, u32[]{:S(2)}, u32[]{:S(2)}) collective-permute-start(bf16[256,192]{1,0:T(8,128)(2,1)S(1)} %get-tuple-element.306), channel_id=1, source_target_pairs={{0,4},{4,0},{8,12},{12,8},{1,5},{5,1},{9,13},{13,9},{2,6},{6,2},{1... | collective-permute-start | bytes 294920 | tf_op jit(solution)/shard_map/ppermute | solution.py:1576
  207.9 12.4 %collective-permute-start.36 = (bf16[256,192]{1,0:T(8,128)(2,1)S(1)}, bf16[256,192]{1,0:T(8,128)(2,1)S(1)}, u32[]{:S(2)}, u32[]{:S(2)}) collective-permute-start(bf16[256,192]{1,0:T(8,128)(2,1)S(1)} %get-tuple-element.307), channel_id=1, source_target_pairs={{0,20},{4,16},{8,28},{12,24},{16,4},{20,0},{24,12},{28,8},{1,21},{... | collective-permute-start | bytes 294920 | tf_op jit(solution)/shard_map/ppermute | solution.py:1580
  220.3 26.0 %collective-permute-start.38 = (bf16[384,1024]{1,0:T(8,128)(2,1)S(1)}, bf16[384,1024]{1,0:T(8,128)(2,1)}, u32[]{:S(2)}, u32[]{:S(2)}) collective-permute-start(bf16[384,1024]{1,0:T(8,128)(2,1)S(1)} %get-tuple-element.337), channel_id=1, source_target_pairs={{0,8},{4,12},{8,0},{12,4},{1,9},{5,13},{9,1},{13,5},{2,10},{6,14},... | collective-permute-start | bytes 2359304 | tf_op jit(solution)/shard_map/ppermute | solution.py:1576
  220.8 23.9 %collective-permute-start.39 = (bf16[8,96,384]{2,1,0:T(8,128)(2,1)S(1)}, bf16[8,96,384]{2,1,0:T(8,128)(2,1)S(1)}, u32[]{:S(2)}, u32[]{:S(2)}) collective-permute-start(bf16[8,96,384]{2,1,0:T(8,128)(2,1)S(1)} %get-tuple-element.338), channel_id=1, source_target_pairs={{0,4},{4,0},{8,12},{12,8},{1,5},{5,1},{9,13},{13,9},{2,6},{6,2},{1... | collective-permute-start | bytes 1769480 | tf_op jit(solution)/shard_map/ppermute | solution.py:1576
  222.4 38.9 %collective-permute-start.46 = (bf16[384,896]{1,0:T(8,128)(2,1)}, bf16[384,896]{1,0:T(8,128)(2,1)}, u32[]{:S(2)}, u32[]{:S(2)}) collective-permute-start(bf16[384,896]{1,0:T(8,128)(2,1)} %get-tuple-element.353), channel_id=1, source_target_pairs={{0,8},{4,12},{8,0},{12,4},{1,9},{5,13},{9,1},{13,5},{2,10},{6,14},... | collective-permute-start | bytes 2064392 | tf_op jit(solution)/shard_map/ppermute | solution.py:1576
  223.8 37.3 %collective-permute-start.47 = (bf16[8,96,384]{2,1,0:T(8,128)(2,1)}, bf16[8,96,384]{2,1,0:T(8,128)(2,1)}, u32[]{:S(2)}, u32[]{:S(2)}) collective-permute-start(bf16[8,96,384]{2,1,0:T(8,128)(2,1)} %get-tuple-element.354), channel_id=1, source_target_pairs={{0,4},{4,0},{8,12},{12,8},{1,5},{5,1},{9,13},{13,9},{2,6},{6,2},{1... | collective-permute-start | bytes 1769480 | tf_op jit(solution)/shard_map/ppermute | solution.py:1576
  250.2 17.7 %collective-permute-start.44 = (bf16[2,2,48,1152]{3,2,0,1:T(8,128)(2,1)}, bf16[2,2,48,1152]{3,2,0,1:T(8,128)(2,1)S(1)}, u32[]{:S(2)}, u32[]{:S(2)}) collective-permute-start(bf16[2,2,48,1152]{3,2,0,1:T(8,128)(2,1)} %bitcast.151), channel_id=1, source_target_pairs={{0,1},{1,0},{2,3},{3,2},{4,5},{5,4},{6,7},{7,6},{8,9},{9,8},{10,11... | collective-permute-start | bytes 1327112 | tf_op jit(solution)/shard_map/ppermute | solution.py:1584
  251.7 12.1 %collective-permute-start.43 = (bf16[256,768]{1,0:T(8,128)(2,1)}, bf16[256,768]{1,0:T(8,128)(2,1)S(1)}, u32[]{:S(2)}, u32[]{:S(2)}) collective-permute-start(bf16[256,768]{1,0:T(8,128)(2,1)} %add_convert_fusion.5), channel_id=1, source_target_pairs={{0,4},{4,0},{8,12},{12,8},{1,5},{5,1},{9,13},{13,9},{2,6},{6,2},{1... | collective-permute-start | bytes 1179656 | tf_op jit(solution)/shard_map/ppermute | solution.py:1576
  253.2 10.6 %collective-permute-start.45 = (f32[14,768]{1,0:T(8,128)S(1)}, f32[14,768]{1,0:T(8,128)S(1)}, u32[]{:S(2)}, u32[]{:S(2)}) collective-permute-start(f32[14,768]{1,0:T(8,128)S(1)} %select_add_fusion), channel_id=1, source_target_pairs={{0,4},{4,0},{8,12},{12,8},{1,5},{5,1},{9,13},{13,9},{2,6},{6,2},{1... | collective-permute-start | bytes 129032 | tf_op jit(solution)/shard_map/ppermute | solution.py:1576
  261.2 20.6 %collective-permute-start.56 = (bf16[256,768]{1,0:T(8,128)(2,1)S(1)}, bf16[256,768]{1,0:T(8,128)(2,1)S(1)}, u32[]{:S(2)}, u32[]{:S(2)}) collective-permute-start(bf16[256,768]{1,0:T(8,128)(2,1)S(1)} %copy-done.7), channel_id=1, source_target_pairs={{0,16},{16,0},{1,17},{17,1},{2,18},{18,2},{3,19},{19,3},{4,20},{20... | collective-permute-start | bytes 1179656 | tf_op jit(solution)/shard_map/ppermute | solution.py:1572
  270.0 35.2 %collective-permute-start.49 = (bf16[2,2,48,1920]{3,2,0,1:T(8,128)(2,1)S(1)}, bf16[2,2,48,1920]{3,2,0,1:T(8,128)(2,1)S(1)}, u32[]{:S(2)}, u32[]{:S(2)}) collective-permute-start(bf16[2,2,48,1920]{3,2,0,1:T(8,128)(2,1)S(1)} %bitcast.169), channel_id=1, source_target_pairs={{0,1},{1,0},{2,3},{3,2},{4,5},{5,4},{6,7},{7,6},{8,9},{9,8},{10,11... | collective-permute-start | bytes 2211848 | tf_op jit(solution)/shard_map/ppermute | solution.py:1584
  272.0 33.2 %collective-permute-start.48 = (bf16[384,640]{1,0:T(8,128)(2,1)S(1)}, bf16[384,640]{1,0:T(8,128)(2,1)S(1)}, u32[]{:S(2)}, u32[]{:S(2)}) collective-permute-start(bf16[384,640]{1,0:T(8,128)(2,1)S(1)} %get-tuple-element.367), channel_id=1, source_target_pairs={{0,8},{4,12},{8,0},{12,4},{1,9},{5,13},{9,1},{13,5},{2,10},{6,14},... | collective-permute-start | bytes 1474568 | tf_op jit(solution)/shard_map/ppermute | solution.py:1576
  272.0 33.2 %collective-permute-start.50 = (bf16[384,512]{1,0:T(8,128)(2,1)S(1)}, bf16[384,512]{1,0:T(8,128)(2,1)S(1)}, u32[]{:S(2)}, u32[]{:S(2)}) collective-permute-start(bf16[384,512]{1,0:T(8,128)(2,1)S(1)} %get-tuple-element.369), channel_id=1, source_target_pairs={{0,8},{4,12},{8,0},{12,4},{1,9},{5,13},{9,1},{13,5},{2,10},{6,14},... | collective-permute-start | bytes 1179656 | tf_op jit(solution)/shard_map/ppermute | solution.py:1576
  275.6 28.0 %collective-permute-start.51 = (bf16[2,48,1152]{2,1,0:T(8,128)(2,1)S(1)}, bf16[2,48,1152]{2,1,0:T(8,128)(2,1)S(1)}, u32[]{:S(2)}, u32[]{:S(2)}) collective-permute-start(bf16[2,48,1152]{2,1,0:T(8,128)(2,1)S(1)} %dynamic-slice_bitcast_fusion.3), channel_id=1, source_target_pairs={{0,2},{1,3},{2,0},{3,1},{4,6},{5,7},{6,4},{7,5},{8,10},{9,11},{10,... | collective-permute-start | bytes 663560 | tf_op jit(solution)/shard_map/ppermute | solution.py:1584
  281.9 30.1 %collective-permute-start.57 = (bf16[256,768]{1,0:T(8,128)(2,1)S(1)}, bf16[256,768]{1,0:T(8,128)(2,1)S(1)}, u32[]{:S(2)}, u32[]{:S(2)}) collective-permute-start(bf16[256,768]{1,0:T(8,128)(2,1)S(1)} %add_convert_fusion.4), channel_id=1, source_target_pairs={{0,0},{4,4},{24,8},{28,12},{1,1},{5,5},{25,9},{29,13},{2,2},{6,6},... | collective-permute-start | bytes 1179656 | tf_op jit(solution)/shard_map/ppermute | solution.py:1599
  303.6 13.3 %collective-permute-start.58 = (bf16[256,768]{1,0:T(8,128)(2,1)S(1)}, bf16[256,768]{1,0:T(8,128)(2,1)S(1)}, u32[]{:S(2)}, u32[]{:S(2)}) collective-permute-start(bf16[256,768]{1,0:T(8,128)(2,1)S(1)} %add_convert_fusion.4), channel_id=1, source_target_pairs={{16,8},{20,12},{8,0},{12,4},{17,9},{21,13},{9,1},{13,5},{18,10},{2... | collective-permute-start | bytes 1179656 | tf_op jit(solution)/shard_map/ppermute | solution.py:1599
  305.7 26.6 %collective-permute-start.53 = (bf16[2,2,192,384]{3,2,0,1:T(8,128)(2,1)S(1)}, bf16[2,2,192,384]{3,2,0,1:T(8,128)(2,1)S(1)}, u32[]{:S(2)}, u32[]{:S(2)}) collective-permute-start(bf16[2,2,192,384]{3,2,0,1:T(8,128)(2,1)S(1)} %bitcast.170), channel_id=1, source_target_pairs={{0,8},{4,12},{8,0},{12,4},{1,9},{5,13},{9,1},{13,5},{2,10},{6,14},... | collective-permute-start | bytes 1769480 | tf_op jit(solution)/shard_map/ppermute | solution.py:1576
  308.4 23.1 %collective-permute-start.54 = (bf16[2,2,48,1152]{3,2,0,1:T(8,128)(2,1)S(1)}, bf16[2,2,48,1152]{3,2,0,1:T(8,128)(2,1)S(1)}, u32[]{:S(2)}, u32[]{:S(2)}) collective-permute-start(bf16[2,2,48,1152]{3,2,0,1:T(8,128)(2,1)S(1)} %bitcast.171), channel_id=1, source_target_pairs={{0,1},{1,0},{2,3},{3,2},{4,5},{5,4},{6,7},{7,6},{8,9},{9,8},{10,11... | collective-permute-start | bytes 1327112 | tf_op jit(solution)/shard_map/ppermute | solution.py:1584
  311.9 19.6 %collective-permute-start.52 = (bf16[2,48,1920]{2,1,0:T(8,128)(2,1)S(1)}, bf16[2,48,1920]{2,1,0:T(8,128)(2,1)S(1)}, u32[]{:S(2)}, u32[]{:S(2)}) collective-permute-start(bf16[2,48,1920]{2,1,0:T(8,128)(2,1)S(1)} %dynamic-slice_bitcast_fusion), channel_id=1, source_target_pairs={{0,2},{1,3},{2,0},{3,1},{4,6},{5,7},{6,4},{7,5},{8,10},{9,11},{10,... | collective-permute-start | bytes 1105928 | tf_op jit(solution)/shard_map/ppermute | solution.py:1584
  312.0 18.0 %collective-permute-start.55 = (f32[14,768]{1,0:T(8,128)S(1)}, f32[14,768]{1,0:T(8,128)S(1)}, u32[]{:S(2)}, u32[]{:S(2)}) collective-permute-start(f32[14,768]{1,0:T(8,128)S(1)} %add.219), channel_id=1, source_target_pairs={{0,1},{1,0},{2,3},{3,2},{4,5},{5,4},{6,7},{7,6},{8,9},{9,8},{10,11... | collective-permute-start | bytes 129032 | tf_op jit(solution)/shard_map/ppermute | solution.py:1584
  316.9 20.5 %collective-permute-start.64 = (bf16[2,256,768]{2,1,0:T(8,128)(2,1)}, bf16[2,256,768]{2,1,0:T(8,128)(2,1)}, u32[]{:S(2)}, u32[]{:S(2)}) collective-permute-start(bf16[2,256,768]{2,1,0:T(8,128)(2,1)} %pad_maximum_fusion), channel_id=1, source_target_pairs={{0,16},{4,20},{24,24},{28,28},{1,17},{5,21},{25,25},{29,29},{2,18}... | collective-permute-start | bytes 2359304 | tf_op jit(solution)/shard_map/ppermute | solution.py:1599
  330.0 7.9 %collective-permute-start.65 = (bf16[2,256,768]{2,1,0:T(8,128)(2,1)}, bf16[2,256,768]{2,1,0:T(8,128)(2,1)}, u32[]{:S(2)}, u32[]{:S(2)}) collective-permute-start(bf16[2,256,768]{2,1,0:T(8,128)(2,1)} %pad_maximum_fusion), channel_id=1, source_target_pairs={{16,24},{20,28},{8,16},{12,20},{17,25},{21,29},{9,17},{13,21},{18,... | collective-permute-start | bytes 2359304 | tf_op jit(solution)/shard_map/ppermute | solution.py:1599
  333.9 14.1 %collective-permute-start.60 = (bf16[2,192,384]{2,1,0:T(8,128)(2,1)S(1)}, bf16[2,192,384]{2,1,0:T(8,128)(2,1)S(1)}, u32[]{:S(2)}, u32[]{:S(2)}) collective-permute-start(bf16[2,192,384]{2,1,0:T(8,128)(2,1)S(1)} %dynamic-slice_bitcast_fusion.1), channel_id=1, source_target_pairs={{0,1},{1,0},{2,3},{3,2},{4,5},{5,4},{6,7},{7,6},{8,9},{9,8},{10,11... | collective-permute-start | bytes 884744 | tf_op jit(solution)/shard_map/ppermute | solution.py:1584
  335.7 11.9 %collective-permute-start.59 = (bf16[2,48,1152]{2,1,0:T(8,128)(2,1)S(1)}, bf16[2,48,1152]{2,1,0:T(8,128)(2,1)S(1)}, u32[]{:S(2)}, u32[]{:S(2)}) collective-permute-start(bf16[2,48,1152]{2,1,0:T(8,128)(2,1)S(1)} %dynamic-slice_bitcast_fusion.2), channel_id=1, source_target_pairs={{0,2},{1,3},{2,0},{3,1},{4,6},{5,7},{6,4},{7,5},{8,10},{9,11},{10,... | collective-permute-start | bytes 663560 | tf_op jit(solution)/shard_map/ppermute | solution.py:1584
  335.9 9.9 %collective-permute-start.61 = (bf16[48,1920]{1,0:T(8,128)(2,1)S(1)}, bf16[48,1920]{1,0:T(8,128)(2,1)S(1)}, u32[]{:S(2)}, u32[]{:S(2)}) collective-permute-start(bf16[48,1920]{1,0:T(8,128)(2,1)S(1)} %dynamic-slice_bitcast_fusion.6), channel_id=1, source_target_pairs={{0,4},{4,0},{8,12},{12,8},{1,5},{5,1},{9,13},{13,9},{2,6},{6,2},{1... | collective-permute-start | bytes 552968 | tf_op jit(solution)/shard_map/ppermute | solution.py:1576
  337.4 8.4 %collective-permute-start.63 = (bf16[48,1152]{1,0:T(8,128)(2,1)S(1)}, bf16[48,1152]{1,0:T(8,128)(2,1)S(1)}, u32[]{:S(2)}, u32[]{:S(2)}) collective-permute-start(bf16[48,1152]{1,0:T(8,128)(2,1)S(1)} %copy-done.51), channel_id=1, source_target_pairs={{0,4},{4,0},{8,12},{12,8},{1,5},{5,1},{9,13},{13,9},{2,6},{6,2},{1... | collective-permute-start | bytes 331784 | tf_op jit(solution)/shard_map/ppermute | solution.py:1576
  337.9 6.9 %collective-permute-start.62 = (f32[14,768]{1,0:T(8,128)S(1)}, f32[14,768]{1,0:T(8,128)S(1)}, u32[]{:S(2)}, u32[]{:S(2)}) collective-permute-start(f32[14,768]{1,0:T(8,128)S(1)} %add.228), channel_id=1, source_target_pairs={{0,8},{4,12},{8,0},{12,4},{1,9},{5,13},{9,1},{13,5},{2,10},{6,14},... | collective-permute-start | bytes 129032 | tf_op jit(solution)/shard_map/ppermute | solution.py:1576
  348.3 12.4 %collective-permute-start.66 = (bf16[192,384]{1,0:T(8,128)(2,1)S(1)}, bf16[192,384]{1,0:T(8,128)(2,1)S(1)}, u32[]{:S(2)}, u32[]{:S(2)}) collective-permute-start(bf16[192,384]{1,0:T(8,128)(2,1)S(1)} %dynamic-slice_bitcast_fusion.7), channel_id=1, source_target_pairs={{0,2},{1,3},{2,0},{3,1},{4,6},{5,7},{6,4},{7,5},{8,10},{9,11},{10,... | collective-permute-start | bytes 442376 | tf_op jit(solution)/shard_map/ppermute | solution.py:1584
  351.3 9.4 %collective-permute-start.67 = (bf16[48,1152]{1,0:T(8,128)(2,1)S(1)}, bf16[48,1152]{1,0:T(8,128)(2,1)S(1)}, u32[]{:S(2)}, u32[]{:S(2)}) collective-permute-start(bf16[48,1152]{1,0:T(8,128)(2,1)S(1)} %get-tuple-element.410), channel_id=1, source_target_pairs={{0,4},{4,0},{8,12},{12,8},{1,5},{5,1},{9,13},{13,9},{2,6},{6,2},{1... | collective-permute-start | bytes 331784 | tf_op jit(solution)/shard_map/ppermute | solution.py:1576
  352.9 7.8 %collective-permute-start.68 = (f32[14,768]{1,0:T(8,128)S(1)}, f32[14,768]{1,0:T(8,128)S(1)}, u32[]{:S(2)}, u32[]{:S(2)}) collective-permute-start(f32[14,768]{1,0:T(8,128)S(1)} %add.234), channel_id=1, source_target_pairs={{0,2},{1,3},{2,0},{3,1},{4,6},{5,7},{6,4},{7,5},{8,10},{9,11},{10,... | collective-permute-start | bytes 129032 | tf_op jit(solution)/shard_map/ppermute | solution.py:1584
  (68 other events, 416.3 us)
Sparse Core Ops, SparseCore 0:
  149.9 81.5 reduce-scatter.2
  253.3 43.9 reduce-scatter.4

commit v2 on v1

--- a/solution.py
+++ b/solution.py
@@ -648,9 +648,7 @@
     return pltpu.make_async_copy(first, target, sem)
 
 
-def prepare_kernel(
-    ids, lw, gw, lb, gb, ob, ng, ns, db, ub, own_o, send_o, pack_o, win_s, sems
-):
+def prepare_kernel(ids, lw, gw, own_o, send_o, win_s, sems):
     width = lw.shape[0]
     hw = width // 4
     sources = [(lw, 0), (lw, 1), (lw, 2), (gw, 1), (gw, 2), (gw, 0)]
@@ -664,6 +662,19 @@
                 )
             )
             copies[-1].start()
+    for t, target in enumerate((send_o, own_o)):
+        for i in range(6):
+            copies[6 * t + i].wait()
+        for odd in range(2):
+
+            @pl.when(ids[6] == odd)
+            def _(t=t, target=target, odd=odd):
+                parts = [win_s[t, i][:, 64 * odd : 64 * odd + hw] for i in range(6)]
+                target[...] = jnp.concatenate(parts, axis=1)
+
+
+def pack_kernel(lb, gb, ob, ng, ns, db, ub, pack_o):
+    width = pack_o.shape[1]
     pack_o[...] = jnp.zeros(pack_o.shape, f32)
     at = 0
     for ref in (lb, gb, ob, ng, ns, db):
@@ -671,27 +682,29 @@
         at += ref.shape[0]
     for i in range(ub.shape[1] // width):
         pack_o[at + i : at + i + 1, :] = ub[:, i * width : (i + 1) * width].astype(f32)
-    for t, target in enumerate((send_o, own_o)):
-        for i in range(6):
-            copies[6 * t + i].wait()
-        for odd in range(2):
-
-            @pl.when(ids[6] == odd)
-            def _(t=t, target=target, odd=odd):
-                parts = [win_s[t, i][:, 64 * odd : 64 * odd + hw] for i in range(6)]
-                target[...] = jnp.concatenate(parts, axis=1)
-
-
-def prepare(ids, local_w, global_w, rows):
+
+
+def packed(rows, width):
+    return pl.pallas_call(
+        pack_kernel,
+        out_shape=jax.ShapeDtypeStruct((16, width), f32),
+        in_specs=[pl.BlockSpec(memory_space=pltpu.VMEM)] * 7,
+        out_specs=pl.BlockSpec(memory_space=pltpu.VMEM),
+        compiler_params=pltpu.CompilerParams(vmem_limit_bytes=VMEM_BYTES),
+        name="packed",
+    )(*rows)
+
+
+def prepare(ids, local_w, global_w):
     width = local_w.shape[0]
     vm = pl.BlockSpec(memory_space=pltpu.VMEM)
     hbm = pl.BlockSpec(memory_space=pl.ANY)
     chosen = jax.ShapeDtypeStruct((width, 6 * width // 4), bf16)
     return pl.pallas_call(
         prepare_kernel,
-        out_shape=[chosen, chosen, jax.ShapeDtypeStruct((16, width), f32)],
-        in_specs=[pl.BlockSpec(memory_space=pltpu.SMEM), hbm, hbm] + [vm] * 7,
-        out_specs=[vm] * 3,
+        out_shape=[chosen, chosen],
+        in_specs=[pl.BlockSpec(memory_space=pltpu.SMEM), hbm, hbm],
+        out_specs=[vm] * 2,
         scratch_shapes=[
             pltpu.VMEM((2, 6, width, 256), bf16),
             pltpu.SemaphoreType.DMA((12,)),
@@ -699,7 +712,7 @@
         compiler_params=pltpu.CompilerParams(vmem_limit_bytes=VMEM_BYTES),
         cost_estimate=cost(3),
         name="prepare",
-    )(ids, local_w, global_w, *rows)
+    )(ids, local_w, global_w)
 
 
 def attend_kernel(layer, *refs):
@@ -1644,17 +1657,14 @@
 
     ids = jnp.stack([g, g_other, 2 * c + 1 - x, 2 * (1 - c) + 1 - x, c, y, x, z]).astype(jnp.int32)
     ids, _ = lax.optimization_barrier((ids, (mine_part, away_part)))
-    w_own, w_send, pack = prepare(
-        ids,
-        local_weight[0],
-        global_weight[0],
+    w_own, w_send = prepare(ids, local_weight[0], global_weight[0])
+    pack = packed(
         (local_bias[0], global_bias[0], out_bias, norm_gain[0], norm_shift[0], down_bias, up_bias),
+        width,
     )
     own = (out_weight[0], up_weight[0], down_weight[0])
     other_up = core_flip(own[1])
-    (w_own, w_send, pack), (got, other_up) = lax.optimization_barrier(
-        ((w_own, w_send, pack), (got, other_up))
-    )
+    (w_own, pack), (got, other_up) = lax.optimization_barrier(((w_own, pack), (got, other_up)))
     weights = (w_own, core_flip(w_send))
     packs = (pack, core_flip(pack))
     positions = of_micro(global_positions[:, 0], y)

time: 378 us -> 368 us (0.974)
  Pallas kernels: 147 us -> 135 us
  waiting for transfers between devices: 93.7 us -> 103 us
  local copies, waits for them, and re-layouts: 29.2 us -> 23.7 us
    pallas_call x1, Pallas kernels: 27.3 us -> 14.7 us  [rows_both(): pl.pallas_call(rows_both_kernel, out_shape=[sds((rows, width), bf16), sds...]
    ppermute x26, waiting for transfers between devices: 34.4 us -> 45.3 us  [seq_flip(): return lax.ppermute(v, SEQ, [(i, i ^ by) for i in range(4)])]
    ppermute x26, starting transfers between devices: 37.4 us -> 31.5 us  [seq_flip(): return lax.ppermute(v, SEQ, [(i, i ^ by) for i in range(4)])]
    unnamed x124, local copies, waits for them, and re-layouts: 23.6 us -> 18.1 us
  transfers between devices with their start and end apart: 73 -> 73, of which waited for: 21 -> 24; matrix products, arithmetic and copies ran while one was open for 5% -> 5% of each run, Pallas kernels for 29% -> 30%
where the time goes in v2:
time: 368 us; the launch traced here: 363 us
  Pallas kernels  135 us (37%)
  waiting for transfers between devices  103 us (28%)
  starting transfers between devices  71.4 us (19%)
  local copies, waits for them, and re-layouts  23.7 us (6%)
  between operations  15.7 us (4%)
  other arithmetic  13.4 us (4%)
    ppermute x26, waiting for transfers between devices, seq_flip(): return lax.ppermute(v, SEQ, [(i, i ^ by) for i in range(4)])  45.3 us
    ppermute x10, waiting for transfers between devices, dp_flip(): return lax.ppermute(v, DP, [(i, i ^ by) for i in range(lax.axis_size(DP))])  43.7 us
    pallas_call x2, Pallas kernels, attend_back(): pl.pallas_call(partial(attend_back_kernel, layer), out_shape=[jax.ShapeDt...  35.9 us
    ppermute x26, starting transfers between devices, seq_flip(): return lax.ppermute(v, SEQ, [(i, i ^ by) for i in range(4)])  31.5 us
    pallas_call x2, Pallas kernels, attend(): pl.pallas_call(partial(attend_kernel, layer), out_shape=outs, in_specs=[p...  30.4 us
    ppermute x10, starting transfers between devices, dp_flip(): return lax.ppermute(v, DP, [(i, i ^ by) for i in range(lax.axis_size(DP))])  19.4 us
    unnamed x124, local copies, waits for them, and re-layouts  18.1 us
    pallas_call x2, Pallas kernels, grads(): pl.pallas_call(partial(grads_kernel, layer), out_shape=[jax.ShapeDtypeStr...  17.2 us
  transfers between devices with their start and end apart: 73, of which 24 were waited for; matrix products, arithmetic and copies ran while one was open for 5% of the time, Pallas kernels for 30%

profile of v2, /device:TPU:0, one launch (start us, length us, event | category | flops | bytes accessed | tf_op | source)
XLA Modules:
  0.0 362.5 jit_solution(3144650618903128286)
XLA Ops:
  9.0 3.4 prepare.1
  12.4 1.2 copy-done.16
  13.7 2.9 collective-permute-start
  16.6 1.5 collective-permute-start.1
  18.2 4.1 %collective-permute-done.refs_2_ = bf16[128,768]{1,0:T(8,128)(2,1)S(1)} collective-permute-done((bf16[128,768]{1,0:T(8,128)(2,1)S(1)}, bf16[128,768]{1,0:T(8,128)(2,1)S(1)}, u32[]{:S(2)}, u32[]{:S(2)}) %collective-permute-start) | collective-permute-done | bytes 196640 | tf_op jit(solution)/shard_map/ppermute | solution.py:1589
  22.3 5.1 %collective-permute-done.1.refs_3_ = bf16[128,768]{1,0:T(8,128)(2,1)S(1)} collective-permute-done((bf16[128,768]{1,0:T(8,128)(2,1)S(1)}, bf16[128,768]{1,0:T(8,128)(2,1)S(1)}, u32[]{:S(2)}, u32[]{:S(2)}) %collective-permute-start.1) | collective-permute-done | bytes 196640 | tf_op jit(solution)/shard_map/ppermute | solution.py:1589
  30.2 15.3 %attend.2 = (bf16[256,192]{1,0:T(8,128)(2,1)S(1)}, bf16[256,192]{1,0:T(8,128)(2,1)S(1)}, bf16[256,192]{1,0:T(8,128)(2,1)S(1)}, bf16[256,192]{1,0:T(8,128)(2,1)S(...) custom-call(s32[8]{0:T(128)S(1)} %stack.98.ids.refs_0_, ...), custom_call_target="tpu_custom_call" | custom-call | flops 14000000000 | bytes 49000000 | tf_op jit(solution)/shard_map/attend/pallas_call | solution.py:858
  47.7 1.2 collective-permute-start.12
  49.3 4.7 %collective-permute-done.12.c2 = bf16[256,192]{1,0:T(8,128)(2,1)S(1)} collective-permute-done((bf16[256,192]{1,0:T(8,128)(2,1)S(1)}, bf16[256,192]{1,0:T(8,128)(2,1)S(1)}, u32[]{:S(2)}, u32[]{:S(2)}) %collective-permute-start.12) | collective-permute-done | bytes 98336 | tf_op jit(solution)/shard_map/ppermute | solution.py:1589
  54.0 1.5 collective-permute-done.13.c3
  55.5 8.9 %rows_forward.1 = (bf16[256,768]{1,0:T(8,128)(2,1)S(1)}, bf16[256,4608]{1,0:T(8,128)(2,1)}, bf16[256,3072]{1,0:T(8,128)(2,1)}, f32[256,768]{1,0:T(8,128)S(1)}, f...) custom-call(s32[8]{0:T(128)S(1)} %stack.98.ids.refs_0_, ...), custom_call_target="tpu_custom_call" | custom-call | flops 10000000000 | bytes 35000000 | tf_op jit(solution)/shard_map/rows_forward/pallas_call | solution.py:1108
  66.8 1.2 collective-permute-start.15
  69.2 1.2 collective-permute-start.17
  70.4 2.3 collective-permute-done.17
  72.7 5.1 %collective-permute-done.15.refs_3_ = bf16[256,768]{1,0:T(8,128)(2,1)S(1)} collective-permute-done((bf16[256,768]{1,0:T(8,128)(2,1)S(1)}, bf16[256,768]{1,0:T(8,128)(2,1)S(1)}, u32[]{:S(2)}, u32[]{:S(2)}) %collective-permute-start.15) | collective-permute-done | bytes 393248 | tf_op jit(solution)/shard_map/ppermute | solution.py:1589
  78.5 1.3 collective-permute-start.24
  79.8 15.1 %attend.3 = (bf16[256,192]{1,0:T(8,128)(2,1)S(1)}, bf16[256,192]{1,0:T(8,128)(2,1)S(1)}, bf16[256,192]{1,0:T(8,128)(2,1)S(1)}, bf16[256,192]{1,0:T(8,128)(2,1)S(...) custom-call(s32[8]{0:T(128)S(1)} %stack.98.ids.refs_0_, ...), custom_call_target="tpu_custom_call" | custom-call | flops 14000000000 | bytes 49000000 | tf_op jit(solution)/shard_map/attend/pallas_call | solution.py:858
  95.8 2.9 collective-permute-start.20
  100.4 4.7 %collective-permute-done.21.c2 = bf16[256,192]{1,0:T(8,128)(2,1)S(1)} collective-permute-done((bf16[256,192]{1,0:T(8,128)(2,1)S(1)}, bf16[256,192]{1,0:T(8,128)(2,1)S(1)}, u32[]{:S(2)}, u32[]{:S(2)}) %collective-permute-start.21) | collective-permute-done | bytes 98336 | tf_op jit(solution)/shard_map/ppermute | solution.py:1589
  105.9 14.7 %rows_both.1 = (bf16[256,768]{1,0:T(8,128)(2,1)S(1)}, f32[256,768]{1,0:T(8,128)S(1)}, bf16[256,192]{1,0:T(8,128)(2,1)S(1)}, bf16[256,192]{1,0:T(8,128)(2,1)S(1)}...) custom-call(s32[8]{0:T(128)S(1)} %stack.98.ids.refs_0_, ...), custom_call_target="tpu_custom_call" | custom-call | flops 15000000512 | bytes 52500000 | tf_op jit(solution)/shard_map/rows_both/pallas_call | solution.py:1372
  124.0 4.4 %collective-permute-done.29.k1 = bf16[256,2304]{1,0:T(8,128)(2,1)S(1)} collective-permute-done((bf16[256,2304]{1,0:T(8,128)(2,1)}, bf16[256,2304]{1,0:T(8,128)(2,1)S(1)}, u32[]{:S(2)}, u32[]{:S(2)}) %collective-permute-start.29) | collective-permute-done | bytes 1179680 | tf_op jit(solution)/shard_map/ppermute | solution.py:1585
  128.4 1.5 copy-done.56
  129.8 1.3 copy-done.17
  131.1 7.7 %grads.2 = bf16[16,432,384]{2,1,0:T(8,128)(2,1)} custom-call(s32[8]{0:T(128)S(1)} %stack.98.ids.refs_0_, bf16[256,4608]{1,0:T(8,128)(2,1)} %get-tuple-element.259.f0, bf16[256,4608]{1,0:T(8,128)(2,1)} %copy-done.56, bf16[256,2304]{1,0:T(8,128)(2,1)S(1)} %copy-done.17, bf16[256,2304]{1,0:T(8,128)(2,1)S(1)} %collective-permute-done.29.k1), custom_call_target="tpu_custom_call" | custom-call | flops 5000000000 | bytes 17500000 | tf_op jit(solution)/shard_map/grads/pallas_call | solution.py:1496
  140.0 18.0 %attend_back.2 = (bf16[1024,1152]{1,0:T(8,128)(2,1)}, f32[4,192]{1,0:T(4,128)S(1)}, f32[256,768]{1,0:T(8,128)S(1)}, bf16[256,768]{1,0:T(8,128)(2,1)S(1)}, f32[25...) custom-call(s32[8]{0:T(128)S(1)} %stack.98.ids.refs_0_, bf16[256,192]{1,0:T(8,128)(2,1)S(1)} %get-tuple-element.262.d0, ...), custom_call_target="tpu_custom_call" | custom-call | flops 17999998976 | bytes 63000000 | tf_op jit(solution)/shard_map/attend_back/pallas_call | solution.py:999
  158.4 1.4 collective-permute-done.31
  160.6 5.7 %proj_grads.2 = (bf16[384,640]{1,0:T(8,128)(2,1)S(1)}, bf16[384,512]{1,0:T(8,128)(2,1)}, bf16[384,1152]{1,0:T(8,128)(2,1)S(1)}) custom-call(s32[8]{0:T(128)S(1)} %stack.98.ids.refs_0_, bf16[1024,768]{1,0:T(8,128)(2,1)S(1)} %copy-done.19, bf16[1024,1152]{1,0:T(8,128)(2,1)} %get-tuple-element.281.d_h), custom_call_target="tpu_custom_call" | custom-call | flops 4000000000 | bytes 14000000 | tf_op jit(solution)/shard_map/proj_grads/pallas_call | solution.py:1531
  166.3 13.8 %collective-permute-done.32 = bf16[256,768]{1,0:T(8,128)(2,1)S(1)} collective-permute-done((bf16[256,768]{1,0:T(8,128)(2,1)S(1)}, bf16[256,768]{1,0:T(8,128)(2,1)S(1)}, u32[]{:S(2)}, u32[]{:S(2)}) %collective-permute-start.32) | collective-permute-done | bytes 393248 | tf_op jit(solution)/shard_map/ppermute | solution.py:1589
  180.9 10.9 %rows_back.1 = (f32[256,768]{1,0:T(8,128)S(1)}, bf16[256,192]{1,0:T(8,128)(2,1)S(1)}, bf16[256,192]{1,0:T(8,128)(2,1)S(1)}, bf16[256,192]{1,0:T(8,128)(2,1)S(1)}...) custom-call(s32[8]{0:T(128)S(1)} %stack.98.ids.refs_0_, ...), custom_call_target="tpu_custom_call" | custom-call | flops 11000000512 | bytes 38500000 | tf_op jit(solution)/shard_map/rows_back/pallas_call | solution.py:1221
  193.7 1.3 collective-permute-start.40
  195.8 1.1 collective-permute-start.36
  196.9 9.5 %grads.3 = (bf16[384,1024]{1,0:T(8,128)(2,1)S(1)}, bf16[384,896]{1,0:T(8,128)(2,1)}, bf16[384,1920]{1,0:T(8,128)(2,1)}, bf16[8,96,384]{2,1,0:T(8,128)(2,1)S(1)},...) custom-call(s32[8]{0:T(128)S(1)} %stack.98.ids.refs_0_, bf16[256,4608]{1,0:T(8,128)(2,1)} %get-tuple-element.240.f0, ...), custom_call_target="tpu_custom_call" | custom-call | flops 5000000000 | bytes 17500000 | tf_op jit(solution)/shard_map/grads/pallas_call | solution.py:1496
  206.4 2.7 collective-permute-done.36.d3
  211.7 1.5 collective-permute-start.47
  213.2 17.9 %attend_back.3 = (bf16[1024,1152]{1,0:T(8,128)(2,1)}, f32[4,192]{1,0:T(4,128)S(1)}, f32[256,768]{1,0:T(8,128)S(1)}, bf16[256,768]{1,0:T(8,128)(2,1)S(1)}, f32[25...) custom-call(s32[8]{0:T(128)S(1)} %stack.98.ids.refs_0_, bf16[256,192]{1,0:T(8,128)(2,1)S(1)} %get-tuple-element.313.d0, ...), custom_call_target="tpu_custom_call" | custom-call | flops 17999998976 | bytes 63000000 | tf_op jit(solution)/shard_map/attend_back/pallas_call | solution.py:999
  235.7 1.4 add_convert_fusion.3
  239.0 1.6 collective-permute-start.44
  241.2 1.5 collective-permute-start.45
  242.6 1.4 copy-done.18
  244.1 5.9 %proj_grads.3 = (bf16[384,640]{1,0:T(8,128)(2,1)S(1)}, bf16[384,512]{1,0:T(8,128)(2,1)S(1)}, bf16[384,1152]{1,0:T(8,128)(2,1)S(1)}) custom-call(s32[8]{0:T(128)S(1)} %stack.98.ids.refs_0_, bf16[1024,768]{1,0:T(8,128)(2,1)S(1)} %copy-done.18, bf16[1024,1152]{1,0:T(8,128)(2,1)} %get-tuple-element.352.d_h), custom_call_target="tpu_custom_call" | custom-call | flops 4000000000 | bytes 14000000 | tf_op jit(solution)/shard_map/proj_grads/pallas_call | solution.py:1531
  250.1 2.5 collective-permute-done.45
  252.6 3.8 %collective-permute-done.44 = bf16[2,2,48,1152]{3,2,0,1:T(8,128)(2,1)S(1)} collective-permute-done((bf16[2,2,48,1152]{3,2,0,1:T(8,128)(2,1)}, bf16[2,2,48,1152]{3,2,0,1:T(8,128)(2,1)S(1)}, u32[]{:S(2)}, u32[]{:S(2)}) %collective-permute-start.44) | collective-permute-done | bytes 442400 | tf_op jit(solution)/shard_map/ppermute | solution.py:1597
  256.5 1.8 add_convert_fusion
  260.6 2.0 collective-permute-start.50
  262.7 1.4 add_convert_fusion.1
  264.3 6.2 %collective-permute-start.51 = (bf16[2,48,1152]{2,1,0:T(8,128)(2,1)S(1)}, bf16[2,48,1152]{2,1,0:T(8,128)(2,1)S(1)}, u32[]{:S(2)}, u32[]{:S(2)}) collective-permute-start(bf16[2,48,1152]{2,1,0:T(8,128)(2,1)S(1)} %dynamic-slice_bitcast_fusion.3), channel_id=1, source_target_pairs={{0,2},{1,3},{2,0},{3,1},{4,6},{5,7},{6,4},{7,5},{8,10},{9,11},{10,... | collective-permute-start | bytes 663560 | tf_op jit(solution)/shard_map/ppermute | solution.py:1597
  271.4 21.1 %collective-permute-done.51 = bf16[2,48,1152]{2,1,0:T(8,128)(2,1)S(1)} collective-permute-done((bf16[2,48,1152]{2,1,0:T(8,128)(2,1)S(1)}, bf16[2,48,1152]{2,1,0:T(8,128)(2,1)S(1)}, u32[]{:S(2)}, u32[]{:S(2)}) %collective-permute-start.51) | collective-permute-done | bytes 221216 | tf_op jit(solution)/shard_map/ppermute | solution.py:1597
  292.5 1.5 collective-permute-start.58
  294.6 2.7 collective-permute-start.53
  297.3 3.5 collective-permute-start.54
  300.9 2.0 collective-permute-start.55
  303.5 1.9 collective-permute-done.58
  305.4 2.2 collective-permute-start.64
  307.6 11.4 %collective-permute-done.55 = f32[14,768]{1,0:T(8,128)S(1)} collective-permute-done((f32[14,768]{1,0:T(8,128)S(1)}, f32[14,768]{1,0:T(8,128)S(1)}, u32[]{:S(2)}, u32[]{:S(2)}) %collective-permute-start.55) | collective-permute-done | bytes 43040 | tf_op jit(solution)/shard_map/ppermute | solution.py:1597
  319.1 1.5 collective-permute-start.65
  321.5 1.2 fusion.2
  323.0 1.8 collective-permute-start.60
  327.0 4.8 %collective-permute-start.62 = (f32[14,768]{1,0:T(8,128)S(1)}, f32[14,768]{1,0:T(8,128)S(1)}, u32[]{:S(2)}, u32[]{:S(2)}) collective-permute-start(f32[14,768]{1,0:T(8,128)S(1)} %add.228), channel_id=1, source_target_pairs={{0,8},{4,12},{8,0},{12,4},{1,9},{5,13},{9,1},{13,5},{2,10},{6,14},... | collective-permute-start | bytes 129032 | tf_op jit(solution)/shard_map/ppermute | solution.py:1589
  331.8 2.1 collective-permute-done.62
  334.6 1.8 collective-permute-done.59
  337.2 2.9 collective-permute-start.66
  341.2 1.5 fusion.8
  344.8 5.0 %collective-permute-done.68 = f32[14,768]{1,0:T(8,128)S(1)} collective-permute-done((f32[14,768]{1,0:T(8,128)S(1)}, f32[14,768]{1,0:T(8,128)S(1)}, u32[]{:S(2)}, u32[]{:S(2)}) %collective-permute-start.68) | collective-permute-done | bytes 43040 | tf_op jit(solution)/shard_map/ppermute | solution.py:1597
  353.1 2.1 assemble.1
  (286 shorter events, 49.3 us)
Async XLA Ops:
  7.2 227.9 %reduce-scatter.3.cloned.1.call-start = ((), (), s32[]{:S(2)}) async-start(), calls=%async_computation.2 | async-start | bytes 6635520 | tf_op jit(solution)/shard_map/reduce_scatter | solution.py:1741
  7.2 20.2 %collective-permute-start.3 = (bf16[768,3072]{1,0:T(8,128)(2,1)}, bf16[768,3072]{1,0:T(8,128)(2,1)}, u32[]{:S(2)}, u32[]{:S(2)}) collective-permute-start(bf16[768,3072]{1,0:T(8,128)(2,1)} %bitcast.178), channel_id=1, source_target_pairs={{0,16},{16,0},{1,17},{17,1},{2,18},{18,2},{3,19},{19,3},{4,20},{20... | collective-permute-start | bytes 14155784 | tf_op jit(solution)/shard_map/ppermute | solution.py:1585
  13.6 14.8 %collective-permute-start.7 = (bf16[768,1152]{1,0:T(8,128)(2,1)S(1)}, bf16[768,1152]{1,0:T(8,128)(2,1)S(1)}, u32[]{:S(2)}, u32[]{:S(2)}) collective-permute-start(bf16[768,1152]{1,0:T(8,128)(2,1)S(1)} %get-tuple-element.222), channel_id=1, source_target_pairs={{0,16},{16,0},{1,17},{17,1},{2,18},{18,2},{3,19},{19,3},{4,20},{20... | collective-permute-start | bytes 5308424 | tf_op jit(solution)/shard_map/ppermute | solution.py:1585
  13.7 8.6 %collective-permute-start = (bf16[128,768]{1,0:T(8,128)(2,1)S(1)}, bf16[128,768]{1,0:T(8,128)(2,1)S(1)}, u32[]{:S(2)}, u32[]{:S(2)}) collective-permute-start(bf16[128,768]{1,0:T(8,128)(2,1)S(1)} %get-tuple-element.433), channel_id=1, source_target_pairs={{0,4},{4,0},{8,12},{12,8},{1,5},{5,1},{9,13},{13,9},{2,6},{6,2},{1... | collective-permute-start | bytes 589832 | tf_op jit(solution)/shard_map/ppermute | solution.py:1589
  16.6 10.8 %collective-permute-start.1 = (bf16[128,768]{1,0:T(8,128)(2,1)S(1)}, bf16[128,768]{1,0:T(8,128)(2,1)S(1)}, u32[]{:S(2)}, u32[]{:S(2)}) collective-permute-start(bf16[128,768]{1,0:T(8,128)(2,1)S(1)} %get-tuple-element.432), channel_id=1, source_target_pairs={{0,8},{4,12},{8,0},{12,4},{1,9},{5,13},{9,1},{13,5},{2,10},{6,14},... | collective-permute-start | bytes 589832 | tf_op jit(solution)/shard_map/ppermute | solution.py:1589
  18.1 9.3 %collective-permute-start.2 = (bf16[128,768]{1,0:T(8,128)(2,1)S(1)}, bf16[128,768]{1,0:T(8,128)(2,1)S(1)}, u32[]{:S(2)}, u32[]{:S(2)}) collective-permute-start(bf16[128,768]{1,0:T(8,128)(2,1)S(1)} %get-tuple-element.432), channel_id=1, source_target_pairs={{0,12},{4,8},{8,4},{12,0},{1,13},{5,9},{9,5},{13,1},{2,14},{6,10},... | collective-permute-start | bytes 589832 | tf_op jit(solution)/shard_map/ppermute | solution.py:1589
  29.5 17.9 %collective-permute-start.10 = (bf16[3072,768]{1,0:T(8,128)(2,1)}, bf16[3072,768]{1,0:T(8,128)(2,1)}, u32[]{:S(2)}, u32[]{:S(2)}) collective-permute-start(bf16[3072,768]{1,0:T(8,128)(2,1)} %bitcast.21.wd_a), channel_id=1, source_target_pairs={{0,16},{16,0},{1,17},{17,1},{2,18},{18,2},{3,19},{19,3},{4,20},{20... | collective-permute-start | bytes 14155784 | tf_op jit(solution)/shard_map/ppermute | solution.py:1585
  29.9 17.5 %collective-permute-start.9 = (bf16[768,768]{1,0:T(8,128)(2,1)}, bf16[768,768]{1,0:T(8,128)(2,1)S(1)}, u32[]{:S(2)}, u32[]{:S(2)}) collective-permute-start(bf16[768,768]{1,0:T(8,128)(2,1)} %bitcast.184), channel_id=1, source_target_pairs={{0,16},{16,0},{1,17},{17,1},{2,18},{18,2},{3,19},{19,3},{4,20},{20... | collective-permute-start | bytes 3538952 | tf_op jit(solution)/shard_map/ppermute | solution.py:1585
  47.7 6.3 %collective-permute-start.12 = (bf16[256,192]{1,0:T(8,128)(2,1)S(1)}, bf16[256,192]{1,0:T(8,128)(2,1)S(1)}, u32[]{:S(2)}, u32[]{:S(2)}) collective-permute-start(bf16[256,192]{1,0:T(8,128)(2,1)S(1)} %get-tuple-element.233), channel_id=1, source_target_pairs={{0,4},{4,0},{8,12},{12,8},{1,5},{5,1},{9,13},{13,9},{2,6},{6,2},{1... | collective-permute-start | bytes 294920 | tf_op jit(solution)/shard_map/ppermute | solution.py:1589
  48.9 6.6 %collective-permute-start.13 = (bf16[256,192]{1,0:T(8,128)(2,1)S(1)}, bf16[256,192]{1,0:T(8,128)(2,1)S(1)}, u32[]{:S(2)}, u32[]{:S(2)}) collective-permute-start(bf16[256,192]{1,0:T(8,128)(2,1)S(1)} %get-tuple-element.234), channel_id=1, source_target_pairs={{0,20},{4,16},{8,28},{12,24},{16,4},{20,0},{24,12},{28,8},{1,21},{... | collective-permute-start | bytes 294920 | tf_op jit(solution)/shard_map/ppermute | solution.py:1593
  66.2 11.6 %collective-permute-start.18 = (bf16[256,4608]{1,0:T(8,128)(2,1)}, bf16[256,4608]{1,0:T(8,128)(2,1)}, u32[]{:S(2)}, u32[]{:S(2)}) collective-permute-start(bf16[256,4608]{1,0:T(8,128)(2,1)} %get-tuple-element.240.f0), channel_id=1, source_target_pairs={{0,16},{16,0},{1,17},{17,1},{2,18},{18,2},{3,19},{19,3},{4,20},{20... | collective-permute-start | bytes 7077896 | tf_op jit(solution)/shard_map/ppermute | solution.py:1585
  66.8 11.0 %collective-permute-start.15 = (bf16[256,768]{1,0:T(8,128)(2,1)S(1)}, bf16[256,768]{1,0:T(8,128)(2,1)S(1)}, u32[]{:S(2)}, u32[]{:S(2)}) collective-permute-start(bf16[256,768]{1,0:T(8,128)(2,1)S(1)} %get-tuple-element.239.refs_1_), channel_id=1, source_target_pairs={{0,4},{4,0},{8,12},{12,8},{1,5},{5,1},{9,13},{13,9},{2,6},{6,2},{1... | collective-permute-start | bytes 1179656 | tf_op jit(solution)/shard_map/ppermute | solution.py:1589
  68.3 4.4 %collective-permute-start.16 = (bf16[38,768]{1,0:T(8,128)(2,1)S(1)}, bf16[38,768]{1,0:T(8,128)(2,1)S(1)}, u32[]{:S(2)}, u32[]{:S(2)}) collective-permute-start(bf16[38,768]{1,0:T(8,128)(2,1)S(1)} %bitcast.176), channel_id=1, source_target_pairs={{0,8},{4,12},{8,0},{12,4},{1,9},{5,13},{9,1},{13,5},{2,10},{6,14},... | collective-permute-start | bytes 175112 | tf_op jit(solution)/shard_map/ppermute | solution.py:1589
  69.2 3.5 collective-permute-start.17
  70.4 9.4 %collective-permute-start.14 = (bf16[256,768]{1,0:T(8,128)(2,1)S(1)}, bf16[256,768]{1,0:T(8,128)(2,1)S(1)}, u32[]{:S(2)}, u32[]{:S(2)}) collective-permute-start(bf16[256,768]{1,0:T(8,128)(2,1)S(1)} %get-tuple-element.239.refs_1_), channel_id=1, source_target_pairs={{0,16},{16,0},{1,17},{17,1},{2,18},{18,2},{3,19},{19,3},{4,20},{20... | collective-permute-start | bytes 1179656 | tf_op jit(solution)/shard_map/ppermute | solution.py:1585
  77.8 22.6 %collective-permute-start.23 = (bf16[256,768]{1,0:T(8,128)(2,1)S(1)}, bf16[256,768]{1,0:T(8,128)(2,1)S(1)}, u32[]{:S(2)}, u32[]{:S(2)}) collective-permute-start(bf16[256,768]{1,0:T(8,128)(2,1)S(1)} %get-tuple-element.239.refs_1_), channel_id=1, source_target_pairs={{0,0},{4,4},{24,8},{28,12},{1,1},{5,5},{25,9},{29,13},{2,2},{6,6},... | collective-permute-start | bytes 1179656 | tf_op jit(solution)/shard_map/ppermute | solution.py:1612
  78.5 21.9 %collective-permute-start.24 = (bf16[256,768]{1,0:T(8,128)(2,1)S(1)}, bf16[256,768]{1,0:T(8,128)(2,1)S(1)}, u32[]{:S(2)}, u32[]{:S(2)}) collective-permute-start(bf16[256,768]{1,0:T(8,128)(2,1)S(1)} %get-tuple-element.239.refs_1_), channel_id=1, source_target_pairs={{16,8},{20,12},{8,0},{12,4},{17,9},{21,13},{9,1},{13,5},{18,10},{2... | collective-permute-start | bytes 1179656 | tf_op jit(solution)/shard_map/ppermute | solution.py:1612
  95.8 4.6 %collective-permute-start.20 = (bf16[256,192]{1,0:T(8,128)(2,1)S(1)}, bf16[256,192]{1,0:T(8,128)(2,1)S(1)}, u32[]{:S(2)}, u32[]{:S(2)}) collective-permute-start(bf16[256,192]{1,0:T(8,128)(2,1)S(1)} %get-tuple-element.243), channel_id=1, source_target_pairs={{0,16},{16,0},{1,17},{17,1},{2,18},{18,2},{3,19},{19,3},{4,20},{20... | collective-permute-start | bytes 294920 | tf_op jit(solution)/shard_map/ppermute | solution.py:1585
  98.7 6.4 %collective-permute-start.21 = (bf16[256,192]{1,0:T(8,128)(2,1)S(1)}, bf16[256,192]{1,0:T(8,128)(2,1)S(1)}, u32[]{:S(2)}, u32[]{:S(2)}) collective-permute-start(bf16[256,192]{1,0:T(8,128)(2,1)S(1)} %get-tuple-element.244), channel_id=1, source_target_pairs={{0,4},{4,0},{8,12},{12,8},{1,5},{5,1},{9,13},{13,9},{2,6},{6,2},{1... | collective-permute-start | bytes 294920 | tf_op jit(solution)/shard_map/ppermute | solution.py:1589
  99.2 6.7 %collective-permute-start.22 = (bf16[256,192]{1,0:T(8,128)(2,1)S(1)}, bf16[256,192]{1,0:T(8,128)(2,1)S(1)}, u32[]{:S(2)}, u32[]{:S(2)}) collective-permute-start(bf16[256,192]{1,0:T(8,128)(2,1)S(1)} %get-tuple-element.245), channel_id=1, source_target_pairs={{0,20},{4,16},{8,28},{12,24},{16,4},{20,0},{24,12},{28,8},{1,21},{... | collective-permute-start | bytes 294920 | tf_op jit(solution)/shard_map/ppermute | solution.py:1593
  121.4 6.9 %collective-permute-start.28 = (bf16[256,4608]{1,0:T(8,128)(2,1)}, bf16[256,4608]{1,0:T(8,128)(2,1)S(1)}, u32[]{:S(2)}, u32[]{:S(2)}) collective-permute-start(bf16[256,4608]{1,0:T(8,128)(2,1)} %get-tuple-element.259.f0), channel_id=1, source_target_pairs={{0,16},{16,0},{1,17},{17,1},{2,18},{18,2},{3,19},{19,3},{4,20},{20... | collective-permute-start | bytes 7077896 | tf_op jit(solution)/shard_map/ppermute | solution.py:1585
  122.1 6.2 %collective-permute-start.29 = (bf16[256,2304]{1,0:T(8,128)(2,1)}, bf16[256,2304]{1,0:T(8,128)(2,1)S(1)}, u32[]{:S(2)}, u32[]{:S(2)}) collective-permute-start(bf16[256,2304]{1,0:T(8,128)(2,1)} %get-tuple-element.261), channel_id=1, source_target_pairs={{0,16},{16,0},{1,17},{17,1},{2,18},{18,2},{3,19},{19,3},{4,20},{20... | collective-permute-start | bytes 3538952 | tf_op jit(solution)/shard_map/ppermute | solution.py:1585
  122.1 16.7 %collective-permute-start.25 = (bf16[256,192]{1,0:T(8,128)(2,1)S(1)}, bf16[256,192]{1,0:T(8,128)(2,1)S(1)}, u32[]{:S(2)}, u32[]{:S(2)}) collective-permute-start(bf16[256,192]{1,0:T(8,128)(2,1)S(1)} %get-tuple-element.256), channel_id=1, source_target_pairs={{0,16},{16,0},{1,17},{17,1},{2,18},{18,2},{3,19},{19,3},{4,20},{20... | collective-permute-start | bytes 294920 | tf_op jit(solution)/shard_map/ppermute | solution.py:1585
  122.6 16.2 %collective-permute-start.26 = (bf16[256,192]{1,0:T(8,128)(2,1)S(1)}, bf16[256,192]{1,0:T(8,128)(2,1)S(1)}, u32[]{:S(2)}, u32[]{:S(2)}) collective-permute-start(bf16[256,192]{1,0:T(8,128)(2,1)S(1)} %get-tuple-element.257), channel_id=1, source_target_pairs={{0,4},{4,0},{8,12},{12,8},{1,5},{5,1},{9,13},{13,9},{2,6},{6,2},{1... | collective-permute-start | bytes 294920 | tf_op jit(solution)/shard_map/ppermute | solution.py:1589
  123.2 15.7 %collective-permute-start.27 = (bf16[256,192]{1,0:T(8,128)(2,1)S(1)}, bf16[256,192]{1,0:T(8,128)(2,1)S(1)}, u32[]{:S(2)}, u32[]{:S(2)}) collective-permute-start(bf16[256,192]{1,0:T(8,128)(2,1)S(1)} %get-tuple-element.258), channel_id=1, source_target_pairs={{0,20},{4,16},{8,28},{12,24},{16,4},{20,0},{24,12},{28,8},{1,21},{... | collective-permute-start | bytes 294920 | tf_op jit(solution)/shard_map/ppermute | solution.py:1593
  138.9 182.5 %reduce-scatter.5.cloned.1.call-start = ((), (), s32[]{:S(2)}) async-start(), calls=%async_computation.3 | async-start | bytes 1658880 | tf_op jit(solution)/shard_map/reduce_scatter | solution.py:1767
  159.9 20.3 %collective-permute-start.32 = (bf16[256,768]{1,0:T(8,128)(2,1)S(1)}, bf16[256,768]{1,0:T(8,128)(2,1)S(1)}, u32[]{:S(2)}, u32[]{:S(2)}) collective-permute-start(bf16[256,768]{1,0:T(8,128)(2,1)S(1)} %add_convert_fusion.7), channel_id=1, source_target_pairs={{0,4},{4,0},{8,12},{12,8},{1,5},{5,1},{9,13},{13,9},{2,6},{6,2},{1... | collective-permute-start | bytes 1179656 | tf_op jit(solution)/shard_map/ppermute | solution.py:1589
  160.5 20.2 %collective-permute-start.30 = (bf16[256,768]{1,0:T(8,128)(2,1)S(1)}, bf16[256,768]{1,0:T(8,128)(2,1)S(1)}, u32[]{:S(2)}, u32[]{:S(2)}) collective-permute-start(bf16[256,768]{1,0:T(8,128)(2,1)S(1)} %get-tuple-element.276), channel_id=1, source_target_pairs={{0,16},{16,0},{1,17},{17,1},{2,18},{18,2},{3,19},{19,3},{4,20},{20... | collective-permute-start | bytes 1179656 | tf_op jit(solution)/shard_map/ppermute | solution.py:1585
  180.1 12.7 %collective-permute-start.33 = (bf16[384,640]{1,0:T(8,128)(2,1)S(1)}, bf16[384,640]{1,0:T(8,128)(2,1)S(1)}, u32[]{:S(2)}, u32[]{:S(2)}) collective-permute-start(bf16[384,640]{1,0:T(8,128)(2,1)S(1)} %get-tuple-element.299), channel_id=1, source_target_pairs={{0,8},{4,12},{8,0},{12,4},{1,9},{5,13},{9,1},{13,5},{2,10},{6,14},... | collective-permute-start | bytes 1474568 | tf_op jit(solution)/shard_map/ppermute | solution.py:1589
  193.6 3.2 collective-permute-start.37
  193.7 39.8 %collective-permute-start.40 = (bf16[384,512]{1,0:T(8,128)(2,1)}, bf16[384,512]{1,0:T(8,128)(2,1)S(1)}, u32[]{:S(2)}, u32[]{:S(2)}) collective-permute-start(bf16[384,512]{1,0:T(8,128)(2,1)} %get-tuple-element.335), channel_id=1, source_target_pairs={{0,8},{4,12},{8,0},{12,4},{1,9},{5,13},{9,1},{13,5},{2,10},{6,14},... | collective-permute-start | bytes 1179656 | tf_op jit(solution)/shard_map/ppermute | solution.py:1589
  195.0 11.3 %collective-permute-start.34 = (bf16[256,192]{1,0:T(8,128)(2,1)S(1)}, bf16[256,192]{1,0:T(8,128)(2,1)S(1)}, u32[]{:S(2)}, u32[]{:S(2)}) collective-permute-start(bf16[256,192]{1,0:T(8,128)(2,1)S(1)} %get-tuple-element.301), channel_id=1, source_target_pairs={{0,16},{16,0},{1,17},{17,1},{2,18},{18,2},{3,19},{19,3},{4,20},{20... | collective-permute-start | bytes 294920 | tf_op jit(solution)/shard_map/ppermute | solution.py:1585
  195.2 11.1 %collective-permute-start.35 = (bf16[256,192]{1,0:T(8,128)(2,1)S(1)}, bf16[256,192]{1,0:T(8,128)(2,1)S(1)}, u32[]{:S(2)}, u32[]{:S(2)}) collective-permute-start(bf16[256,192]{1,0:T(8,128)(2,1)S(1)} %get-tuple-element.302), channel_id=1, source_target_pairs={{0,4},{4,0},{8,12},{12,8},{1,5},{5,1},{9,13},{13,9},{2,6},{6,2},{1... | collective-permute-start | bytes 294920 | tf_op jit(solution)/shard_map/ppermute | solution.py:1589
  195.8 13.4 %collective-permute-start.36 = (bf16[256,192]{1,0:T(8,128)(2,1)S(1)}, bf16[256,192]{1,0:T(8,128)(2,1)S(1)}, u32[]{:S(2)}, u32[]{:S(2)}) collective-permute-start(bf16[256,192]{1,0:T(8,128)(2,1)S(1)} %get-tuple-element.303), channel_id=1, source_target_pairs={{0,20},{4,16},{8,28},{12,24},{16,4},{20,0},{24,12},{28,8},{1,21},{... | collective-permute-start | bytes 294920 | tf_op jit(solution)/shard_map/ppermute | solution.py:1593
  209.1 26.0 %collective-permute-start.38 = (bf16[384,1024]{1,0:T(8,128)(2,1)S(1)}, bf16[384,1024]{1,0:T(8,128)(2,1)}, u32[]{:S(2)}, u32[]{:S(2)}) collective-permute-start(bf16[384,1024]{1,0:T(8,128)(2,1)S(1)} %get-tuple-element.333), channel_id=1, source_target_pairs={{0,8},{4,12},{8,0},{12,4},{1,9},{5,13},{9,1},{13,5},{2,10},{6,14},... | collective-permute-start | bytes 2359304 | tf_op jit(solution)/shard_map/ppermute | solution.py:1589
  209.9 23.6 %collective-permute-start.39 = (bf16[8,96,384]{2,1,0:T(8,128)(2,1)S(1)}, bf16[8,96,384]{2,1,0:T(8,128)(2,1)S(1)}, u32[]{:S(2)}, u32[]{:S(2)}) collective-permute-start(bf16[8,96,384]{2,1,0:T(8,128)(2,1)S(1)} %get-tuple-element.334), channel_id=1, source_target_pairs={{0,4},{4,0},{8,12},{12,8},{1,5},{5,1},{9,13},{13,9},{2,6},{6,2},{1... | collective-permute-start | bytes 1769480 | tf_op jit(solution)/shard_map/ppermute | solution.py:1589
  210.8 39.2 %collective-permute-start.46 = (bf16[384,896]{1,0:T(8,128)(2,1)}, bf16[384,896]{1,0:T(8,128)(2,1)}, u32[]{:S(2)}, u32[]{:S(2)}) collective-permute-start(bf16[384,896]{1,0:T(8,128)(2,1)} %get-tuple-element.349), channel_id=1, source_target_pairs={{0,8},{4,12},{8,0},{12,4},{1,9},{5,13},{9,1},{13,5},{2,10},{6,14},... | collective-permute-start | bytes 2064392 | tf_op jit(solution)/shard_map/ppermute | solution.py:1589
  211.7 38.3 %collective-permute-start.47 = (bf16[8,96,384]{2,1,0:T(8,128)(2,1)}, bf16[8,96,384]{2,1,0:T(8,128)(2,1)}, u32[]{:S(2)}, u32[]{:S(2)}) collective-permute-start(bf16[8,96,384]{2,1,0:T(8,128)(2,1)} %get-tuple-element.350), channel_id=1, source_target_pairs={{0,4},{4,0},{8,12},{12,8},{1,5},{5,1},{9,13},{13,9},{2,6},{6,2},{1... | collective-permute-start | bytes 1769480 | tf_op jit(solution)/shard_map/ppermute | solution.py:1589
  239.0 17.5 %collective-permute-start.44 = (bf16[2,2,48,1152]{3,2,0,1:T(8,128)(2,1)}, bf16[2,2,48,1152]{3,2,0,1:T(8,128)(2,1)S(1)}, u32[]{:S(2)}, u32[]{:S(2)}) collective-permute-start(bf16[2,2,48,1152]{3,2,0,1:T(8,128)(2,1)} %bitcast.151), channel_id=1, source_target_pairs={{0,1},{1,0},{2,3},{3,2},{4,5},{5,4},{6,7},{7,6},{8,9},{9,8},{10,11... | collective-permute-start | bytes 1327112 | tf_op jit(solution)/shard_map/ppermute | solution.py:1597
  240.5 12.1 %collective-permute-start.43 = (bf16[256,768]{1,0:T(8,128)(2,1)}, bf16[256,768]{1,0:T(8,128)(2,1)S(1)}, u32[]{:S(2)}, u32[]{:S(2)}) collective-permute-start(bf16[256,768]{1,0:T(8,128)(2,1)} %add_convert_fusion.5), channel_id=1, source_target_pairs={{0,4},{4,0},{8,12},{12,8},{1,5},{5,1},{9,13},{13,9},{2,6},{6,2},{1... | collective-permute-start | bytes 1179656 | tf_op jit(solution)/shard_map/ppermute | solution.py:1589
  241.2 11.4 %collective-permute-start.45 = (f32[14,768]{1,0:T(8,128)S(1)}, f32[14,768]{1,0:T(8,128)S(1)}, u32[]{:S(2)}, u32[]{:S(2)}) collective-permute-start(f32[14,768]{1,0:T(8,128)S(1)} %select_add_fusion), channel_id=1, source_target_pairs={{0,4},{4,0},{8,12},{12,8},{1,5},{5,1},{9,13},{13,9},{2,6},{6,2},{1... | collective-permute-start | bytes 129032 | tf_op jit(solution)/shard_map/ppermute | solution.py:1589
  250.0 20.5 %collective-permute-start.56 = (bf16[256,768]{1,0:T(8,128)(2,1)S(1)}, bf16[256,768]{1,0:T(8,128)(2,1)S(1)}, u32[]{:S(2)}, u32[]{:S(2)}) collective-permute-start(bf16[256,768]{1,0:T(8,128)(2,1)S(1)} %copy-done.14), channel_id=1, source_target_pairs={{0,16},{16,0},{1,17},{17,1},{2,18},{18,2},{3,19},{19,3},{4,20},{20... | collective-permute-start | bytes 1179656 | tf_op jit(solution)/shard_map/ppermute | solution.py:1585
  258.6 35.4 %collective-permute-start.49 = (bf16[2,2,48,1920]{3,2,0,1:T(8,128)(2,1)S(1)}, bf16[2,2,48,1920]{3,2,0,1:T(8,128)(2,1)S(1)}, u32[]{:S(2)}, u32[]{:S(2)}) collective-permute-start(bf16[2,2,48,1920]{3,2,0,1:T(8,128)(2,1)S(1)} %bitcast.169), channel_id=1, source_target_pairs={{0,1},{1,0},{2,3},{3,2},{4,5},{5,4},{6,7},{7,6},{8,9},{9,8},{10,11... | collective-permute-start | bytes 2211848 | tf_op jit(solution)/shard_map/ppermute | solution.py:1597
  260.6 33.4 %collective-permute-start.48 = (bf16[384,640]{1,0:T(8,128)(2,1)S(1)}, bf16[384,640]{1,0:T(8,128)(2,1)S(1)}, u32[]{:S(2)}, u32[]{:S(2)}) collective-permute-start(bf16[384,640]{1,0:T(8,128)(2,1)S(1)} %get-tuple-element.363), channel_id=1, source_target_pairs={{0,8},{4,12},{8,0},{12,4},{1,9},{5,13},{9,1},{13,5},{2,10},{6,14},... | collective-permute-start | bytes 1474568 | tf_op jit(solution)/shard_map/ppermute | solution.py:1589
  260.6 33.4 %collective-permute-start.50 = (bf16[384,512]{1,0:T(8,128)(2,1)S(1)}, bf16[384,512]{1,0:T(8,128)(2,1)S(1)}, u32[]{:S(2)}, u32[]{:S(2)}) collective-permute-start(bf16[384,512]{1,0:T(8,128)(2,1)S(1)} %get-tuple-element.365), channel_id=1, source_target_pairs={{0,8},{4,12},{8,0},{12,4},{1,9},{5,13},{9,1},{13,5},{2,10},{6,14},... | collective-permute-start | bytes 1179656 | tf_op jit(solution)/shard_map/ppermute | solution.py:1589
  264.3 28.1 %collective-permute-start.51 = (bf16[2,48,1152]{2,1,0:T(8,128)(2,1)S(1)}, bf16[2,48,1152]{2,1,0:T(8,128)(2,1)S(1)}, u32[]{:S(2)}, u32[]{:S(2)}) collective-permute-start(bf16[2,48,1152]{2,1,0:T(8,128)(2,1)S(1)} %dynamic-slice_bitcast_fusion.3), channel_id=1, source_target_pairs={{0,2},{1,3},{2,0},{3,1},{4,6},{5,7},{6,4},{7,5},{8,10},{9,11},{10,... | collective-permute-start | bytes 663560 | tf_op jit(solution)/shard_map/ppermute | solution.py:1597
  270.6 30.2 %collective-permute-start.57 = (bf16[256,768]{1,0:T(8,128)(2,1)S(1)}, bf16[256,768]{1,0:T(8,128)(2,1)S(1)}, u32[]{:S(2)}, u32[]{:S(2)}) collective-permute-start(bf16[256,768]{1,0:T(8,128)(2,1)S(1)} %add_convert_fusion.4), channel_id=1, source_target_pairs={{0,0},{4,4},{24,8},{28,12},{1,1},{5,5},{25,9},{29,13},{2,2},{6,6},... | collective-permute-start | bytes 1179656 | tf_op jit(solution)/shard_map/ppermute | solution.py:1612
  292.5 13.0 %collective-permute-start.58 = (bf16[256,768]{1,0:T(8,128)(2,1)S(1)}, bf16[256,768]{1,0:T(8,128)(2,1)S(1)}, u32[]{:S(2)}, u32[]{:S(2)}) collective-permute-start(bf16[256,768]{1,0:T(8,128)(2,1)S(1)} %add_convert_fusion.4), channel_id=1, source_target_pairs={{16,8},{20,12},{8,0},{12,4},{17,9},{21,13},{9,1},{13,5},{18,10},{2... | collective-permute-start | bytes 1179656 | tf_op jit(solution)/shard_map/ppermute | solution.py:1612
  294.6 26.8 %collective-permute-start.53 = (bf16[2,2,192,384]{3,2,0,1:T(8,128)(2,1)S(1)}, bf16[2,2,192,384]{3,2,0,1:T(8,128)(2,1)S(1)}, u32[]{:S(2)}, u32[]{:S(2)}) collective-permute-start(bf16[2,2,192,384]{3,2,0,1:T(8,128)(2,1)S(1)} %bitcast.170), channel_id=1, source_target_pairs={{0,8},{4,12},{8,0},{12,4},{1,9},{5,13},{9,1},{13,5},{2,10},{6,14},... | collective-permute-start | bytes 1769480 | tf_op jit(solution)/shard_map/ppermute | solution.py:1589
  297.3 23.3 %collective-permute-start.54 = (bf16[2,2,48,1152]{3,2,0,1:T(8,128)(2,1)S(1)}, bf16[2,2,48,1152]{3,2,0,1:T(8,128)(2,1)S(1)}, u32[]{:S(2)}, u32[]{:S(2)}) collective-permute-start(bf16[2,2,48,1152]{3,2,0,1:T(8,128)(2,1)S(1)} %bitcast.171), channel_id=1, source_target_pairs={{0,1},{1,0},{2,3},{3,2},{4,5},{5,4},{6,7},{7,6},{8,9},{9,8},{10,11... | collective-permute-start | bytes 1327112 | tf_op jit(solution)/shard_map/ppermute | solution.py:1597
  300.8 19.8 %collective-permute-start.52 = (bf16[2,48,1920]{2,1,0:T(8,128)(2,1)S(1)}, bf16[2,48,1920]{2,1,0:T(8,128)(2,1)S(1)}, u32[]{:S(2)}, u32[]{:S(2)}) collective-permute-start(bf16[2,48,1920]{2,1,0:T(8,128)(2,1)S(1)} %dynamic-slice_bitcast_fusion), channel_id=1, source_target_pairs={{0,2},{1,3},{2,0},{3,1},{4,6},{5,7},{6,4},{7,5},{8,10},{9,11},{10,... | collective-permute-start | bytes 1105928 | tf_op jit(solution)/shard_map/ppermute | solution.py:1597
  300.9 18.2 %collective-permute-start.55 = (f32[14,768]{1,0:T(8,128)S(1)}, f32[14,768]{1,0:T(8,128)S(1)}, u32[]{:S(2)}, u32[]{:S(2)}) collective-permute-start(f32[14,768]{1,0:T(8,128)S(1)} %add.219), channel_id=1, source_target_pairs={{0,1},{1,0},{2,3},{3,2},{4,5},{5,4},{6,7},{7,6},{8,9},{9,8},{10,11... | collective-permute-start | bytes 129032 | tf_op jit(solution)/shard_map/ppermute | solution.py:1597
  305.4 20.5 %collective-permute-start.64 = (bf16[2,256,768]{2,1,0:T(8,128)(2,1)}, bf16[2,256,768]{2,1,0:T(8,128)(2,1)}, u32[]{:S(2)}, u32[]{:S(2)}) collective-permute-start(bf16[2,256,768]{2,1,0:T(8,128)(2,1)} %pad_maximum_fusion), channel_id=1, source_target_pairs={{0,16},{4,20},{24,24},{28,28},{1,17},{5,21},{25,25},{29,29},{2,18}... | collective-permute-start | bytes 2359304 | tf_op jit(solution)/shard_map/ppermute | solution.py:1612
  319.1 7.9 %collective-permute-start.65 = (bf16[2,256,768]{2,1,0:T(8,128)(2,1)}, bf16[2,256,768]{2,1,0:T(8,128)(2,1)}, u32[]{:S(2)}, u32[]{:S(2)}) collective-permute-start(bf16[2,256,768]{2,1,0:T(8,128)(2,1)} %pad_maximum_fusion), channel_id=1, source_target_pairs={{16,24},{20,28},{8,16},{12,20},{17,25},{21,29},{9,17},{13,21},{18,... | collective-permute-start | bytes 2359304 | tf_op jit(solution)/shard_map/ppermute | solution.py:1612
  323.0 13.9 %collective-permute-start.60 = (bf16[2,192,384]{2,1,0:T(8,128)(2,1)S(1)}, bf16[2,192,384]{2,1,0:T(8,128)(2,1)S(1)}, u32[]{:S(2)}, u32[]{:S(2)}) collective-permute-start(bf16[2,192,384]{2,1,0:T(8,128)(2,1)S(1)} %dynamic-slice_bitcast_fusion.1), channel_id=1, source_target_pairs={{0,1},{1,0},{2,3},{3,2},{4,5},{5,4},{6,7},{7,6},{8,9},{9,8},{10,11... | collective-permute-start | bytes 884744 | tf_op jit(solution)/shard_map/ppermute | solution.py:1597
  324.8 11.6 %collective-permute-start.59 = (bf16[2,48,1152]{2,1,0:T(8,128)(2,1)S(1)}, bf16[2,48,1152]{2,1,0:T(8,128)(2,1)S(1)}, u32[]{:S(2)}, u32[]{:S(2)}) collective-permute-start(bf16[2,48,1152]{2,1,0:T(8,128)(2,1)S(1)} %dynamic-slice_bitcast_fusion.2), channel_id=1, source_target_pairs={{0,2},{1,3},{2,0},{3,1},{4,6},{5,7},{6,4},{7,5},{8,10},{9,11},{10,... | collective-permute-start | bytes 663560 | tf_op jit(solution)/shard_map/ppermute | solution.py:1597
  325.0 9.7 %collective-permute-start.61 = (bf16[48,1920]{1,0:T(8,128)(2,1)S(1)}, bf16[48,1920]{1,0:T(8,128)(2,1)S(1)}, u32[]{:S(2)}, u32[]{:S(2)}) collective-permute-start(bf16[48,1920]{1,0:T(8,128)(2,1)S(1)} %dynamic-slice_bitcast_fusion.6), channel_id=1, source_target_pairs={{0,4},{4,0},{8,12},{12,8},{1,5},{5,1},{9,13},{13,9},{2,6},{6,2},{1... | collective-permute-start | bytes 552968 | tf_op jit(solution)/shard_map/ppermute | solution.py:1589
  325.9 8.7 %collective-permute-start.63 = (bf16[48,1152]{1,0:T(8,128)(2,1)S(1)}, bf16[48,1152]{1,0:T(8,128)(2,1)S(1)}, u32[]{:S(2)}, u32[]{:S(2)}) collective-permute-start(bf16[48,1152]{1,0:T(8,128)(2,1)S(1)} %copy-done.51), channel_id=1, source_target_pairs={{0,4},{4,0},{8,12},{12,8},{1,5},{5,1},{9,13},{13,9},{2,6},{6,2},{1... | collective-permute-start | bytes 331784 | tf_op jit(solution)/shard_map/ppermute | solution.py:1589
  327.0 6.9 %collective-permute-start.62 = (f32[14,768]{1,0:T(8,128)S(1)}, f32[14,768]{1,0:T(8,128)S(1)}, u32[]{:S(2)}, u32[]{:S(2)}) collective-permute-start(f32[14,768]{1,0:T(8,128)S(1)} %add.228), channel_id=1, source_target_pairs={{0,8},{4,12},{8,0},{12,4},{1,9},{5,13},{9,1},{13,5},{2,10},{6,14},... | collective-permute-start | bytes 129032 | tf_op jit(solution)/shard_map/ppermute | solution.py:1589
  337.2 12.6 %collective-permute-start.66 = (bf16[192,384]{1,0:T(8,128)(2,1)S(1)}, bf16[192,384]{1,0:T(8,128)(2,1)S(1)}, u32[]{:S(2)}, u32[]{:S(2)}) collective-permute-start(bf16[192,384]{1,0:T(8,128)(2,1)S(1)} %dynamic-slice_bitcast_fusion.7), channel_id=1, source_target_pairs={{0,2},{1,3},{2,0},{3,1},{4,6},{5,7},{6,4},{7,5},{8,10},{9,11},{10,... | collective-permute-start | bytes 442376 | tf_op jit(solution)/shard_map/ppermute | solution.py:1597
  340.1 9.6 %collective-permute-start.67 = (bf16[48,1152]{1,0:T(8,128)(2,1)S(1)}, bf16[48,1152]{1,0:T(8,128)(2,1)S(1)}, u32[]{:S(2)}, u32[]{:S(2)}) collective-permute-start(bf16[48,1152]{1,0:T(8,128)(2,1)S(1)} %get-tuple-element.406), channel_id=1, source_target_pairs={{0,4},{4,0},{8,12},{12,8},{1,5},{5,1},{9,13},{13,9},{2,6},{6,2},{1... | collective-permute-start | bytes 331784 | tf_op jit(solution)/shard_map/ppermute | solution.py:1589
  340.8 9.0 %collective-permute-start.68 = (f32[14,768]{1,0:T(8,128)S(1)}, f32[14,768]{1,0:T(8,128)S(1)}, u32[]{:S(2)}, u32[]{:S(2)}) collective-permute-start(f32[14,768]{1,0:T(8,128)S(1)} %add.234), channel_id=1, source_target_pairs={{0,2},{1,3},{2,0},{3,1},{4,6},{5,7},{6,4},{7,5},{8,10},{9,11},{10,... | collective-permute-start | bytes 129032 | tf_op jit(solution)/shard_map/ppermute | solution.py:1597
  349.9 3.2 collective-permute-start.70
  350.1 3.0 collective-permute-start.69
  (68 other events, 464.1 us)
Sparse Core Ops, SparseCore 0:
  139.0 80.7 reduce-scatter.2
  241.3 44.9 reduce-scatter.4
